TPU v7x, 32 devices: a whole 2x2x4 slice. The times are simulated.
32 devices in a mesh: dp: 8 (over z, x), mp: 4 (over y, core).
Axes of the slice: x: 2, y: 2, z: 4, core: 2. Of those that a mesh axis runs over, the one named last changes fastest.
Arguments:
- inputs: bfloat16 [4096, 2048], P('dp'), may hold values from -8 to 8
- seq_lengths: int32 [8], P('dp'), may hold values from 64 to 512, as said below
- norm_in: float32 [2048], replicated, may hold values from 0.25 to 1.75
- w_query: bfloat16 [2048, 2048], P(None, 'mp'), may hold values from -0.125 to 0.125
- w_key: bfloat16 [2048, 128], replicated, may hold values from -0.125 to 0.125
- w_value: bfloat16 [2048, 128], replicated, may hold values from -0.125 to 0.125
- w_out: bfloat16 [2048, 2048], P('mp'), may hold values from -0.5 to 0.5
- norm_mid: float32 [2048], replicated, may hold values from 0.25 to 1.75
- w_gate: bfloat16 [2048, 5632], P(None, 'mp'), may hold values from -0.125 to 0.125
- w_up: bfloat16 [2048, 5632], P(None, 'mp'), may hold values from -0.125 to 0.125
- w_down: bfloat16 [5632, 2048], P('mp'), may hold values from -0.078125 to 0.078125
- out_cotangent: bfloat16 [4096, 2048], P('dp'), may hold values from -8 to 8
- kv_cotangent: bfloat16 [4096, 256], P('dp'), may hold values from -6 to 6
Outputs:
- result: bfloat16 [4096, 2048], P('dp')
- grad_inputs: bfloat16 [4096, 2048], P('dp')
- grad_norm_in: float32 [2048], P('dp')
- grad_w_query: float32 [2048, 2048], P('dp', 'mp')
- grad_w_key: float32 [2048, 128], P('dp')
- grad_w_value: float32 [2048, 128], P('dp')
- grad_w_out: float32 [2048, 2048], P('mp', 'dp')
- grad_norm_mid: float32 [2048], P('dp')
- grad_w_gate: float32 [2048, 5632], P('dp', 'mp')
- grad_w_up: float32 [2048, 5632], P('dp', 'mp')
- grad_w_down: float32 [5632, 2048], P('mp', 'dp')
Inputs may be any that keep to these rules, and one draw needn't show every extreme that they name: Each dp index holds one sequence in the first seq_lengths of its 512 slots, the rest padding; one sequence has exactly 512 tokens and another exactly 64.
All inputs are finite; a program needn't handle non-finite values.
Results may differ from a plain program's by a relative error of at most 0.015.
Values sent between devices are 32-bit elements; how exact they have to be, the bound alone decides.
No kernel may reach another device: no remote copies, remote signals or barrier semaphores. Data moves between devices by JAX's collectives and lax.ppermute only.
A program may use at most 192 MiB of HBM per device.

v0:
```python
import jax
import jax.numpy as jnp
from jax import lax
from jax.sharding import PartitionSpec as P

epsilon = 1e-06
masked_value = -1e30


def rotary_tables(length, size):
    half_size = size // 2
    inverse = 10000.0 ** (-2.0 * jnp.arange(half_size, dtype=jnp.float32) / size)
    angles = jnp.arange(length, dtype=jnp.float32)[:, None] * inverse[None, :]
    return (jnp.cos(angles), jnp.sin(angles))


def rotate(values, cosine_table, sine_table):
    half_size = values.shape[-1] // 2
    front_half = values[..., :half_size]
    back_half = values[..., half_size:]
    return jnp.concatenate(
        [
            front_half * cosine_table - back_half * sine_table,
            back_half * cosine_table + front_half * sine_table,
        ],
        axis=-1,
    )


def unrotate(values, cosine_table, sine_table):
    half_size = values.shape[-1] // 2
    front_half = values[..., :half_size]
    back_half = values[..., half_size:]
    return jnp.concatenate(
        [
            front_half * cosine_table + back_half * sine_table,
            back_half * cosine_table - front_half * sine_table,
        ],
        axis=-1,
    )


def norm_back(stream, inverse_rms, gain, grad_normed):
    weighted = gain * grad_normed
    feature_count = stream.shape[-1]
    return (
        inverse_rms * weighted
        - stream
        * inverse_rms**3
        * jnp.sum(weighted * stream, axis=-1, keepdims=True)
        / feature_count
    )


def scores_block(query_block, key_part, row_start, length, score_scale):
    row_count = query_block.shape[0]
    scores = (
        jnp.einsum("qhe,ke->hqk", query_block, key_part, preferred_element_type=jnp.float32)
        * score_scale
    )
    query_pos = row_start + jnp.arange(row_count)
    key_pos = jnp.arange(key_part.shape[0])
    allowed = (key_pos[None, :] <= query_pos[:, None]) & (key_pos[None, :] < length)
    valid_query = (query_pos < length).astype(jnp.float32)
    return (jnp.where(allowed[None], scores, masked_value), valid_query)


def forward_block(query_block, key_part, value_part, row_start, length, score_scale):
    scores, valid_query = scores_block(query_block, key_part, row_start, length, score_scale)
    row_max = jnp.max(scores, axis=-1, keepdims=True)
    exponent = jnp.exp(scores - row_max)
    totals = jnp.sum(exponent, axis=-1, keepdims=True)
    weights = (exponent / totals).astype(jnp.bfloat16)
    attended = (
        jnp.einsum("hqk,ke->qhe", weights, value_part, preferred_element_type=jnp.float32)
        * valid_query[:, None, None]
    )
    return (attended.astype(jnp.bfloat16), row_max + jnp.log(totals))


def backward_block(
    query_block, key_part, value_part, grad_block, log_total, row_start, length, score_scale
):
    scores, valid_query = scores_block(query_block, key_part, row_start, length, score_scale)
    probs = jnp.exp(scores - log_total)
    grad_block = grad_block * valid_query.astype(jnp.bfloat16)[:, None, None]
    grad_probs = jnp.einsum(
        "qhe,ke->hqk", grad_block, value_part, preferred_element_type=jnp.float32
    )
    delta_row = jnp.sum(probs * grad_probs, axis=-1, keepdims=True)
    grad_scores = (probs * (grad_probs - delta_row)).astype(jnp.bfloat16)
    grad_query = (
        jnp.einsum("hqk,ke->qhe", grad_scores, key_part, preferred_element_type=jnp.float32)
        * score_scale
    )
    grad_key = (
        jnp.einsum("hqk,qhe->ke", grad_scores, query_block, preferred_element_type=jnp.float32)
        * score_scale
    )
    grad_value = jnp.einsum(
        "hqk,qhe->ke", probs.astype(jnp.bfloat16), grad_block, preferred_element_type=jnp.float32
    )
    return (grad_query, grad_key, grad_value)


def shards(
    inputs,
    seq_lengths,
    norm_in,
    w_query,
    w_key,
    w_value,
    w_out,
    norm_mid,
    w_gate,
    w_up,
    w_down,
    out_cotangent,
    kv_cotangent,
):
    stream = inputs.astype(jnp.float32)
    seq_len = stream.shape[0]
    head_size = w_key.shape[1]
    local_heads = w_query.shape[1] // head_size
    length = seq_lengths[0]
    valid_rows = (jnp.arange(seq_len) < length).astype(jnp.float32)[:, None]
    score_scale = head_size ** (-0.5)
    block_rows = min(256, seq_len)
    block_count = seq_len // block_rows
    cosine_table, sine_table = rotary_tables(seq_len, head_size)
    inverse_in = lax.rsqrt(jnp.mean(stream * stream, axis=-1, keepdims=True) + epsilon)
    normed = (stream * inverse_in * norm_in).astype(jnp.bfloat16)
    queries = jnp.dot(normed, w_query, preferred_element_type=jnp.float32).reshape(
        seq_len, local_heads, head_size
    )
    queries = rotate(queries, cosine_table[:, None, :], sine_table[:, None, :]).astype(jnp.bfloat16)
    key_rot = rotate(
        jnp.dot(normed, w_key, preferred_element_type=jnp.float32), cosine_table, sine_table
    ).astype(jnp.bfloat16)
    value_rows = jnp.dot(normed, w_value, preferred_element_type=jnp.float32).astype(jnp.bfloat16)
    attended_blocks = []
    log_totals = []
    for block_index in range(block_count):
        row_start = block_index * block_rows
        row_end = row_start + block_rows
        query_block = queries[row_start:row_end]
        attended_block, log_total = forward_block(
            query_block, key_rot, value_rows, row_start, length, score_scale
        )
        attended_blocks.append(attended_block)
        log_totals.append(log_total)
    attended = jnp.concatenate(attended_blocks, axis=0).reshape(seq_len, local_heads * head_size)
    attention_part = jnp.dot(attended, w_out, preferred_element_type=jnp.float32)
    hidden_stream = stream + lax.psum(attention_part, "mp")
    inverse_mid = lax.rsqrt(
        jnp.mean(hidden_stream * hidden_stream, axis=-1, keepdims=True) + epsilon
    )
    normed_mid = (hidden_stream * inverse_mid * norm_mid).astype(jnp.bfloat16)
    gate_value = jnp.dot(normed_mid, w_gate, preferred_element_type=jnp.float32)
    up_value = jnp.dot(normed_mid, w_up, preferred_element_type=jnp.float32)
    sigmoid_gate = jax.nn.sigmoid(gate_value)
    mixed = (gate_value * sigmoid_gate * up_value).astype(jnp.bfloat16)
    down_part = jnp.dot(mixed, w_down, preferred_element_type=jnp.float32)
    result = hidden_stream + lax.psum(down_part, "mp")
    grad_out = out_cotangent.astype(jnp.float32) * valid_rows
    grad_down_in = grad_out.astype(jnp.bfloat16)
    grad_w_down = jnp.einsum("tf,td->fd", mixed, grad_down_in, preferred_element_type=jnp.float32)
    grad_mixed = (
        jnp.einsum("td,fd->tf", grad_down_in, w_down, preferred_element_type=jnp.float32)
        .astype(jnp.bfloat16)
        .astype(jnp.float32)
    )
    grad_gate = (
        grad_mixed * up_value * sigmoid_gate * (1.0 + gate_value * (1.0 - sigmoid_gate))
    ).astype(jnp.bfloat16)
    grad_up = (grad_mixed * gate_value * sigmoid_gate).astype(jnp.bfloat16)
    grad_w_gate = jnp.einsum("td,tf->df", normed_mid, grad_gate, preferred_element_type=jnp.float32)
    grad_w_up = jnp.einsum("td,tf->df", normed_mid, grad_up, preferred_element_type=jnp.float32)
    mid_part = jnp.einsum("tf,df->td", grad_gate, w_gate, preferred_element_type=jnp.float32)
    mid_part = mid_part + jnp.einsum("tf,df->td", grad_up, w_up, preferred_element_type=jnp.float32)
    grad_normed_mid = lax.psum(mid_part, "mp")
    grad_norm_mid = jnp.sum(grad_normed_mid * hidden_stream * inverse_mid, axis=0)
    grad_hidden = grad_out + norm_back(hidden_stream, inverse_mid, norm_mid, grad_normed_mid)
    grad_attention = grad_hidden.astype(jnp.bfloat16)
    grad_w_out = jnp.einsum(
        "tc,td->cd", attended, grad_attention, preferred_element_type=jnp.float32
    )
    grad_attended = jnp.einsum(
        "td,cd->tc", grad_attention, w_out, preferred_element_type=jnp.float32
    )
    grad_attended = grad_attended.astype(jnp.bfloat16).reshape(seq_len, local_heads, head_size)
    grad_query_blocks = []
    grad_key_total = jnp.zeros((seq_len, head_size), jnp.float32)
    grad_value_total = jnp.zeros((seq_len, head_size), jnp.float32)
    for block_index in range(block_count):
        row_start = block_index * block_rows
        row_end = row_start + block_rows
        query_block = queries[row_start:row_end]
        grad_block = grad_attended[row_start:row_end]
        grad_query, grad_key, grad_value = backward_block(
            query_block,
            key_rot,
            value_rows,
            grad_block,
            log_totals[block_index],
            row_start,
            length,
            score_scale,
        )
        grad_key_total = grad_key_total + grad_key
        grad_value_total = grad_value_total + grad_value
        grad_query_blocks.append(grad_query)
    grad_queries_rot = jnp.concatenate(grad_query_blocks, axis=0)
    grad_query_rows = (
        unrotate(grad_queries_rot, cosine_table[:, None, :], sine_table[:, None, :])
        .astype(jnp.bfloat16)
        .reshape(seq_len, local_heads * head_size)
    )
    grad_w_query = jnp.einsum(
        "td,tc->dc", normed, grad_query_rows, preferred_element_type=jnp.float32
    )
    query_input_part = jnp.einsum(
        "tc,dc->td", grad_query_rows, w_query, preferred_element_type=jnp.float32
    )
    summed_input, summed_key, summed_value = lax.psum(
        (query_input_part, grad_key_total, grad_value_total), "mp"
    )
    partner_part = kv_cotangent.astype(jnp.float32) * valid_rows
    grad_key_rows = unrotate(
        summed_key + partner_part[:, :head_size], cosine_table, sine_table
    ).astype(jnp.bfloat16)
    grad_value_rows = (summed_value + partner_part[:, head_size:]).astype(jnp.bfloat16)
    grad_w_key = jnp.einsum("td,te->de", normed, grad_key_rows, preferred_element_type=jnp.float32)
    grad_w_value = jnp.einsum(
        "td,te->de", normed, grad_value_rows, preferred_element_type=jnp.float32
    )
    grad_normed = summed_input + jnp.einsum(
        "te,de->td", grad_key_rows, w_key, preferred_element_type=jnp.float32
    )
    grad_normed = grad_normed + jnp.einsum(
        "te,de->td", grad_value_rows, w_value, preferred_element_type=jnp.float32
    )
    grad_norm_in = jnp.sum(grad_normed * stream * inverse_in, axis=0)
    grad_inputs = grad_hidden + norm_back(stream, inverse_in, norm_in, grad_normed)
    weight_sums = (
        lax.psum_scatter(grad_norm_in, "dp", scatter_dimension=0, tiled=True),
        lax.psum_scatter(grad_w_query, "dp", scatter_dimension=0, tiled=True),
        lax.psum_scatter(grad_w_key, "dp", scatter_dimension=0, tiled=True),
        lax.psum_scatter(grad_w_value, "dp", scatter_dimension=0, tiled=True),
        lax.psum_scatter(grad_w_out, "dp", scatter_dimension=1, tiled=True),
        lax.psum_scatter(grad_norm_mid, "dp", scatter_dimension=0, tiled=True),
        lax.psum_scatter(grad_w_gate, "dp", scatter_dimension=0, tiled=True),
        lax.psum_scatter(grad_w_up, "dp", scatter_dimension=0, tiled=True),
        lax.psum_scatter(grad_w_down, "dp", scatter_dimension=1, tiled=True),
    )
    return (
        result.astype(jnp.bfloat16),
        grad_inputs.astype(jnp.bfloat16),
        weight_sums[0],
        weight_sums[1],
        weight_sums[2],
        weight_sums[3],
        weight_sums[4],
        weight_sums[5],
        weight_sums[6],
        weight_sums[7],
        weight_sums[8],
    )


def solution(mesh):
    return jax.shard_map(
        shards,
        mesh=mesh,
        in_specs=(
            P("dp", None),
            P("dp"),
            P(),
            P(None, "mp"),
            P(),
            P(),
            P("mp", None),
            P(),
            P(None, "mp"),
            P(None, "mp"),
            P("mp", None),
            P("dp", None),
            P("dp", None),
        ),
        out_specs=(
            P("dp", None),
            P("dp", None),
            P("dp"),
            P("dp", "mp"),
            P("dp", None),
            P("dp", None),
            P("mp", "dp"),
            P("dp"),
            P("dp", "mp"),
            P("dp", "mp"),
            P("mp", "dp"),
        ),
        check_vma=False,
    )
```

profile of v0, /device:TPU:0, one launch (start us, length us, event | category | flops | bytes accessed | tf_op | source)
XLA Modules:
  0.0 1347.9 jit_solution(2252742041494927995)
XLA Ops:
  38.0 7.8 convolution_convert_fusion
  45.8 80.3 %all-reduce.8.cloned.1.call-done = f32[512,2048]{1,0:T(8,128)} async-done(((f32[512,2048]{1,0:T(8,128)}), f32[512,2048]{1,0:T(8,128)}) %all-reduce.8.cloned.1.call-update) | async-done | bytes 4194320 | tf_op jit(solution)/shard_map/psum | solution.py:154
  131.7 7.2 fusion.82
  139.0 5.1 fusion.14
  148.7 5.1 convolution_add_fusion
  154.0 8.4 fusion.83
  162.4 77.2 %all-reduce.10.cloned.1.call-done = f32[512,2048]{1,0:T(8,128)} async-done(((f32[512,2048]{1,0:T(8,128)}), f32[512,2048]{1,0:T(8,128)}) %all-reduce.10.cloned.1.call-update) | async-done | bytes 4194320 | tf_op jit(solution)/shard_map/psum | solution.py:181
  239.6 5.2 multiply_reduce_fusion
  245.6 3.5 subtract_add_fusion
  263.5 5.1 fusion.85
  272.4 161.6 %all-reduce.12.cloned.1.call-done = (f32[512,2048]{1,0:T(8,128)}, f32[512,2048]{1,0:T(8,128)}, f32[512,128]{0,1:T(8,128)}, f32[512,128]{0,1:T(8,128)}) async-done(((f32[512,2048]{1,0:T(8,128)}, f32[512,2048]{1,0:T(8,128)}, f32[512,128]{0,1:T(8,128)}, f32[512,128]{0,1:T(8,128)}), (f32[512,2048]{1,0:T(8,128)}, f32[512,2048]{1,0:T(8,128)}, f32[512,128]{0,1:T(8,128)}, ...) | async-done | bytes 8912912 | tf_op jit(solution)/shard_map/psum | solution.py:164
  443.8 5.5 fusion.40
  450.9 7.6 fusion.88
  458.5 8.7 fusion.72
  468.8 7.5 fusion.44
  479.9 5.9 fusion.10
  485.8 37.2 %all-reduce.2 = (f32[2048]{0:T(1024)S(1)}, f32[2048]{0:T(1024)S(1)}) all-reduce(f32[2048]{0:T(1024)S(1)} %get-tuple-element.13, f32[2048]{0:T(1024)S(1)} %copy-done.41), channel_id=2, replica_groups=mesh['dp'=8,'mp'=4] {'dp'}, use_global_device_ids=true, to_apply=%region_17.18.clone | all-reduce | flops 4096 | bytes 32768
  524.3 5.6 add_convert_fusion
  534.3 33.9 %reduce-scatter.12.cloned.1.call-done = f32[256,128]{1,0:T(8,128)} async-done(((f32[2048,128]{1,0:T(8,128)}), f32[256,128]{1,0:T(8,128)}) %reduce-scatter.12.cloned.1.call-update) | async-done | bytes 131088 | tf_op jit(solution)/shard_map/reduce_scatter | solution.py:249
  568.2 91.0 %reduce-scatter.8.cloned.1.call-done = f32[256,512]{1,0:T(8,128)} async-done(((f32[2048,512]{1,0:T(8,128)}), f32[256,512]{1,0:T(8,128)}) %reduce-scatter.8.cloned.1.call-update) | async-done | bytes 524304 | tf_op jit(solution)/shard_map/reduce_scatter | solution.py:247
  659.2 92.7 %reduce-scatter.14.cloned.1.call-done = f32[512,256]{1,0:T(8,128)} async-done(((f32[512,2048]{1,0:T(8,128)}), f32[512,256]{1,0:T(8,128)}) %reduce-scatter.14.cloned.1.call-update) | async-done | bytes 524304 | tf_op jit(solution)/shard_map/reduce_scatter | solution.py:250
  751.9 196.6 %reduce-scatter.16.cloned.1.call-done = f32[256,1408]{1,0:T(8,128)} async-done(((f32[2048,1408]{1,0:T(8,128)}), f32[256,1408]{1,0:T(8,128)}) %reduce-scatter.16.cloned.1.call-update) | async-done | bytes 1441808 | tf_op jit(solution)/shard_map/reduce_scatter | solution.py:252
  948.6 196.0 %reduce-scatter.18.cloned.1.call-done = f32[256,1408]{1,0:T(8,128)} async-done(((f32[2048,1408]{1,0:T(8,128)}), f32[256,1408]{1,0:T(8,128)}) %reduce-scatter.18.cloned.1.call-update) | async-done | bytes 1441808 | tf_op jit(solution)/shard_map/reduce_scatter | solution.py:253
  1144.6 196.2 %reduce-scatter.20.cloned.1.call-done = f32[1408,256]{1,0:T(8,128)} async-done(((f32[1408,2048]{1,0:T(8,128)}), f32[1408,256]{1,0:T(8,128)}) %reduce-scatter.20.cloned.1.call-update) | async-done | bytes 1441808 | tf_op jit(solution)/shard_map/reduce_scatter | solution.py:254
  (203 shorter events, 80.3 us)
Async XLA Ops:
  7.2 27.2 %copy-start = (bf16[512,2048]{1,0:T(8,128)(2,1)S(1)}, bf16[512,2048]{1,0:T(8,128)(2,1)}, u32[]{:S(2)}) copy-start(bf16[512,2048]{1,0:T(8,128)(2,1)} %param.19) | copy-start | bytes 6291460
  7.2 118.9 %all-reduce.8.cloned.1.call-start = ((), (), s32[]{:S(2)}) async-start(), calls=%async_computation.7 | async-start | bytes 8388608 | tf_op jit(solution)/shard_map/psum | solution.py:154
  37.7 201.9 %all-reduce.10.cloned.1.call-start = ((), (), s32[]{:S(2)}) async-start(), calls=%async_computation.8 | async-start | bytes 8388608 | tf_op jit(solution)/shard_map/psum | solution.py:181
  38.0 206.9 %copy-start.42 = (f32[512]{0:T(512)}, f32[512]{0:T(512)S(1)}, u32[]{:S(2)}) copy-start(f32[512]{0:T(512)S(1)} %fusion.69) | copy-start | bytes 6148
  45.8 83.8 %copy-start.40 = (f32[2048]{0:T(1024)S(1)}, f32[2048]{0:T(1024)}, u32[]{:S(2)}) copy-start(f32[2048]{0:T(1024)} %param.20) | copy-start | bytes 24580
  129.6 9.3 slice-start.2
  131.7 7.2 slice-start.3
  131.7 7.2 copy-start.53
  131.7 13.5 %slice-start = ((s8[5767168]{0:T(1024)(128)(4,1)}), s8[4194304]{0:T(1024)(128)(4,1)S(1)}, s32[]{:S(2)}) async-start(s8[5767168]{0:T(1024)(128)(4,1)} %bitcast.122), calls=%async_computation.17 | async-start | bytes 8388608
  139.0 9.7 copy-start.52
  153.8 280.1 %all-reduce.12.cloned.1.call-start = ((), (), s32[]{:S(2)}) async-start(), calls=%async_computation.16 | async-start | bytes 17825792 | tf_op jit(solution)/shard_map/psum | solution.py:164
  153.9 104.2 %copy-start.45 = (bf16[256]{0:T(256)(128)(2,1)}, bf16[256]{0:T(256)(128)(2,1)S(1)}, u32[]{:S(2)}) copy-start(bf16[256]{0:T(256)(128)(2,1)S(1)} %get-tuple-element.58) | copy-start | bytes 1540
  271.3 163.8 %copy-start.48 = (f32[64]{0:T(128)S(1)}, f32[64]{0:T(128)}, u32[]{:S(2)}) copy-start(f32[64]{0:T(128)} %multiply_power_fusion) | copy-start | bytes 772
  271.3 164.4 %copy-start.3 = (bf16[512,2048]{1,0:T(8,128)(2,1)S(1)}, bf16[512,2048]{1,0:T(8,128)(2,1)}, u32[]{:S(2)}) copy-start(bf16[512,2048]{1,0:T(8,128)(2,1)} %copy-done.2) | copy-start | bytes 6291460
  271.3 263.0 %reduce-scatter.10.cloned.1.call-start = ((), (), s32[]{:S(2)}) async-start(), calls=%async_computation.10 | async-start | bytes 1179648 | tf_op jit(solution)/shard_map/reduce_scatter | solution.py:248
  437.4 130.8 %reduce-scatter.12.cloned.1.call-start = ((), (), s32[]{:S(2)}) async-start(), calls=%async_computation.11 | async-start | bytes 1179648 | tf_op jit(solution)/shard_map/reduce_scatter | solution.py:249
  439.2 220.0 %reduce-scatter.8.cloned.1.call-start = ((), (), s32[]{:S(2)}) async-start(), calls=%async_computation.9 | async-start | bytes 4718592 | tf_op jit(solution)/shard_map/reduce_scatter | solution.py:247
  442.7 309.2 %reduce-scatter.14.cloned.1.call-start = ((), (), s32[]{:S(2)}) async-start(), calls=%async_computation.12 | async-start | bytes 4718592 | tf_op jit(solution)/shard_map/reduce_scatter | solution.py:250
  449.3 499.3 %reduce-scatter.16.cloned.1.call-start = ((), (), s32[]{:S(2)}) async-start(), calls=%async_computation.13 | async-start | bytes 12976128 | tf_op jit(solution)/shard_map/reduce_scatter | solution.py:252
  458.5 686.1 %reduce-scatter.18.cloned.1.call-start = ((), (), s32[]{:S(2)}) async-start(), calls=%async_computation.14 | async-start | bytes 12976128 | tf_op jit(solution)/shard_map/reduce_scatter | solution.py:253
  467.2 873.6 %reduce-scatter.20.cloned.1.call-start = ((), (), s32[]{:S(2)}) async-start(), calls=%async_computation.15 | async-start | bytes 12976128 | tf_op jit(solution)/shard_map/reduce_scatter | solution.py:254
  524.3 7.3 copy-start.15
  524.3 7.3 copy-start.44
  531.6 809.2 %copy-start.1 = (bf16[512,2048]{1,0:T(8,128)(2,1)S(1)}, bf16[512,2048]{1,0:T(8,128)(2,1)}, u32[]{:S(2)}) copy-start(bf16[512,2048]{1,0:T(8,128)(2,1)} %param.19) | copy-start | bytes 6291460
  (44 other events, 118.0 us)
Sparse Core Ops, SparseCore 0:
  37.8 88.1 all-reduce.7
  154.0 85.6 all-reduce.9
  271.4 162.5 all-reduce.11
  437.8 63.5 reduce-scatter.9
  505.6 62.4 reduce-scatter.11
  572.2 86.9 reduce-scatter.7
  663.8 88.0 reduce-scatter.13
  756.1 192.4 reduce-scatter.15
  952.7 191.8 reduce-scatter.17
  1148.6 192.1 reduce-scatter.19
where the time goes:
time: 1360 us; the launch traced here: 1350 us
  waiting for transfers between devices  1130 us (83%)
  matrix products  107 us (8%)
  blocking collectives  37.2 us (3%)
  other arithmetic  33.4 us (2%)
  local copies, waits for them, and re-layouts  27.7 us (2%)
  between operations  16.4 us (1%)
    reduce_scatter x1, waiting for transfers between devices, shards(): lax.psum_scatter(grad_w_gate, 'dp', scatter_dimension=0, tiled=True)  197 us
    reduce_scatter x1, waiting for transfers between devices, shards(): lax.psum_scatter(grad_w_down, 'dp', scatter_dimension=1, tiled=True)  196 us
    reduce_scatter x1, waiting for transfers between devices, shards(): lax.psum_scatter(grad_w_up, 'dp', scatter_dimension=0, tiled=True)  196 us
    psum x1, waiting for transfers between devices, shards(): result = hidden_stream + lax.psum(down_part, 'mp')  162 us
    reduce_scatter x1, waiting for transfers between devices, shards(): lax.psum_scatter(grad_w_out, 'dp', scatter_dimension=1, tiled=True)  92.7 us
    reduce_scatter x1, waiting for transfers between devices, shards(): lax.psum_scatter(grad_w_query, 'dp', scatter_dimension=0, tiled=True)  91 us
    psum x1, waiting for transfers between devices, shards(): hidden_stream = stream + lax.psum(attention_part, 'mp')  80.3 us
    psum x1, waiting for transfers between devices, shards(): grad_normed_mid = lax.psum(mid_part, 'mp')  77.2 us
  transfers between devices with their start and end apart: 10, of which 9 were waited for; matrix products, arithmetic and copies ran while one was open for 5% of the time, Pallas kernels for 0%

commit v1 on v0

v1 whole, which is shorter than its diff:
```python
import jax
import jax.numpy as jnp
from jax import lax
from jax.sharding import Mesh, PartitionSpec as P

epsilon = 1e-06
masked_value = -1e30
GROUP = 4
f32 = jnp.float32
bf16 = jnp.bfloat16


def dot(a, b):
    return jnp.dot(a, b, preferred_element_type=f32)


def dot_nt(a, b):
    return lax.dot_general(a, b, (((1,), (1,)), ((), ())), preferred_element_type=f32)


def dot_tn(a, b):
    return lax.dot_general(a, b, (((0,), (0,)), ((), ())), preferred_element_type=f32)


def swap(a, axis):
    return lax.ppermute(a, axis, [(0, 1), (1, 0)])


def relative(a):
    q = a.shape[0] // 4
    c, y = lax.axis_index("c"), lax.axis_index("y")
    me = 2 * c + y
    parts = [lax.dynamic_slice_in_dim(a, (me ^ k) * q, q, 0) for k in range(4)]
    return jnp.concatenate(parts, axis=0)


def rotary_tables(positions, size):
    half_size = size // 2
    inverse = 10000.0 ** (-2.0 * jnp.arange(half_size, dtype=f32) / size)
    angles = positions.astype(f32)[:, None] * inverse[None, :]
    return (jnp.cos(angles), jnp.sin(angles))


def rotate(values, cosine_table, sine_table):
    half_size = values.shape[-1] // 2
    a, b = values[..., :half_size], values[..., half_size:]
    return jnp.concatenate([a * cosine_table - b * sine_table, b * cosine_table + a * sine_table], axis=-1)


def unrotate(values, cosine_table, sine_table):
    return rotate(values, cosine_table, -sine_table)


def norm_back(stream, inverse_rms, gain, grad_normed):
    weighted = gain * grad_normed
    return inverse_rms * weighted - stream * inverse_rms**3 * jnp.mean(weighted * stream, axis=-1, keepdims=True)


def reduce_half(part):
    h = part.shape[0] // 2
    q = h // 2
    mine = part[:h] + swap(part[h:], "c")
    own = mine[:q] + swap(mine[q:], "y")
    return jnp.concatenate([own, swap(own, "y")], axis=0)


def reduce_full(part):
    half = reduce_half(part)
    return jnp.concatenate([half, swap(half, "c")], axis=0)


def remote_blocks(gathered):
    z = lax.axis_index("z")
    return jnp.stack(
        [
            lax.dynamic_index_in_dim(gathered, lax.rem(z + k, GROUP), 0, keepdims=False)
            for k in range(1, GROUP)
        ]
    )


def ffn_pre(normed_mid, w_gate, w_up):
    gate = dot(normed_mid, w_gate)
    up = dot(normed_mid, w_up)
    sig = jax.nn.sigmoid(gate)
    return gate, up, sig


def ffn_back(gate, up, sig, grad_mixed):
    grad_mixed = grad_mixed.astype(bf16).astype(f32)
    grad_gate = (grad_mixed * up * sig * (1.0 + gate * (1.0 - sig))).astype(bf16)
    grad_up = (grad_mixed * gate * sig).astype(bf16)
    return grad_gate, grad_up


def scores_of(query_block, key_rot, pos_q, pos_k, length, score_scale):
    scores = jnp.einsum("qhe,ke->hqk", query_block, key_rot, preferred_element_type=f32) * score_scale
    allowed = (pos_k[None, :] <= pos_q[:, None]) & (pos_k[None, :] < length)
    return jnp.where(allowed[None], scores, masked_value)


def shards(
    sizes,
    inputs,
    seq_lengths,
    norm_in,
    w_query,
    w_key,
    w_value,
    w_out,
    norm_mid,
    w_gate,
    w_up,
    w_down,
    out_cotangent,
    kv_cotangent,
):
    n_outer, n_dp = sizes
    dp_axes = ("o", "z", "x")
    seq_len, width = inputs.shape
    half, quarter = seq_len // 2, seq_len // 4
    head = w_key.shape[1]
    heads = w_query.shape[1] // head
    score_scale = head ** (-0.5)
    rows = width // n_dp
    z, x = lax.axis_index("z"), lax.axis_index("x")
    length = seq_lengths[0]
    one = jnp.minimum(length, 1).astype(f32)
    positions = relative(jnp.arange(seq_len))
    valid = (positions < length).astype(f32)[:, None]
    stream = relative(inputs).astype(f32)
    grad_out = relative(out_cotangent).astype(f32) * valid
    cosine, sine = rotary_tables(positions, head)

    go_z = lax.all_gather(grad_out[:quarter], "z", axis=0, tiled=False)

    inverse_in = lax.rsqrt(jnp.mean(stream * stream, axis=-1, keepdims=True) + epsilon)
    normed = (stream * inverse_in * norm_in).astype(bf16)
    queries = dot(normed, w_query).reshape(seq_len, heads, head)
    queries = rotate(queries, cosine[:, None, :], sine[:, None, :]).astype(bf16)
    key_rot = rotate(dot(normed, w_key), cosine, sine).astype(bf16)
    value_rows = dot(normed, w_value).astype(bf16)
    attended, logs = [], []
    for b in range(2):
        at = slice(b * half, (b + 1) * half)
        scores = scores_of(queries[at], key_rot, positions[at], positions, length, score_scale)
        row_max = jnp.max(scores, axis=-1, keepdims=True)
        exponent = jnp.exp(scores - row_max)
        totals = jnp.sum(exponent, axis=-1, keepdims=True)
        weights = (exponent / totals).astype(bf16)
        out = jnp.einsum("hqk,ke->qhe", weights, value_rows, preferred_element_type=f32)
        attended.append((out * valid[at][:, :, None]).astype(bf16))
        logs.append(row_max + jnp.log(totals))
    attended = jnp.concatenate(attended, axis=0).reshape(seq_len, heads * head)
    hidden_half = stream[:half] + reduce_half(dot(attended, w_out))
    hidden = jnp.concatenate([hidden_half, swap(hidden_half, "c")], axis=0)

    scaled_half = hidden_half * lax.rsqrt(jnp.mean(hidden_half * hidden_half, axis=-1, keepdims=True) + epsilon)
    nm_z = lax.all_gather(scaled_half, "z", axis=0, tiled=False)

    inverse_mid = lax.rsqrt(jnp.mean(hidden * hidden, axis=-1, keepdims=True) + epsilon)
    normed_mid = (hidden * inverse_mid * norm_mid).astype(bf16)
    gate, up, sig = ffn_pre(normed_mid, w_gate, w_up)
    mixed = (gate * sig * up).astype(bf16)
    grad_down_in = grad_out.astype(bf16)
    grad_gate, grad_up = ffn_back(gate, up, sig, dot_nt(grad_down_in, w_down))
    mid_part = dot_nt(grad_gate, w_gate) + dot_nt(grad_up, w_up)
    grad_normed_mid = reduce_full(mid_part)
    result = hidden + reduce_full(dot(mixed, w_down))
    grad_norm_mid = jnp.sum(grad_normed_mid * hidden * inverse_mid, axis=0)
    grad_hidden = grad_out + norm_back(hidden, inverse_mid, norm_mid, grad_normed_mid)

    grad_attention = grad_hidden.astype(bf16)
    grad_w_out = dot_tn(attended, grad_attention)
    grad_w_out = lax.psum_scatter(grad_w_out, dp_axes, scatter_dimension=1, tiled=True)
    grad_attended = (dot_nt(grad_attention, w_out).astype(bf16) * valid.astype(bf16)).reshape(seq_len, heads, head)
    grad_queries = []
    grad_key = jnp.zeros((seq_len, head), f32)
    grad_value = jnp.zeros((seq_len, head), f32)
    for b in range(2):
        at = slice(b * half, (b + 1) * half)
        scores = scores_of(queries[at], key_rot, positions[at], positions, length, score_scale)
        probs = jnp.exp(scores - logs[b])
        grad_probs = jnp.einsum("qhe,ke->hqk", grad_attended[at], value_rows, preferred_element_type=f32)
        delta = jnp.sum(probs * grad_probs, axis=-1, keepdims=True)
        grad_scores = (probs * (grad_probs - delta)).astype(bf16)
        grad_queries.append(jnp.einsum("hqk,ke->qhe", grad_scores, key_rot, preferred_element_type=f32) * score_scale)
        grad_key += jnp.einsum("hqk,qhe->ke", grad_scores, queries[at], preferred_element_type=f32) * score_scale
        grad_value += jnp.einsum("hqk,qhe->ke", probs.astype(bf16), grad_attended[at], preferred_element_type=f32)
    grad_query = unrotate(jnp.concatenate(grad_queries, axis=0), cosine[:, None, :], sine[:, None, :])
    grad_query = grad_query.astype(bf16).reshape(seq_len, heads * head)
    grad_w_query = dot_tn(normed, grad_query)
    grad_w_query = lax.psum_scatter(grad_w_query, dp_axes, scatter_dimension=0, tiled=True)
    grad_kv = reduce_full(jnp.concatenate([grad_key, grad_value], axis=1))
    summed_input = reduce_full(dot_nt(grad_query, w_query))
    grad_kv = grad_kv + relative(kv_cotangent).astype(f32) * valid
    grad_key = unrotate(grad_kv[:, :head], cosine, sine).astype(bf16)
    grad_value = grad_kv[:, head:].astype(bf16)
    grad_w_key = dot_tn(normed, grad_key)
    grad_w_value = dot_tn(normed, grad_value)
    grad_normed = summed_input + dot_nt(grad_key, w_key) + dot_nt(grad_value, w_value)
    grad_norm_in = jnp.sum(grad_normed * stream * inverse_in, axis=0)
    grad_inputs = grad_hidden + norm_back(stream, inverse_in, norm_in, grad_normed)

    piece = rows // 4
    m = 2 * lax.axis_index("y") + lax.axis_index("c")
    kv = jnp.concatenate([grad_w_key, grad_w_value], axis=1).reshape(n_dp, 4, piece, 2 * head)
    kv = lax.dynamic_index_in_dim(kv, m, 1, keepdims=False)
    gains = jnp.stack([grad_norm_in, grad_norm_mid]).reshape(2, n_dp, rows).transpose(1, 0, 2)
    gains = gains.reshape(n_dp, 2 * rows // (2 * head) if rows >= 2 * head else 2, -1)
    gains = jnp.pad(gains, ((0, 0), (0, 6), (0, 2 * head - gains.shape[2])))
    small = lax.psum_scatter(jnp.concatenate([kv, gains], axis=1), dp_axes, scatter_dimension=0, tiled=True)[0]
    kv = lax.all_gather(small[:piece], ("y", "c"), axis=0, tiled=True)
    out_norm_in, out_norm_mid = small[piece, :rows], small[piece + 1, :rows]

    go_own = remote_blocks(go_z)
    go_other = swap(go_own, "y")
    go_half = jnp.concatenate([go_own, go_other], axis=1)
    go_halves = (go_half, swap(go_half, "c"))
    nm_half = remote_blocks(nm_z)
    nm_halves = (nm_half, swap(nm_half, "c"))
    all_nm, all_go, all_mixed, all_gate, all_up = [normed_mid], [grad_down_in], [mixed], [grad_gate], [grad_up]
    for nm, go in zip(nm_halves, go_halves):
        nm = (nm.reshape(-1, width) * norm_mid).astype(bf16)
        go = (go.reshape(-1, width) * one).astype(bf16)
        gate, up, sig = ffn_pre(nm, w_gate, w_up)
        gg, gu = ffn_back(gate, up, sig, dot_nt(go, w_down))
        all_nm.append(nm)
        all_go.append(go)
        all_mixed.append((gate * sig * up).astype(bf16))
        all_gate.append(gg)
        all_up.append(gu)

    def columns(parts, which):
        taken = []
        for part in parts:
            part = part.reshape(-1, n_outer, GROUP, 2, rows)
            part = lax.dynamic_index_in_dim(part, z, 2, keepdims=False)
            part = lax.dynamic_index_in_dim(part, which, 2, keepdims=False)
            taken.append(part.reshape(-1, n_outer * rows))
        return jnp.concatenate(taken, axis=0)

    all_mixed = jnp.concatenate(all_mixed, axis=0)
    all_gate = jnp.concatenate(all_gate, axis=0)
    all_up = jnp.concatenate(all_up, axis=0)
    nm_send, nm_keep = columns(all_nm, 1 - x), columns(all_nm, x)
    go_send, go_keep = columns(all_go, 1 - x), columns(all_go, x)
    grad_w_down = dot_tn(all_mixed, go_keep) + swap(dot_tn(all_mixed, go_send), "x")
    grad_w_gate = dot_tn(nm_keep, all_gate) + swap(dot_tn(nm_send, all_gate), "x")
    grad_w_up = dot_tn(nm_keep, all_up) + swap(dot_tn(nm_send, all_up), "x")
    if n_outer > 1:
        grad_w_down = lax.psum_scatter(grad_w_down, "o", scatter_dimension=1, tiled=True)
        grad_w_gate = lax.psum_scatter(grad_w_gate, "o", scatter_dimension=0, tiled=True)
        grad_w_up = lax.psum_scatter(grad_w_up, "o", scatter_dimension=0, tiled=True)

    return (
        relative(result.astype(bf16)),
        relative(grad_inputs.astype(bf16)),
        out_norm_in,
        grad_w_query,
        kv[:, :head],
        kv[:, head:],
        grad_w_out,
        out_norm_mid,
        grad_w_gate,
        grad_w_up,
        grad_w_down,
    )


def solution(mesh):
    n_dp = mesh.shape["dp"]
    n_outer = n_dp // (2 * GROUP)
    split = Mesh(mesh.devices.reshape(n_outer, GROUP, 2, 2, 2), ("o", "z", "x", "y", "c"))
    dp, mp = ("o", "z", "x"), ("y", "c")

    def program(*args):
        return shards((n_outer, n_dp), *args)

    return jax.shard_map(
        program,
        mesh=split,
        in_specs=(
            P(dp, None),
            P(dp),
            P(),
            P(None, mp),
            P(),
            P(),
            P(mp, None),
            P(),
            P(None, mp),
            P(None, mp),
            P(mp, None),
            P(dp, None),
            P(dp, None),
        ),
        out_specs=(
            P(dp, None),
            P(dp, None),
            P(dp),
            P(dp, mp),
            P(dp, None),
            P(dp, None),
            P(mp, dp),
            P(dp),
            P(dp, mp),
            P(dp, mp),
            P(mp, dp),
        ),
        check_vma=False,
    )
```

time: 1360 us -> 740 us (0.54)
  waiting for transfers between devices: 1130 us -> 332 us
  local copies, waits for them, and re-layouts: 27.7 us -> 110 us
  other arithmetic: 33.4 us -> 99.8 us
  matrix products: 107 us -> 141 us
  blocking collectives: 37.2 us -> 5.77 us
  starting transfers between devices: 0.76 us -> 23 us
    reduce_scatter x7 -> x3, waiting for transfers between devices: 807 us -> 0.01 us  [the longest x1 0.01 us: shards(): lax.psum_scatter(jnp.concatenate([kv, gains], axis=1), dp_axes, scatter_d...]
    ppermute x0 -> x26, waiting for transfers between devices: none -> 332 us  [swap(): return lax.ppermute(a, axis, [(0, 1), (1, 0)])]
    psum x3 -> x0, waiting for transfers between devices: 319 us -> none  [the longest x1 162 us: shards(): result = hidden_stream + lax.psum(down_part, 'mp')]
    unnamed x1 -> x0, blocking collectives: 37.2 us -> none
    dot_general x33 -> x42, matrix products: 107 us -> 141 us  [the longest x11 65.2 us: dot(): return jnp.dot(a, b, preferred_element_type=f32)]
    convert_element_type x10 -> x14, other arithmetic: 11.4 us -> 45.1 us  [the longest x2 18.6 us: shards(): nm = (nm.reshape(-1, width) * norm_mid).astype(bf16)]
    dynamic_slice x0 -> x21, local copies, waits for them, and re-layouts: none -> 28.8 us  [the longest x6 14 us: columns(): part = lax.dynamic_index_in_dim(part, which, 2, keepdims=False)]
    ppermute x0 -> x26, starting transfers between devices: none -> 22.8 us  [swap(): return lax.ppermute(a, axis, [(0, 1), (1, 0)])]
  transfers between devices with their start and end apart: 10 -> 31, of which waited for: 9 -> 15; matrix products, arithmetic and copies ran while one was open for 5% -> 39% of each run, Pallas kernels for 0% -> 0%
where the time goes in v1:
time: 740 us; the launch traced here: 730 us
  waiting for transfers between devices  332 us (45%)
  matrix products  141 us (19%)
  local copies, waits for them, and re-layouts  110 us (15%)
  other arithmetic  99.8 us (13%)
  starting transfers between devices  23 us (3%)
  between operations  18.6 us (3%)
    ppermute x26, waiting for transfers between devices, swap(): return lax.ppermute(a, axis, [(0, 1), (1, 0)])  332 us
    dot_general x11, matrix products, dot(): return jnp.dot(a, b, preferred_element_type=f32)  65.2 us
    dot_general x9, matrix products, dot_nt(): lax.dot_general(a, b, (((1,), (1,)), ((), ())), preferred_element_type=f32)  47.8 us
    ppermute x26, starting transfers between devices, swap(): return lax.ppermute(a, axis, [(0, 1), (1, 0)])  22.8 us
    dot_general x10, matrix products, dot_tn(): lax.dot_general(a, b, (((0,), (0,)), ((), ())), preferred_element_type=f32)  21.6 us
    unnamed x300, local copies, waits for them, and re-layouts  19.6 us
    convert_element_type x2, other arithmetic, shards(): nm = (nm.reshape(-1, width) * norm_mid).astype(bf16)  18.6 us
    reshape x2, local copies, waits for them, and re-layouts, shards(): nm = (nm.reshape(-1, width) * norm_mid).astype(bf16)  18.6 us
  transfers between devices with their start and end apart: 31, of which 15 were waited for; matrix products, arithmetic and copies ran while one was open for 39% of the time, Pallas kernels for 0%

profile of v1, /device:TPU:0, one launch (start us, length us, event | category | flops | bytes accessed | tf_op | source)
XLA Modules:
  0.0 729.9 jit_solution(5786853230265333913)
XLA Ops:
  48.7 23.5 %collective-permute-done.1 = f32[128,2048]{1,0:T(8,128)S(1)} collective-permute-done((f32[128,2048]{1,0:T(8,128)S(1)}, f32[128,2048]{1,0:T(8,128)S(1)}, u32[]{:S(2)}, u32[]{:S(2)}) %collective-permute-start.1) | collective-permute-done | bytes 1048608 | tf_op jit(solution)/shard_map/ppermute | solution.py:26
  74.7 22.4 %collective-permute-done.2 = f32[128,2048]{1,0:T(8,128)S(1)} collective-permute-done((f32[128,2048]{1,0:T(8,128)S(1)}, f32[128,2048]{1,0:T(8,128)S(1)}, u32[]{:S(2)}, u32[]{:S(2)}) %collective-permute-start.2) | collective-permute-done | bytes 1048608 | tf_op jit(solution)/shard_map/ppermute | solution.py:26
  110.6 7.3 %fusion.28 = (bf16[512,1408]{1,0:T(8,128)(2,1)S(1)}, bf16[512,1408]{1,0:T(8,128)(2,1)}, bf16[512,1408]{1,0:T(8,128)(2,1)}) fusion(bf16[512,1408]{1,0:T(8,128)(2,1)} %convolution_convert_fusion.2, f32[512,1408]{1,0:T(8,128)} %fusion.106, bf16[2048,1408]{1,0:T(8,128)(2,1)S(1)} %bitcast.219, f32[2048]{0:T(1024)S(1)} %copy-done.98, ...), kind=kOutput, calls=%fused_computation.71 | convolution fusion | flops 2969239552 | bytes 18622464 | tf_op jit(solution)/shard_map/dot_general | solution.py:14
  146.0 21.9 %collective-permute-done.9 = f32[128,2048]{1,0:T(8,128)S(1)} collective-permute-done((f32[128,2048]{1,0:T(8,128)S(1)}, f32[128,2048]{1,0:T(8,128)S(1)}, u32[]{:S(2)}, u32[]{:S(2)}) %collective-permute-start.9) | collective-permute-done | bytes 1048608 | tf_op jit(solution)/shard_map/ppermute | solution.py:26
  169.6 20.9 %collective-permute-done.5 = f32[128,2048]{1,0:T(8,128)S(1)} collective-permute-done((f32[128,2048]{1,0:T(8,128)S(1)}, f32[128,2048]{1,0:T(8,128)S(1)}, u32[]{:S(2)}, u32[]{:S(2)}) %collective-permute-start.5) | collective-permute-done | bytes 1048608 | tf_op jit(solution)/shard_map/ppermute | solution.py:26
  192.0 20.9 %collective-permute-done.10 = f32[128,2048]{1,0:T(8,128)S(1)} collective-permute-done((f32[128,2048]{1,0:T(8,128)S(1)}, f32[128,2048]{1,0:T(8,128)S(1)}, u32[]{:S(2)}, u32[]{:S(2)}) %collective-permute-start.10) | collective-permute-done | bytes 1048608 | tf_op jit(solution)/shard_map/ppermute | solution.py:26
  214.5 19.9 %collective-permute-done.6 = f32[128,2048]{1,0:T(8,128)S(1)} collective-permute-done((f32[128,2048]{1,0:T(8,128)S(1)}, f32[128,2048]{1,0:T(8,128)S(1)}, u32[]{:S(2)}, u32[]{:S(2)}) %collective-permute-start.6) | collective-permute-done | bytes 1048608 | tf_op jit(solution)/shard_map/ppermute | solution.py:26
  249.2 10.1 %subtract_add_fusion = (f32[512,2048]{1,0:T(8,128)S(1)}, bf16[512,2048]{1,0:T(8,128)(2,1)}) fusion(f32[512]{0:T(512)S(1)} %broadcast_multiply_fusion.2, f32[512]{0:T(512)S(1)} %copy-done.119, f32[2048]{0:T(1024)S(1)} %copy-done.98, f32[512]{0:T(512)S(1)} %copy-done.110, f32[256,2048]{1,0:T(8,128)} %collective-permute-done.11, f32[128,2048]{1,0:T(8,128)S(1)} %copy-done.38, ...), kind=kLoop, calls=%fused_computation.57 | loop fusion | flops 23068672 | bytes 20987904 | tf_op jit(solution)/shard_map/add | solution.py:171
  280.1 21.7 %collective-permute-done.13 = f32[128,2048]{1,0:T(8,128)S(1)} collective-permute-done((f32[128,2048]{1,0:T(8,128)S(1)}, f32[128,2048]{1,0:T(8,128)S(1)}, u32[]{:S(2)}, u32[]{:S(2)}) %collective-permute-start.13) | collective-permute-done | bytes 1048608 | tf_op jit(solution)/shard_map/ppermute | solution.py:26
  304.2 25.4 %collective-permute-done.17 = f32[128,256]{0,1:T(8,128)S(1)} collective-permute-done((f32[128,256]{0,1:T(8,128)S(1)}, f32[128,256]{0,1:T(8,128)S(1)}, u32[]{:S(2)}, u32[]{:S(2)}) %collective-permute-start.17) | collective-permute-done | bytes 131104 | tf_op jit(solution)/shard_map/ppermute | solution.py:26
  367.3 65.6 %collective-permute-done.21 = f32[3,128,2048]{2,1,0:T(8,128)} collective-permute-done((f32[3,128,2048]{2,1,0:T(8,128)}, f32[3,128,2048]{2,1,0:T(8,128)}, u32[]{:S(2)}, u32[]{:S(2)}) %collective-permute-start.21) | collective-permute-done | bytes 3145760 | tf_op jit(solution)/shard_map/ppermute | solution.py:26
  478.1 9.6 %convolution_convert_fusion.1 = bf16[768,1408]{1,0:T(8,128)(2,1)} fusion(bf16[768,2048]{1,0:T(8,128)(2,1)} %bitcast.177, bf16[1408,2048]{1,0:T(8,128)(2,1)} %param.23), kind=kOutput, calls=%fused_computation.65 | convolution fusion | flops 4430266368 | bytes 11075584 | tf_op jit(solution)/shard_map/dot_general | solution.py:18
  513.4 8.9 %convolution_convert_fusion = bf16[768,1408]{1,0:T(8,128)(2,1)} fusion(bf16[768,2048]{1,0:T(8,128)(2,1)S(1)} %bitcast.178, bf16[1408,2048]{1,0:T(8,128)(2,1)} %param.23), kind=kOutput, calls=%fused_computation.64 | convolution fusion | flops 4430266368 | bytes 11075584 | tf_op jit(solution)/shard_map/dot_general | solution.py:18
  522.4 9.3 %reshape.676 = f32[768,1,4,2,256]{4,3,2,0,1:T(2,128)} reshape(f32[3,256,2048]{2,1,0:T(8,128)} %pad_maximum_fusion) | data formatting | bytes 12582912 | tf_op jit(solution)/shard_map/reshape | solution.py:224
  546.2 6.8 fusion.1
  553.1 11.6 %fusion.122 = f32[768,1408]{1,0:T(8,128)} fusion(bf16[768,2048]{1,0:T(8,128)(2,1)S(1)} %get-tuple-element.89, bf16[2048,1408]{1,0:T(8,128)(2,1)} %param.21), kind=kOutput, calls=%fused_computation.297 | convolution fusion | flops 4429185024 | bytes 13238272 | tf_op jit(solution)/shard_map/dot_general | solution.py:14
  564.6 9.4 %fusion.123 = f32[768,1408]{1,0:T(8,128)} fusion(bf16[768,2048]{1,0:T(8,128)(2,1)S(1)} %get-tuple-element.90, bf16[2048,1408]{1,0:T(8,128)(2,1)} %param.21), kind=kOutput, calls=%fused_computation.298 | convolution fusion | flops 4429185024 | bytes 13238272 | tf_op jit(solution)/shard_map/dot_general | solution.py:14
  574.0 9.3 %reshape.678 = f32[768,1,4,2,256]{4,3,2,0,1:T(2,128)} reshape(f32[3,256,2048]{2,1,0:T(8,128)} %collective-permute-done.20) | data formatting | bytes 12582912 | tf_op jit(solution)/shard_map/reshape | solution.py:224
  583.3 11.8 %multiply_convert_fusion.3 = (bf16[768,1,4,2,256]{4,3,2,0,1:T(2,128)(2,1)}, bf16[768,1,4,2,256]{4,3,2,0,1:T(2,128)(2,1)}) fusion(f32[768,1,4,2,256]{4,3,2,0,1:T(2,128)} %reshape.676, f32[4,2,256]{2,1,0:T(2,128)S(1)} %mul.621, f32[768,1,4,2,256]{4,3,2,0,1:T(2,128)} %reshape.678), kind=kLoop, calls=%fused_computation.9 | loop fusion | flops 6291456 | bytes 18882560 | tf_op jit(solution)/shard_map/convert_element_type | solution.py:224
  600.9 11.6 %multiply_convert_fusion.5 = (bf16[768,1408]{1,0:T(8,128)(2,1)}, bf16[768,1408]{1,0:T(8,128)(2,1)S(1)}, bf16[768,1408]{1,0:T(8,128)(2,1)S(1)}) fusion(f32[768,1408]{1,0:T(8,128)} %fusion.122, bf16[768,1408]{1,0:T(8,128)(2,1)S(1)} %copy-done.132, bf16[768,2048]{1,0:T(8,128)(2,1)S(1)} %copy-done.70, bf16[2048,1408]{1,0:T(8,128)(2,1)} %param.22), kind=kOutput, calls=%fused_computation.33 | convolution fusion | flops 4447567872 | bytes 21889024 | tf_op jit(solution)/shard_map/dot_general | solution.py:14
  612.5 9.1 %multiply_convert_fusion.4 = (bf16[768,1408]{1,0:T(8,128)(2,1)}, bf16[768,1408]{1,0:T(8,128)(2,1)S(1)}, bf16[768,1408]{1,0:T(8,128)(2,1)S(1)}) fusion(f32[768,1408]{1,0:T(8,128)S(1)} %bitcast.223, bf16[768,1408]{1,0:T(8,128)(2,1)} %convolution_convert_fusion, bf16[768,2048]{1,0:T(8,128)(2,1)S(1)} %copy-done.68, bf16[2048,1408]{1,0:T(8,128)(2,1)S(1)} %bitcast.221), kind=kOutput, calls=%fused_computation.32 | convolution fusion | flops 4447567872 | bytes 21889024 | tf_op jit(solution)/shard_map/dot_general | solution.py:14
  633.1 24.9 %collective-permute-done.24 = f32[256,1408]{1,0:T(8,128)S(1)} collective-permute-done((f32[256,1408]{1,0:T(8,128)S(1)}, f32[256,1408]{1,0:T(8,128)S(1)}, u32[]{:S(2)}, u32[]{:S(2)}) %collective-permute-start.24) | collective-permute-done | bytes 1441824 | tf_op jit(solution)/shard_map/ppermute | solution.py:26
  660.9 27.9 %collective-permute-done.23 = f32[256,1408]{1,0:T(8,128)S(1)} collective-permute-done((f32[256,1408]{1,0:T(8,128)S(1)}, f32[256,1408]{1,0:T(8,128)S(1)}, u32[]{:S(2)}, u32[]{:S(2)}) %collective-permute-start.23) | collective-permute-done | bytes 1441824 | tf_op jit(solution)/shard_map/ppermute | solution.py:26
  691.8 27.3 %collective-permute-done.25 = f32[1408,256]{1,0:T(8,128)S(1)} collective-permute-done((f32[1408,256]{1,0:T(8,128)S(1)}, f32[1408,256]{1,0:T(8,128)S(1)}, u32[]{:S(2)}, u32[]{:S(2)}) %collective-permute-start.25) | collective-permute-done | bytes 1441824 | tf_op jit(solution)/shard_map/ppermute | solution.py:26
  (511 shorter events, 274.3 us)
Async XLA Ops:
  8.0 329.4 %all-gather.8.cloned.1.call-start = ((), (), s32[]{:S(2)}) async-start(), calls=%async_computation.7 | async-start | bytes 5242880 | tf_op jit(solution)/shard_map/all_gather | solution.py:135
  45.8 26.4 %collective-permute-start.1 = (f32[128,2048]{1,0:T(8,128)S(1)}, f32[128,2048]{1,0:T(8,128)S(1)}, u32[]{:S(2)}, u32[]{:S(2)}) collective-permute-start(f32[128,2048]{1,0:T(8,128)S(1)} %slice.210), channel_id=1, source_target_pairs={{0,2},{2,0},{1,3},{3,1},{4,6},{6,4},{5,7},{7,5},{8,10},{10,8},{9,1... | collective-permute-start | bytes 3145736 | tf_op jit(solution)/shard_map/ppermute | solution.py:26
  72.3 24.8 %collective-permute-start.2 = (f32[128,2048]{1,0:T(8,128)S(1)}, f32[128,2048]{1,0:T(8,128)S(1)}, u32[]{:S(2)}, u32[]{:S(2)}) collective-permute-start(f32[128,2048]{1,0:T(8,128)S(1)} %slice_add_fusion.8), channel_id=1, source_target_pairs={{0,2},{2,0},{1,3},{3,1},{4,6},{6,4},{5,7},{7,5},{8,10},{10,8},{9,1... | collective-permute-start | bytes 3145736 | tf_op jit(solution)/shard_map/ppermute | solution.py:26
  139.1 308.2 %all-gather.6.cloned.1.call-start = ((), (), s32[]{:S(2)}) async-start(), calls=%async_computation.6 | async-start | bytes 10485760 | tf_op jit(solution)/shard_map/all_gather | solution.py:159
  141.9 26.1 %collective-permute-start.9 = (f32[128,2048]{1,0:T(8,128)S(1)}, f32[128,2048]{1,0:T(8,128)S(1)}, u32[]{:S(2)}, u32[]{:S(2)}) collective-permute-start(f32[128,2048]{1,0:T(8,128)S(1)} %slice.218), channel_id=1, source_target_pairs={{0,2},{2,0},{1,3},{3,1},{4,6},{6,4},{5,7},{7,5},{8,10},{10,8},{9,1... | collective-permute-start | bytes 3145736 | tf_op jit(solution)/shard_map/ppermute | solution.py:26
  145.4 45.1 %collective-permute-start.5 = (f32[128,2048]{1,0:T(8,128)S(1)}, f32[128,2048]{1,0:T(8,128)S(1)}, u32[]{:S(2)}, u32[]{:S(2)}) collective-permute-start(f32[128,2048]{1,0:T(8,128)S(1)} %slice.214), channel_id=1, source_target_pairs={{0,2},{2,0},{1,3},{3,1},{4,6},{6,4},{5,7},{7,5},{8,10},{10,8},{9,1... | collective-permute-start | bytes 3145736 | tf_op jit(solution)/shard_map/ppermute | solution.py:26
  168.1 44.8 %collective-permute-start.10 = (f32[128,2048]{1,0:T(8,128)S(1)}, f32[128,2048]{1,0:T(8,128)S(1)}, u32[]{:S(2)}, u32[]{:S(2)}) collective-permute-start(f32[128,2048]{1,0:T(8,128)S(1)} %slice_add_fusion.6), channel_id=1, source_target_pairs={{0,2},{2,0},{1,3},{3,1},{4,6},{6,4},{5,7},{7,5},{8,10},{10,8},{9,1... | collective-permute-start | bytes 3145736 | tf_op jit(solution)/shard_map/ppermute | solution.py:26
  190.6 43.9 %collective-permute-start.6 = (f32[128,2048]{1,0:T(8,128)S(1)}, f32[128,2048]{1,0:T(8,128)S(1)}, u32[]{:S(2)}, u32[]{:S(2)}) collective-permute-start(f32[128,2048]{1,0:T(8,128)S(1)} %slice_add_fusion.7), channel_id=1, source_target_pairs={{0,2},{2,0},{1,3},{3,1},{4,6},{6,4},{5,7},{7,5},{8,10},{10,8},{9,1... | collective-permute-start | bytes 3145736 | tf_op jit(solution)/shard_map/ppermute | solution.py:26
  214.5 29.3 %collective-permute-start.11 = (f32[256,2048]{1,0:T(8,128)}, f32[256,2048]{1,0:T(8,128)}, u32[]{:S(2)}, u32[]{:S(2)}) collective-permute-start(f32[256,2048]{1,0:T(8,128)} %pad_maximum_fusion.17), channel_id=1, source_target_pairs={{0,1},{1,0},{2,3},{3,2},{4,5},{5,4},{6,7},{7,6},{8,9},{9,8},{10,11... | collective-permute-start | bytes 6291464 | tf_op jit(solution)/shard_map/ppermute | solution.py:26
  236.1 12.2 %collective-permute-start.7 = (f32[256,2048]{1,0:T(8,128)}, f32[256,2048]{1,0:T(8,128)}, u32[]{:S(2)}, u32[]{:S(2)}) collective-permute-start(f32[256,2048]{1,0:T(8,128)} %pad_maximum_fusion.15), channel_id=1, source_target_pairs={{0,1},{1,0},{2,3},{3,2},{4,5},{5,4},{6,7},{7,6},{8,9},{9,8},{10,11... | collective-permute-start | bytes 6291464 | tf_op jit(solution)/shard_map/ppermute | solution.py:26
  243.6 295.9 %reduce-scatter.4.cloned.1.call-start = ((), (), s32[]{:S(2)}) async-start(), calls=%async_computation.3 | async-start | bytes 663552 | tf_op jit(solution)/shard_map/reduce_scatter | solution.py:212
  276.3 25.5 %collective-permute-start.13 = (f32[128,2048]{1,0:T(8,128)S(1)}, f32[128,2048]{1,0:T(8,128)S(1)}, u32[]{:S(2)}, u32[]{:S(2)}) collective-permute-start(f32[128,2048]{1,0:T(8,128)S(1)} %slice.226), channel_id=1, source_target_pairs={{0,2},{2,0},{1,3},{3,1},{4,6},{6,4},{5,7},{7,5},{8,10},{10,8},{9,1... | collective-permute-start | bytes 3145736 | tf_op jit(solution)/shard_map/ppermute | solution.py:26
  280.0 23.5 %collective-permute-start.16 = (f32[256,256]{0,1:T(8,128)S(1)}, f32[256,256]{0,1:T(8,128)S(1)}, u32[]{:S(2)}, u32[]{:S(2)}) collective-permute-start(f32[256,256]{0,1:T(8,128)S(1)} %pad_maximum_fusion.30), channel_id=1, source_target_pairs={{0,1},{1,0},{2,3},{3,2},{4,5},{5,4},{6,7},{7,6},{8,9},{9,8},{10,11... | collective-permute-start | bytes 786440 | tf_op jit(solution)/shard_map/ppermute | solution.py:26
  302.0 33.4 %collective-permute-start.14 = (f32[128,2048]{1,0:T(8,128)S(1)}, f32[128,2048]{1,0:T(8,128)S(1)}, u32[]{:S(2)}, u32[]{:S(2)}) collective-permute-start(f32[128,2048]{1,0:T(8,128)S(1)} %slice_add_fusion.5), channel_id=1, source_target_pairs={{0,2},{2,0},{1,3},{3,1},{4,6},{6,4},{5,7},{7,5},{8,10},{10,8},{9,1... | collective-permute-start | bytes 3145736 | tf_op jit(solution)/shard_map/ppermute | solution.py:26
  303.5 26.1 %collective-permute-start.17 = (f32[128,256]{0,1:T(8,128)S(1)}, f32[128,256]{0,1:T(8,128)S(1)}, u32[]{:S(2)}, u32[]{:S(2)}) collective-permute-start(f32[128,256]{0,1:T(8,128)S(1)} %slice.230), channel_id=1, source_target_pairs={{0,2},{2,0},{1,3},{3,1},{4,6},{6,4},{5,7},{7,5},{8,10},{10,8},{9,1... | collective-permute-start | bytes 393224 | tf_op jit(solution)/shard_map/ppermute | solution.py:26
  336.9 14.8 %collective-permute-start.15 = (f32[256,2048]{1,0:T(8,128)}, f32[256,2048]{1,0:T(8,128)}, u32[]{:S(2)}, u32[]{:S(2)}) collective-permute-start(f32[256,2048]{1,0:T(8,128)} %pad_maximum_fusion.18), channel_id=1, source_target_pairs={{0,1},{1,0},{2,3},{3,2},{4,5},{5,4},{6,7},{7,6},{8,9},{9,8},{10,11... | collective-permute-start | bytes 6291464 | tf_op jit(solution)/shard_map/ppermute | solution.py:26
  358.6 363.5 %reduce-scatter.6.cloned.1.call-start = ((), (), s32[]{:S(2)}) async-start(), calls=%async_computation.4 | async-start | bytes 4718592 | tf_op jit(solution)/shard_map/reduce_scatter | solution.py:193
  362.5 70.4 %collective-permute-start.21 = (f32[3,128,2048]{2,1,0:T(8,128)}, f32[3,128,2048]{2,1,0:T(8,128)}, u32[]{:S(2)}, u32[]{:S(2)}) collective-permute-start(f32[3,128,2048]{2,1,0:T(8,128)} %pad_maximum_fusion.7), channel_id=1, source_target_pairs={{0,2},{2,0},{1,3},{3,1},{4,6},{6,4},{5,7},{7,5},{8,10},{10,8},{9,1... | collective-permute-start | bytes 9437192 | tf_op jit(solution)/shard_map/ppermute | solution.py:26
  367.3 354.8 %reduce-scatter.8.cloned.1.call-start = ((), (), s32[]{:S(2)}) async-start(), calls=%async_computation.5 | async-start | bytes 4718592 | tf_op jit(solution)/shard_map/reduce_scatter | solution.py:175
  439.1 55.4 %collective-permute-start.22 = (f32[3,256,2048]{2,1,0:T(8,128)}, f32[3,256,2048]{2,1,0:T(8,128)}, u32[]{:S(2)}, u32[]{:S(2)}) collective-permute-start(f32[3,256,2048]{2,1,0:T(8,128)} %get-tuple-element.30), channel_id=1, source_target_pairs={{0,1},{1,0},{2,3},{3,2},{4,5},{5,4},{6,7},{7,6},{8,9},{9,8},{10,11... | collective-permute-start | bytes 18874376 | tf_op jit(solution)/shard_map/ppermute | solution.py:26
  453.9 92.3 %collective-permute-start.20 = (f32[3,256,2048]{2,1,0:T(8,128)}, f32[3,256,2048]{2,1,0:T(8,128)}, u32[]{:S(2)}, u32[]{:S(2)}) collective-permute-start(f32[3,256,2048]{2,1,0:T(8,128)} %pad_maximum_fusion), channel_id=1, source_target_pairs={{0,1},{1,0},{2,3},{3,2},{4,5},{5,4},{6,7},{7,6},{8,9},{9,8},{10,11... | collective-permute-start | bytes 18874376 | tf_op jit(solution)/shard_map/ppermute | solution.py:26
  623.5 34.5 %collective-permute-start.24 = (f32[256,1408]{1,0:T(8,128)S(1)}, f32[256,1408]{1,0:T(8,128)S(1)}, u32[]{:S(2)}, u32[]{:S(2)}) collective-permute-start(f32[256,1408]{1,0:T(8,128)S(1)} %fusion.32), channel_id=1, source_target_pairs={{0,4},{4,0},{1,5},{5,1},{2,6},{6,2},{3,7},{7,3},{8,12},{12,8},{9,1... | collective-permute-start | bytes 4325384 | tf_op jit(solution)/shard_map/ppermute | solution.py:26
  627.6 61.3 %collective-permute-start.23 = (f32[256,1408]{1,0:T(8,128)S(1)}, f32[256,1408]{1,0:T(8,128)S(1)}, u32[]{:S(2)}, u32[]{:S(2)}) collective-permute-start(f32[256,1408]{1,0:T(8,128)S(1)} %fusion.33), channel_id=1, source_target_pairs={{0,4},{4,0},{1,5},{5,1},{2,6},{6,2},{3,7},{7,3},{8,12},{12,8},{9,1... | collective-permute-start | bytes 4325384 | tf_op jit(solution)/shard_map/ppermute | solution.py:26
  630.6 88.5 %collective-permute-start.25 = (f32[1408,256]{1,0:T(8,128)S(1)}, f32[1408,256]{1,0:T(8,128)S(1)}, u32[]{:S(2)}, u32[]{:S(2)}) collective-permute-start(f32[1408,256]{1,0:T(8,128)S(1)} %fusion.31), channel_id=1, source_target_pairs={{0,4},{4,0},{1,5},{5,1},{2,6},{6,2},{3,7},{7,3},{8,12},{12,8},{9,1... | collective-permute-start | bytes 4325384 | tf_op jit(solution)/shard_map/ppermute | solution.py:26
  (150 other events, 1803.6 us)
Sparse Core Ops, SparseCore 0:
  139.2 81.9 all-gather.7
  243.8 150.9 all-gather.5
Sparse Core Ops, SparseCore 1:
  358.7 86.9 reduce-scatter.3
  450.1 86.8 reduce-scatter.5
  541.0 87.9 reduce-scatter.7

commit v2 on v1

v2 whole, which is shorter than its diff:
```python
import functools

import jax
import jax.numpy as jnp
from jax import lax
from jax.experimental import pallas as pl
from jax.experimental.pallas import tpu as pltpu
from jax.sharding import Mesh, PartitionSpec as P

epsilon = 1e-06
masked_value = -1e30
GROUP = 4
f32 = jnp.float32
bf16 = jnp.bfloat16


def dot(a, b):
    return jnp.dot(a, b, preferred_element_type=f32)


def dot_nt(a, b):
    return lax.dot_general(a, b, (((1,), (1,)), ((), ())), preferred_element_type=f32)


def dot_tn(a, b):
    return lax.dot_general(a, b, (((0,), (0,)), ((), ())), preferred_element_type=f32)


def swap(a, axis):
    return lax.ppermute(a, axis, [(0, 1), (1, 0)])


def relative(a):
    q = a.shape[0] // 4
    c, y = lax.axis_index("c"), lax.axis_index("y")
    me = 2 * c + y
    parts = [lax.dynamic_slice_in_dim(a, (me ^ k) * q, q, 0) for k in range(4)]
    return jnp.concatenate(parts, axis=0)


def rotary_tables(positions, size):
    half_size = size // 2
    inverse = 10000.0 ** (-2.0 * jnp.arange(half_size, dtype=f32) / size)
    angles = positions.astype(f32)[:, None] * inverse[None, :]
    cosine, sine = jnp.cos(angles), jnp.sin(angles)
    return jnp.concatenate([cosine, cosine], axis=1), jnp.concatenate([-sine, sine], axis=1)


def rotate(values, same, crossed):
    return values * same + pltpu.roll(values, values.shape[-1] // 2, 1) * crossed


def norm_back(stream, inverse_rms, gain, grad_normed):
    weighted = gain * grad_normed
    return inverse_rms * weighted - stream * inverse_rms**3 * jnp.mean(weighted * stream, axis=-1, keepdims=True)


def inverse_rms(block):
    return lax.rsqrt(jnp.mean(block * block, axis=-1, keepdims=True) + epsilon)


class Link:
    def __init__(self, axis):
        self.axis = axis
        self.last = ()

    def move(self, a, pairs):
        a = lax.optimization_barrier((a, *self.last))[0]
        a = lax.ppermute(a, self.axis, pairs)
        self.last = (a,)
        return a

    def swap(self, a):
        return self.move(a, [(0, 1), (1, 0)])

    def pair(self, a, bit):
        return self.move(a, [(i, i ^ bit) for i in range(GROUP)])


def reduce_quarter(part, y_link):
    h = part.shape[0] // 2
    q = h // 2
    kept = part[:h] + swap(part[h:], "c")
    return kept[:q] + y_link.swap(kept[q:])


def spread(own, y_link):
    other = y_link.swap(own)
    return [own, other, swap(own, "c"), swap(other, "c")]


def halve(a, axis, mine, exchange):
    n = a.shape[axis] // 2
    kept = lax.dynamic_slice_in_dim(a, mine * n, n, axis)
    return kept + exchange(lax.dynamic_slice_in_dim(a, (1 - mine) * n, n, axis))


def scatter_z(a, axis, n_outer, z_link):
    if n_outer > 1:
        return lax.psum_scatter(a, ("o", "z"), scatter_dimension=axis, tiled=True)
    z = lax.axis_index("z")
    a = halve(a, axis, z // 2, lambda v: z_link.pair(v, 2))
    return halve(a, axis, z % 2, lambda v: z_link.pair(v, 1))


def by_x(a, which, rows):
    n = a.shape[1] // (2 * rows)
    return jnp.concatenate([lax.dynamic_slice_in_dim(a, (2 * i + which) * rows, rows, 1) for i in range(n)], axis=1)


def call(kernel, name, ins, outs, flops=0, transcendentals=0):
    moved = sum(a.size * a.dtype.itemsize for a in (*ins, *outs))
    return pl.pallas_call(
        kernel,
        out_shape=outs,
        name=name,
        compiler_params=pltpu.CompilerParams(vmem_limit_bytes=56 * 2**20),
        cost_estimate=pl.CostEstimate(flops=flops, bytes_accessed=moved, transcendentals=transcendentals),
    )(*ins)


def probabilities(q, k, allowed, scale):
    scores = jnp.where(allowed, dot_nt(q, k) * scale, masked_value)
    exponent = jnp.exp(scores - jnp.max(scores, axis=-1, keepdims=True))
    return exponent / jnp.sum(exponent, axis=-1, keepdims=True)


def forward_kernel(
    scale, x_ref, gain_ref, wq_ref, wk_ref, wv_ref, wo_ref, same_ref, crossed_ref, pos_q_ref, pos_k_ref, length_ref,
    part_ref, normed_ref, q_ref, k_ref, v_ref, attended_ref,
):
    stream = x_ref[...].astype(f32)
    normed_ref[...] = (stream * inverse_rms(stream) * gain_ref[...]).astype(bf16)
    normed = normed_ref[...]
    same, crossed = same_ref[...], crossed_ref[...]
    k = rotate(dot(normed, wk_ref[...]), same, crossed).astype(bf16)
    v = dot(normed, wv_ref[...]).astype(bf16)
    k_ref[...], v_ref[...] = k, v
    raw = dot(normed, wq_ref[...])
    length = length_ref[0, 0]
    allowed = (pos_k_ref[...] <= pos_q_ref[...]) & (pos_k_ref[...] < length)
    valid = (pos_q_ref[...] < length).astype(f32)
    size = k.shape[1]
    for h in range(raw.shape[1] // size):
        at = slice(h * size, (h + 1) * size)
        q = rotate(raw[:, at], same, crossed).astype(bf16)
        q_ref[:, at] = q
        weights = probabilities(q, k, allowed, scale).astype(bf16)
        attended_ref[:, at] = (dot(weights, v) * valid).astype(bf16)
    part_ref[...] = dot(attended_ref[...], wo_ref[...])


def backward_kernel(
    scale, ga_ref, wo_ref, wq_ref, q_ref, k_ref, v_ref, same_ref, crossed_ref, pos_q_ref, pos_k_ref, length_ref,
    part_ref, kv_ref, gq_ref,
):
    k, v = k_ref[...], v_ref[...]
    same, crossed = same_ref[...], crossed_ref[...]
    length = length_ref[0, 0]
    allowed = (pos_k_ref[...] <= pos_q_ref[...]) & (pos_k_ref[...] < length)
    valid = (pos_q_ref[...] < length).astype(f32)
    grad_attended = (dot_nt(ga_ref[...], wo_ref[...]) * valid).astype(bf16)
    size = k.shape[1]
    grad_key = grad_value = 0.0
    for h in range(grad_attended.shape[1] // size):
        at = slice(h * size, (h + 1) * size)
        q, g = q_ref[:, at], grad_attended[:, at]
        probs = probabilities(q, k, allowed, scale)
        grad_probs = dot_nt(g, v)
        delta = jnp.sum(probs * grad_probs, axis=-1, keepdims=True)
        grad_scores = (probs * (grad_probs - delta)).astype(bf16)
        gq_ref[:, at] = rotate(dot(grad_scores, k) * scale, same, -crossed).astype(bf16)
        grad_key += dot_tn(grad_scores, q)
        grad_value += dot_tn(probs.astype(bf16), g)
    kv_ref[:, :size] = grad_key * scale
    kv_ref[:, size:] = grad_value
    part_ref[...] = dot_nt(gq_ref[...], wq_ref[...])


def rows_call(kernel, name, quarters, stacked, shared, outs, totals, tile=16, prefetch=()):
    count, width = quarters[0][0].shape
    args = [a for group in quarters for a in group] + list(stacked) + list(shared)
    specs = [pl.BlockSpec((tile, width), lambda t, *p: (t, 0))] * (4 * len(quarters))
    specs += [pl.BlockSpec((4, tile, a.shape[2]), lambda t, *p: (0, t, 0)) for a in stacked]
    specs += [pl.BlockSpec(a.shape, lambda t, *p: (0, 0)) for a in shared]
    out_specs = [pl.BlockSpec((4, tile, w), lambda t, *p: (0, t, 0)) for w, _ in outs]
    out_specs += [pl.BlockSpec((1, width), lambda t, *p: (0, 0))] * totals
    out_shape = [jax.ShapeDtypeStruct((4, count, w), kind) for w, kind in outs]
    out_shape += [jax.ShapeDtypeStruct((1, width), f32)] * totals
    moved = sum(a.size * a.dtype.itemsize for a in (*args, *out_shape))
    return pl.pallas_call(
        kernel,
        grid_spec=pltpu.PrefetchScalarGridSpec(
            num_scalar_prefetch=len(prefetch), grid=(count // tile,), in_specs=specs, out_specs=out_specs
        ),
        out_shape=out_shape,
        name=name,
        compiler_params=pltpu.CompilerParams(vmem_limit_bytes=32 * 2**20),
        cost_estimate=pl.CostEstimate(flops=20 * count * width, bytes_accessed=moved, transcendentals=0),
    )(*prefetch, *args)


def mid_kernel(*refs):
    hidden, (gain, out) = refs[:4], refs[4:]
    for j in range(4):
        h = hidden[j][...]
        out[j] = (h * inverse_rms(h) * gain[...]).astype(bf16)


def mid_back_kernel(*refs):
    grads, hidden, (grad_out, gain, grad_hidden, rounded, total) = refs[:4], refs[4:8], refs[8:]
    gain = gain[...]
    acc = 0.0
    for j in range(4):
        h, g = hidden[j][...], grads[j][...]
        r = inverse_rms(h)
        acc += jnp.sum(g * h * r, axis=0, keepdims=True)
        back = grad_out[j].astype(f32) + norm_back(h, r, gain, g)
        grad_hidden[j] = back
        rounded[j] = back.astype(bf16)

    @pl.when(pl.program_id(0) == 0)
    def _():
        total[...] = jnp.zeros_like(total)

    total[...] += acc


def in_back_kernel(*refs):
    sums, (keyed, inputs, grad_hidden, gain, out, total) = refs[:4], refs[4:]
    gain = gain[...]
    acc = 0.0
    for j in range(4):
        stream = inputs[j].astype(f32)
        g = sums[j][...] + keyed[j]
        r = inverse_rms(stream)
        acc += jnp.sum(g * stream * r, axis=0, keepdims=True)
        out[j] = (grad_hidden[j] + norm_back(stream, r, gain, g)).astype(bf16)

    @pl.when(pl.program_id(0) == 0)
    def _():
        total[...] = jnp.zeros_like(total)

    total[...] += acc


def add_kernel(*refs):
    left, right, (out,) = refs[:4], refs[4:8], refs[8:]
    for j in range(4):
        out[j] = (left[j][...] + right[j][...]).astype(bf16)


def pack_kernel(n, places, *refs):
    blocks, scale, out, picked = refs[:n], refs[n], refs[n + 1], refs[n + 2]
    width = picked.shape[2] // 2
    for j in range(n):
        out[j] = (blocks[j][...] * scale[...]).astype(bf16)
        for part in range(2):
            at = pl.ds(pl.multiple_of(places[part] * width, width), width)
            picked[j, :, part * width : (part + 1) * width] = (blocks[j][:, at] * scale[:, at]).astype(bf16)


def pack(blocks, scale, places, rows, tile=32):
    n = len(blocks)
    count, width = blocks[0].shape
    block = pl.BlockSpec((tile, width), lambda t, places: (t, 0))
    out, picked = pl.pallas_call(
        functools.partial(pack_kernel, n),
        grid_spec=pltpu.PrefetchScalarGridSpec(
            num_scalar_prefetch=1,
            grid=(count // tile,),
            in_specs=[block] * n + [pl.BlockSpec((1, width), lambda t, places: (0, 0))],
            out_specs=[
                pl.BlockSpec((n, tile, width), lambda t, places: (0, t, 0)),
                pl.BlockSpec((n, tile, 2 * rows), lambda t, places: (0, t, 0)),
            ],
        ),
        out_shape=[
            jax.ShapeDtypeStruct((n, count, width), bf16),
            jax.ShapeDtypeStruct((n, count, 2 * rows), bf16),
        ],
        compiler_params=pltpu.CompilerParams(vmem_limit_bytes=32 * 2**20),
        cost_estimate=pl.CostEstimate(flops=n * count * width, bytes_accessed=6 * n * count * width, transcendentals=0),
    )(places, *blocks, scale.reshape(1, width))
    return out.reshape(n * count, width), picked.reshape(n * count, 2 * rows)


def after(value, *others):
    return lax.optimization_barrier((value, *others))[0]


def ffn_kernel(own, has_prev, *refs):
    nm_ref, go_ref, nmc_ref, goc_ref, wg_ref, wu_ref, wd_ref = refs[:7]
    previous = refs[7:13] if has_prev else None
    outs = refs[13:] if has_prev else refs[7:]
    gate = dot(nm_ref[...], wg_ref[...])
    up = dot(nm_ref[...], wu_ref[...])
    grad_mixed = dot_nt(go_ref[...], wd_ref[...]).astype(bf16).astype(f32)
    sig = jax.nn.sigmoid(gate)
    gate_sig = gate * sig
    mixed = (gate_sig * up).astype(bf16)
    grad_gate = (grad_mixed * up * sig * (1.0 + gate * (1.0 - sig))).astype(bf16)
    grad_up = (grad_mixed * gate_sig).astype(bf16)
    n = nmc_ref.shape[1] // 2
    by_gate = dot_tn(nmc_ref[...], grad_gate)
    by_up = dot_tn(nmc_ref[...], grad_up)
    by_down = dot_tn(mixed, goc_ref[...])
    sums = (by_gate[:n], by_gate[n:], by_up[:n], by_up[n:], by_down[:, :n], by_down[:, n:])
    for i in range(6):
        outs[i][...] = sums[i] + previous[i][...] if has_prev else sums[i]
    if own:
        outs[6][...] = mixed
        outs[7][...] = grad_gate
        outs[8][...] = grad_up


def ffn(nm, go, nm_columns, go_columns, w_gate, w_up, w_down, previous=(), own=False, tile=512):
    count, width = nm.shape
    hidden = w_gate.shape[1]
    n = nm_columns.shape[1] // 2

    def whole(shape):
        return pl.BlockSpec(shape, lambda t: (0, 0), pipeline_mode=pl.Buffered(1))

    across = pl.BlockSpec((n, tile), lambda t: (0, t))
    down = pl.BlockSpec((tile, n), lambda t: (t, 0))
    sums = [across] * 4 + [down] * 2
    out_specs = list(sums)
    out_shape = [jax.ShapeDtypeStruct((n, hidden), f32)] * 4 + [jax.ShapeDtypeStruct((hidden, n), f32)] * 2
    if own:
        out_specs += [pl.BlockSpec((count, tile), lambda t: (0, t))] * 3
        out_shape += [jax.ShapeDtypeStruct((count, hidden), bf16)] * 3
    columns = pl.BlockSpec((width, tile), lambda t: (0, t))
    in_specs = [whole(nm.shape), whole(go.shape), whole(nm_columns.shape), whole(go_columns.shape)]
    in_specs += [columns, columns, pl.BlockSpec((tile, width), lambda t: (t, 0))]
    in_specs += sums if previous else []
    return pl.pallas_call(
        functools.partial(ffn_kernel, own, bool(previous)),
        grid=(pl.cdiv(hidden, tile),),
        in_specs=in_specs,
        out_specs=out_specs,
        out_shape=out_shape,
        compiler_params=pltpu.CompilerParams(vmem_limit_bytes=56 * 2**20),
        cost_estimate=pl.CostEstimate(
            flops=2 * count * hidden * (3 * width + 6 * n),
            bytes_accessed=6 * width * hidden + 4 * count * width + (48 if previous else 24) * n * hidden,
            transcendentals=count * hidden,
        ),
    )(nm, go, nm_columns, go_columns, w_gate, w_up, w_down, *previous)


def shards(
    sizes,
    inputs,
    seq_lengths,
    norm_in,
    w_query,
    w_key,
    w_value,
    w_out,
    norm_mid,
    w_gate,
    w_up,
    w_down,
    out_cotangent,
    kv_cotangent,
):
    n_outer, n_dp = sizes
    seq_len, width = inputs.shape
    quarter = seq_len // 4
    head = w_key.shape[1]
    own_heads = w_query.shape[1]
    scale = head ** (-0.5)
    rows = width // n_dp
    z, x = lax.axis_index("z"), lax.axis_index("x")
    y_link, x_link, z_link = Link("y"), Link("x"), Link("z")
    length = seq_lengths[0]
    one = jnp.minimum(length, 1).astype(f32)
    positions = relative(jnp.arange(seq_len))
    valid = (positions < length)[:, None]
    grad_down_in = jnp.where(valid, relative(out_cotangent), 0)
    go_quarter, inputs = lax.optimization_barrier((grad_down_in[:quarter].astype(f32), inputs))

    go_z = lax.all_gather(go_quarter, "z", axis=0, tiled=False)
    inputs = relative(inputs)
    stream_own = inputs[:quarter].astype(f32)
    gain_in, gain_mid = norm_in.reshape(1, width), norm_mid.reshape(1, width)
    same, crossed = rotary_tables(positions, head)
    masks = (same, crossed, positions[:, None], positions[None, :], seq_lengths.reshape(1, 1))

    def shape(n, kind):
        return jax.ShapeDtypeStruct((seq_len, n), kind)

    part, normed, queries, key_rot, value_rows, attended = call(
        functools.partial(forward_kernel, scale),
        "attention_forward",
        (inputs, gain_in, w_query, w_key, w_value, w_out, *masks),
        [shape(width, f32), shape(width, bf16), shape(own_heads, bf16), shape(head, bf16), shape(head, bf16),
         shape(own_heads, bf16)],
        flops=2 * seq_len * (width * (2 * own_heads + 2 * head) + 2 * seq_len * own_heads),
        transcendentals=seq_len * seq_len * own_heads // head,
    )
    hidden_own = stream_own + reduce_quarter(part, y_link)

    def scaled(block):
        return block * inverse_rms(block)

    def remote(gathered):
        return [lax.dynamic_index_in_dim(gathered, lax.rem(z + k, GROUP), 0, keepdims=False) for k in range(1, GROUP)]

    nm_z_own = lax.all_gather(scaled(hidden_own), "z", axis=0, tiled=False)
    hidden = spread(hidden_own, y_link)
    hidden[1], go_z = lax.optimization_barrier((hidden[1], go_z))
    nm_z_other = lax.all_gather(scaled(hidden[1]), "z", axis=0, tiled=False)
    go_remote = remote(go_z)
    go_other = [y_link.swap(block) for block in go_remote[:2]]

    def columns(part):
        part = part.reshape(part.shape[0], n_outer, GROUP, 2, rows) if n_outer > 1 else part
        taken = []
        for which in (1 - x, x):
            if n_outer > 1:
                cut = lax.dynamic_index_in_dim(part, z, 2, keepdims=False)
                cut = lax.dynamic_index_in_dim(cut, which, 2, keepdims=False)
                taken.append(cut.reshape(part.shape[0], n_outer * rows))
            else:
                taken.append(lax.dynamic_slice_in_dim(part, (2 * z + which) * rows, rows, 1))
        return jnp.concatenate(taken, axis=1)

    (normed_mid,) = rows_call(mid_kernel, "mid_norm", [hidden], [], [gain_mid], [(width, bf16)], 0)
    normed_mid = normed_mid.reshape(seq_len, width)
    weights = (w_gate, w_up, w_down)
    *sums, mixed, grad_gate, grad_up = ffn(
        normed_mid, grad_down_in, columns(normed_mid), columns(grad_down_in), *weights, own=True
    )
    mid_part = dot_nt(grad_gate, w_gate) + dot_nt(grad_up, w_up)
    mid_part, nm_z_own, *go_other = lax.optimization_barrier((mid_part, nm_z_own, *go_other))
    grad_mid = spread(reduce_quarter(mid_part, y_link), y_link)
    grad_hidden, grad_attention, grad_norm_mid = rows_call(
        mid_back_kernel, "mid_back", [grad_mid, hidden], [grad_down_in.reshape(4, quarter, width)], [gain_mid],
        [(width, f32), (width, bf16)], 1,
    )
    grad_attention = grad_attention.reshape(seq_len, width)

    go_other.append(y_link.swap(go_remote[2]))
    input_part, grad_kv, grad_query = call(
        functools.partial(backward_kernel, scale),
        "attention_backward",
        (grad_attention, w_out, w_query, queries, key_rot, value_rows, *masks),
        [shape(width, f32), shape(2 * head, f32), shape(own_heads, bf16)],
        flops=2 * seq_len * (2 * width * own_heads + 5 * seq_len * own_heads),
        transcendentals=seq_len * seq_len * own_heads // head,
    )
    input_part, go_other[2] = lax.optimization_barrier((input_part, go_other[2]))
    out_sent = x_link.swap(dot_tn(attended, by_x(grad_attention, 1 - x, rows)))
    out_kept = dot_tn(attended, by_x(grad_attention, x, rows))
    query_sent = x_link.swap(dot_tn(by_x(normed, 1 - x, rows), grad_query))
    query_kept = dot_tn(by_x(normed, x, rows), grad_query)
    grad_kv = jnp.concatenate(spread(reduce_quarter(grad_kv, y_link), y_link), axis=0)
    summed_own = reduce_quarter(input_part, y_link)
    summed_own, nm_z_other, out_sent = lax.optimization_barrier((summed_own, nm_z_other, out_sent))
    summed = spread(summed_own, y_link)
    grad_kv = grad_kv + jnp.where(valid, relative(kv_cotangent).astype(f32), 0.0)
    grad_key = grad_kv[:, :head]
    crossed_key = jnp.concatenate([grad_key[:, head // 2 :], grad_key[:, : head // 2]], axis=1)
    grad_key = (grad_key * same - crossed_key * crossed).astype(bf16)
    grad_value = grad_kv[:, head:].astype(bf16)
    grad_w_key = dot_tn(normed, grad_key)
    grad_w_value = dot_tn(normed, grad_value)
    keyed = dot_nt(grad_key, w_key) + dot_nt(grad_value, w_value)
    grad_inputs, grad_norm_in = rows_call(
        in_back_kernel, "in_back", [summed],
        [keyed.reshape(4, quarter, width), inputs.reshape(4, quarter, width), grad_hidden], [gain_in], [(width, bf16)], 1,
    )

    places = jnp.stack([2 * z + 1 - x, 2 * z + x]).astype(jnp.int32)
    nm_z_own = after(nm_z_own, grad_query)
    for nm, go in ((remote(nm_z_own), go_remote), (remote(nm_z_other), go_other)):
        nm = nm + [swap(block, "c") for block in nm]
        go = go + [swap(block, "c") for block in go]
        if n_outer == 1:
            nm, nm_columns = pack(nm, norm_mid, places, rows)
            go, go_columns = pack(go, jnp.ones_like(norm_mid), places, rows)
        else:
            nm = (jnp.concatenate(nm, axis=0) * norm_mid).astype(bf16)
            go = (jnp.concatenate(go, axis=0) * one).astype(bf16)
            nm_columns, go_columns = columns(nm), columns(go)
        sums = ffn(nm, go, nm_columns, go_columns, *weights, previous=sums)
    sums, query_sent = lax.optimization_barrier((sums, query_sent))
    grad_w_out = scatter_z(out_kept + out_sent, 1, n_outer, z_link)
    grad_w_query = scatter_z(query_kept + query_sent, 0, n_outer, z_link)
    grad_w_gate = sums[1] + x_link.swap(sums[0])
    grad_w_up = sums[3] + x_link.swap(sums[2])

    piece = rows // 4
    m = 2 * lax.axis_index("y") + lax.axis_index("c")
    kv = jnp.concatenate([grad_w_key, grad_w_value], axis=1).reshape(n_dp, 4, piece, 2 * head)
    kv = lax.dynamic_index_in_dim(kv, m, 1, keepdims=False)
    gains = jnp.concatenate([grad_norm_in, grad_norm_mid]).reshape(2, n_dp, rows).transpose(1, 0, 2)
    gains = jnp.pad(gains, ((0, 0), (0, 6), (0, 2 * head - rows)))
    small = jnp.concatenate([kv, gains], axis=1).reshape(n_dp // 2, 2, -1, 2 * head)
    small = halve(small, 1, x, x_link.swap)
    small = scatter_z(small.reshape(n_dp // 2, -1, 2 * head), 0, n_outer, z_link)[0]
    kv = lax.all_gather(small[:piece], ("y", "c"), axis=0, tiled=True)
    out_norm_in, out_norm_mid = small[piece, :rows], small[piece + 1, :rows]
    grad_w_down = sums[5] + x_link.swap(sums[4])

    down = spread(reduce_quarter(dot(after(mixed, summed[1]), w_down), y_link), y_link)
    (result,) = rows_call(add_kernel, "result", [down, hidden], [], [], [(width, bf16)], 0)
    if n_outer > 1:
        grad_w_down = lax.psum_scatter(grad_w_down, "o", scatter_dimension=1, tiled=True)
        grad_w_gate = lax.psum_scatter(grad_w_gate, "o", scatter_dimension=0, tiled=True)
        grad_w_up = lax.psum_scatter(grad_w_up, "o", scatter_dimension=0, tiled=True)

    return (
        relative(result.reshape(seq_len, width)),
        relative(grad_inputs.reshape(seq_len, width)),
        out_norm_in,
        grad_w_query,
        kv[:, :head],
        kv[:, head:],
        grad_w_out,
        out_norm_mid,
        grad_w_gate,
        grad_w_up,
        grad_w_down,
    )


def solution(mesh):
    n_dp = mesh.shape["dp"]
    n_outer = n_dp // (2 * GROUP)
    split = Mesh(mesh.devices.reshape(n_outer, GROUP, 2, 2, 2), ("o", "z", "x", "y", "c"))
    dp, mp = ("o", "z", "x"), ("y", "c")

    def program(*args):
        return shards((n_outer, n_dp), *args)

    return jax.shard_map(
        program,
        mesh=split,
        in_specs=(
            P(dp, None),
            P(dp),
            P(),
            P(None, mp),
            P(),
            P(),
            P(mp, None),
            P(),
            P(None, mp),
            P(None, mp),
            P(mp, None),
            P(dp, None),
            P(dp, None),
        ),
        out_specs=(
            P(dp, None),
            P(dp, None),
            P(dp),
            P(dp, mp),
            P(dp, None),
            P(dp, None),
            P(mp, dp),
            P(dp),
            P(dp, mp),
            P(dp, mp),
            P(mp, dp),
        ),
        check_vma=False,
    )
```

time: 740 us -> 554 us (0.75)
  Pallas kernels: 0 us -> 131 us
  matrix products: 141 us -> 29.8 us
  waiting for transfers between devices: 332 us -> 239 us
  local copies, waits for them, and re-layouts: 110 us -> 46.6 us
  other arithmetic: 99.8 us -> 43.1 us
  starting transfers between devices: 23 us -> 34.2 us
    ppermute x26 -> x27, waiting for transfers between devices: 332 us -> 8 us  [swap(): return lax.ppermute(a, axis, [(0, 1), (1, 0)])]
    ppermute x0 -> x25, waiting for transfers between devices: none -> 201 us  [move(): a = lax.ppermute(a, self.axis, pairs)]
    pallas_call x0 -> x13, Pallas kernels: none -> 131 us  [the longest x3 76 us: ffn(): pl.pallas_call(functools.partial(ffn_kernel, own, bool(previous)), grid=(...]
    dot_general x11 -> x1, matrix products: 65.2 us -> 3.5 us  [dot(): return jnp.dot(a, b, preferred_element_type=f32)]
    convert_element_type x13 -> x2, other arithmetic: 45.1 us -> 2.1 us  [the longest x1 1.16 us: shards(): grad_down_in[:quarter].astype(f32)]
    dot_general x9 -> x4, matrix products: 47.8 us -> 15.2 us  [dot_nt(): lax.dot_general(a, b, (((1,), (1,)), ((), ())), preferred_element_type=f32)]
    all_gather x2 -> x3, waiting for transfers between devices: 0.01 us -> 29.5 us  [the longest x1 25.1 us: shards(): nm_z_own = lax.all_gather(scaled(hidden_own), 'z', axis=0, tiled=False)]
    ppermute x0 -> x25, starting transfers between devices: none -> 29.2 us  [move(): a = lax.ppermute(a, self.axis, pairs)]
  transfers between devices with their start and end apart: 31 -> 55, of which waited for: 15 -> 23; matrix products, arithmetic and copies ran while one was open for 39% -> 16% of each run, Pallas kernels for 0% -> 23%
where the time goes in v2:
time: 554 us; the launch traced here: 545 us
  waiting for transfers between devices  239 us (43%)
  Pallas kernels  131 us (24%)
  local copies, waits for them, and re-layouts  46.6 us (8%)
  other arithmetic  43.1 us (8%)
  starting transfers between devices  34.2 us (6%)
  matrix products  29.8 us (5%)
  between operations  16.1 us (3%)
  blocking collectives  5.79 us (1%)
    ppermute x25, waiting for transfers between devices, move(): a = lax.ppermute(a, self.axis, pairs)  201 us
    pallas_call x3, Pallas kernels, ffn(): pl.pallas_call(functools.partial(ffn_kernel, own, bool(previous)), grid=(...  76 us
    ppermute x25, starting transfers between devices, move(): a = lax.ppermute(a, self.axis, pairs)  29.2 us
    all_gather x1, waiting for transfers between devices, shards(): nm_z_own = lax.all_gather(scaled(hidden_own), 'z', axis=0, tiled=False)  25.1 us
    pallas_call x2, Pallas kernels, call(): pl.pallas_call(kernel, out_shape=outs, name=name, compiler_params=pltpu.C...  23.5 us
    pallas_call x4, Pallas kernels, rows_call(): pl.pallas_call(kernel, grid_spec=pltpu.PrefetchScalarGridSpec(num_scalar_...  20.3 us
    unnamed x152, local copies, waits for them, and re-layouts  17.1 us
    dot_general x4, matrix products, dot_nt(): lax.dot_general(a, b, (((1,), (1,)), ((), ())), preferred_element_type=f32)  15.2 us
  transfers between devices with their start and end apart: 55, of which 23 were waited for; matrix products, arithmetic and copies ran while one was open for 16% of the time, Pallas kernels for 23%

profile of v2, /device:TPU:0, one launch (start us, length us, event | category | flops | bytes accessed | tf_op | source)
XLA Modules:
  0.0 545.3 jit_solution(9666486608310338817)
XLA Ops:
  21.2 11.6 %attention_forward.1 = (f32[512,2048]{1,0:T(8,128)}, bf16[512,2048]{1,0:T(8,128)(2,1)}, bf16[512,512]{1,0:T(8,128)(2,1)}, bf16[512,128]{1,0:T(8,128)(2,1)}, bf16...) custom-call(bf16[512,2048]{1,0:T(8,128)(2,1)} %pad_maximum_fusion.1.x_ref, f32[1,2048]{1,0:T(1,128)} %bitcast.102, ...), custom_call_target="tpu_custom_call" | custom-call | flops 3221225472 | bytes 15478788 | tf_op jit(solution)/shard_map/attention_forward/pallas_call | solution.py:113
  42.7 23.5 %collective-permute-done.1 = f32[128,2048]{1,0:T(8,128)S(1)} collective-permute-done((f32[128,2048]{1,0:T(8,128)S(1)}, f32[128,2048]{1,0:T(8,128)S(1)}, u32[]{:S(2)}, u32[]{:S(2)}) %collective-permute-start.1) | collective-permute-done | bytes 1048608 | tf_op jit(solution)/shard_map/ppermute | solution.py:69
  70.0 23.1 %collective-permute-done.2.refs_1_.refs_5_ = f32[128,2048]{1,0:T(8,128)S(1)} collective-permute-done((f32[128,2048]{1,0:T(8,128)S(1)}, f32[128,2048]{1,0:T(8,128)S(1)}, u32[]{:S(2)}, u32[]{:S(2)}) %collective-permute-start.2) | collective-permute-done | bytes 1048608 | tf_op jit(solution)/shard_map/ppermute | solution.py:69
  104.1 4.6 mid_norm.1
  110.2 20.1 %shard_map.212 = (f32[256,1408]{1,0:T(8,128)}, f32[256,1408]{1,0:T(8,128)}, f32[256,1408]{1,0:T(8,128)}, f32[256,1408]{1,0:T(8,128)}, f32[1408,256]{1,0:T(8,128)...) custom-call(bf16[512,2048]{1,0:T(8,128)(2,1)} %bitcast.94, ...), custom_call_target="tpu_custom_call" | custom-call | flops 11072962560 | bytes 30146560 | tf_op jit(solution)/shard_map/pallas_call | solution.py:337
  131.2 6.0 %fusion.52 = f32[512,2048]{1,0:T(8,128)S(1)} fusion(bf16[512,1408]{1,0:T(8,128)(2,1)} %get-tuple-element.105, bf16[2048,1408]{1,0:T(8,128)(2,1)} %refs_5_.5), kind=kOutput, calls=%fused_computation.158 | convolution fusion | flops 2952790016 | bytes 11403264 | tf_op jit(solution)/shard_map/dot_general | solution.py:22
  137.3 7.7 %convolution_add_fusion.1 = f32[512,2048]{1,0:T(8,128)} fusion(f32[512,2048]{1,0:T(8,128)S(1)} %fusion.52, bf16[512,1408]{1,0:T(8,128)(2,1)S(1)} %copy-done.71, bf16[2048,1408]{1,0:T(8,128)(2,1)} %refs_4_.5), kind=kOutput, calls=%fused_computation.1 | convolution fusion | flops 2953838592 | bytes 15597568 | tf_op jit(solution)/shard_map/dot_general | solution.py:22
  145.0 10.2 %collective-permute-done.6.refs_1_ = f32[128,2048]{1,0:T(8,128)} collective-permute-done((f32[128,2048]{1,0:T(8,128)S(1)}, f32[128,2048]{1,0:T(8,128)}, u32[]{:S(2)}, u32[]{:S(2)}) %collective-permute-start.6) | collective-permute-done | bytes 1048608 | tf_op jit(solution)/shard_map/ppermute | solution.py:69
  155.2 25.1 %all-gather.10.cloned.1.call-done = f32[512,2048]{1,0:T(8,128)} async-done(((f32[128,2048]{1,0:T(8,128)}), f32[512,2048]{1,0:T(8,128)}) %all-gather.10.cloned.1.call-update) | async-done | bytes 4194320 | tf_op jit(solution)/shard_map/all_gather | solution.py:411
  188.5 23.5 %collective-permute-done.8 = f32[128,2048]{1,0:T(8,128)S(1)} collective-permute-done((f32[128,2048]{1,0:T(8,128)S(1)}, f32[128,2048]{1,0:T(8,128)S(1)}, u32[]{:S(2)}, u32[]{:S(2)}) %collective-permute-start.8) | collective-permute-done | bytes 1048608 | tf_op jit(solution)/shard_map/ppermute | solution.py:69
  215.8 22.0 %collective-permute-done.9.refs_1_ = f32[128,2048]{1,0:T(8,128)} collective-permute-done((f32[128,2048]{1,0:T(8,128)}, f32[128,2048]{1,0:T(8,128)}, u32[]{:S(2)}, u32[]{:S(2)}) %collective-permute-start.9) | collective-permute-done | bytes 1048608 | tf_op jit(solution)/shard_map/ppermute | solution.py:69
  242.3 6.8 %mid_back.1 = (f32[4,128,2048]{2,1,0:T(8,128)S(1)}, bf16[4,128,2048]{2,1,0:T(8,128)(2,1)S(1)}, f32[1,2048]{1,0:T(1,128)S(1)}) custom-call(f32[128,2048]{1,0:T(8,128)} %slice_add_fusion.6.refs_0_, f32[128,2048]{1,0:T(8,128)} %collective-permute-done.9.refs_1_, f32[128,2048]{1,0:T(8,128)} %collective-permute-done.10.refs_2_, ...), custom_call_target="tpu_custom_call" | custom-call | flops 5242880 | bytes 16793600 | tf_op jit(solution)/shard_map/mid_back/pallas_call | solution.py:191
  252.5 11.9 %attention_backward.1 = (f32[512,2048]{1,0:T(8,128)}, f32[512,256]{1,0:T(8,128)}, bf16[512,512]{1,0:T(8,128)(2,1)}) custom-call(bf16[512,2048]{1,0:T(8,128)(2,1)} %bitcast.96, bf16[512,2048]{1,0:T(8,128)(2,1)} %wo_ref.3, bf16[2048,512]{1,0:T(8,128)(2,1)} %wq_ref.3, bf16[512,512]{1,0:T(8,128)(2,1)} %get-tuple-element.113.q_ref, ...), custom_call_target="tpu_custom_call" | custom-call | flops 3489660928 | bytes 12849156 | tf_op jit(solution)/shard_map/attention_backward/pallas_call | solution.py:113
  305.3 14.3 %collective-permute-done.17 = f32[128,2048]{1,0:T(8,128)S(1)} collective-permute-done((f32[128,2048]{1,0:T(8,128)S(1)}, f32[128,2048]{1,0:T(8,128)S(1)}, u32[]{:S(2)}, u32[]{:S(2)}) %collective-permute-start.17) | collective-permute-done | bytes 1048608 | tf_op jit(solution)/shard_map/ppermute | solution.py:69
  320.8 6.7 %collective-permute-done.18 = f32[512,1024]{1,0:T(8,128)} collective-permute-done((f32[512,1024]{1,0:T(8,128)}, f32[512,1024]{1,0:T(8,128)}, u32[]{:S(2)}, u32[]{:S(2)}) %collective-permute-start.18) | collective-permute-done | bytes 2097184 | tf_op jit(solution)/shard_map/ppermute | solution.py:69
  328.5 27.9 %shard_map.217 = (f32[256,1408]{1,0:T(8,128)}, f32[256,1408]{1,0:T(8,128)}, f32[256,1408]{1,0:T(8,128)}, f32[256,1408]{1,0:T(8,128)}, f32[1408,256]{1,0:T(8,128)}, /*index=5*/f32[1408,256]{1,0:T(8,128)}) custom-call(bf16[768,2048]{1,0:T(8,128)(2,1)} %bitcast.106, bf16[768,2048]{1,0:T(8,128)(2,1)} %bitcast.104, bf16[768,512]{1,0:T(8,128)(2,1)} %bitcast.110, ...), custom_call_target="tpu_custom_call" | custom-call | flops 16609443840 | bytes 40894464 | tf_op jit(solution)/shard_map/pallas_call | solution.py:337
  379.0 28.0 %shard_map.218 = (f32[256,1408]{1,0:T(8,128)}, f32[256,1408]{1,0:T(8,128)}, f32[256,1408]{1,0:T(8,128)}, f32[256,1408]{1,0:T(8,128)}, f32[1408,256]{1,0:T(8,128)}, /*index=5*/f32[1408,256]{1,0:T(8,128)}) custom-call(bf16[768,2048]{1,0:T(8,128)(2,1)} %bitcast.107, bf16[768,2048]{1,0:T(8,128)(2,1)} %bitcast.105, bf16[768,512]{1,0:T(8,128)(2,1)} %bitcast.111, ...), custom_call_target="tpu_custom_call" | custom-call | flops 16609443840 | bytes 40894464 | tf_op jit(solution)/shard_map/pallas_call | solution.py:337
  422.2 8.5 %collective-permute-done.46 = f32[512,256]{1,0:T(8,128)S(1)} collective-permute-done((f32[512,256]{1,0:T(8,128)S(1)}, f32[512,256]{1,0:T(8,128)S(1)}, u32[]{:S(2)}, u32[]{:S(2)}) %collective-permute-start.46) | collective-permute-done | bytes 524320 | tf_op jit(solution)/shard_map/ppermute | solution.py:69
  432.4 10.3 %collective-permute-done.42 = f32[256,1408]{1,0:T(8,128)} collective-permute-done((f32[256,1408]{1,0:T(8,128)}, f32[256,1408]{1,0:T(8,128)}, u32[]{:S(2)}, u32[]{:S(2)}) %collective-permute-start.42) | collective-permute-done | bytes 1441824 | tf_op jit(solution)/shard_map/ppermute | solution.py:69
  453.8 23.6 %collective-permute-done.47 = f32[512,512]{1,0:T(8,128)S(1)} collective-permute-done((f32[512,512]{1,0:T(8,128)S(1)}, f32[512,512]{1,0:T(8,128)S(1)}, u32[]{:S(2)}, u32[]{:S(2)}) %collective-permute-start.47) | collective-permute-done | bytes 1048608 | tf_op jit(solution)/shard_map/ppermute | solution.py:69
  487.9 8.4 %collective-permute-done.48 = f32[256,512]{1,0:T(8,128)} collective-permute-done((f32[256,512]{1,0:T(8,128)}, f32[256,512]{1,0:T(8,128)}, u32[]{:S(2)}, u32[]{:S(2)}) %collective-permute-start.48) | collective-permute-done | bytes 524320 | tf_op jit(solution)/shard_map/ppermute | solution.py:69
  510.3 5.8 %all-gather.3 = f32[1,256,256]{2,1,0:T(8,128)S(1)} all-gather(f32[1,64,256]{2,1,0:T(8,128)S(1)} %slice.147), channel_id=5, replica_groups=mesh['o'=1,'z'=4,'x'=2,'y'=2,'c'=2] {'y','c'}, dimensions={1}, use_global_device_ids=true | all-gather | bytes 327680 | tf_op jit(solution)/shard_map/all_gather | solution.py:504
  517.4 11.0 %collective-permute-done.51 = f32[1408,256]{1,0:T(8,128)S(1)} collective-permute-done((f32[1408,256]{1,0:T(8,128)}, f32[1408,256]{1,0:T(8,128)S(1)}, u32[]{:S(2)}, u32[]{:S(2)}) %collective-permute-start.51) | collective-permute-done | bytes 1441824 | tf_op jit(solution)/shard_map/ppermute | solution.py:69
  529.7 4.8 result.1
  (362 shorter events, 183.6 us)
Async XLA Ops:
  7.2 92.2 %all-gather.8.cloned.1.call-start = ((), (), s32[]{:S(2)}) async-start(), calls=%async_computation | async-start | bytes 5242880 | tf_op jit(solution)/shard_map/all_gather | solution.py:384
  15.7 164.5 %all-gather.10.cloned.1.call-start = ((), (), s32[]{:S(2)}) async-start(), calls=%async_computation.1 | async-start | bytes 5242880 | tf_op jit(solution)/shard_map/all_gather | solution.py:411
  39.5 26.6 %collective-permute-start.1 = (f32[128,2048]{1,0:T(8,128)S(1)}, f32[128,2048]{1,0:T(8,128)S(1)}, u32[]{:S(2)}, u32[]{:S(2)}) collective-permute-start(f32[128,2048]{1,0:T(8,128)S(1)} %slice.131), channel_id=1, source_target_pairs={{0,2},{2,0},{1,3},{3,1},{4,6},{6,4},{5,7},{7,5},{8,10},{10,8},{9,1... | collective-permute-start | bytes 3145736 | tf_op jit(solution)/shard_map/ppermute | solution.py:69
  67.6 253.2 %all-gather.12.cloned.1.call-start = ((), (), s32[]{:S(2)}) async-start(), calls=%async_computation.2 | async-start | bytes 5242880 | tf_op jit(solution)/shard_map/all_gather | solution.py:414
  70.0 34.1 %collective-permute-start.3 = (f32[128,2048]{1,0:T(8,128)S(1)}, f32[128,2048]{1,0:T(8,128)S(1)}, u32[]{:S(2)}, u32[]{:S(2)}) collective-permute-start(f32[128,2048]{1,0:T(8,128)S(1)} %get-tuple-element.100.refs_0_.refs_4_), channel_id=1, source_target_pairs={{0,1},{1,0},{2,3},{3,2},{4,5},{5,4},{6,7},{7,6},{8,9},{9,8},{10,11... | collective-permute-start | bytes 3145736 | tf_op jit(solution)/shard_map/ppermute | solution.py:30
  102.6 27.8 %collective-permute-start.5 = (f32[128,2048]{1,0:T(8,128)S(1)}, f32[128,2048]{1,0:T(8,128)}, u32[]{:S(2)}, u32[]{:S(2)}) collective-permute-start(f32[128,2048]{1,0:T(8,128)S(1)} %get-tuple-element.107.refs_0_), channel_id=1, source_target_pairs={{0,2},{2,0},{1,3},{3,1},{4,6},{6,4},{5,7},{7,5},{8,10},{10,8},{9,1... | collective-permute-start | bytes 3145736 | tf_op jit(solution)/shard_map/ppermute | solution.py:69
  239.7 31.1 %collective-permute-start.38 = (f32[128,2048]{1,0:T(8,128)}, f32[128,2048]{1,0:T(8,128)}, u32[]{:S(2)}, u32[]{:S(2)}) collective-permute-start(f32[128,2048]{1,0:T(8,128)} %copy-done.7), channel_id=1, source_target_pairs={{0,1},{1,0},{2,3},{3,2},{4,5},{5,4},{6,7},{7,6},{8,9},{9,8},{10,11... | collective-permute-start | bytes 3145736 | tf_op jit(solution)/shard_map/ppermute | solution.py:30
  240.0 30.8 %collective-permute-start.39 = (f32[128,2048]{1,0:T(8,128)}, f32[128,2048]{1,0:T(8,128)}, u32[]{:S(2)}, u32[]{:S(2)}) collective-permute-start(f32[128,2048]{1,0:T(8,128)} %copy-done.5), channel_id=1, source_target_pairs={{0,1},{1,0},{2,3},{3,2},{4,5},{5,4},{6,7},{7,6},{8,9},{9,8},{10,11... | collective-permute-start | bytes 3145736 | tf_op jit(solution)/shard_map/ppermute | solution.py:30
  240.3 30.5 %collective-permute-start.40 = (f32[128,2048]{1,0:T(8,128)}, f32[128,2048]{1,0:T(8,128)}, u32[]{:S(2)}, u32[]{:S(2)}) collective-permute-start(f32[128,2048]{1,0:T(8,128)} %get-tuple-element.117.refs_2_), channel_id=1, source_target_pairs={{0,1},{1,0},{2,3},{3,2},{4,5},{5,4},{6,7},{7,6},{8,9},{9,8},{10,11... | collective-permute-start | bytes 3145736 | tf_op jit(solution)/shard_map/ppermute | solution.py:30
  279.4 48.1 %collective-permute-start.18 = (f32[512,1024]{1,0:T(8,128)}, f32[512,1024]{1,0:T(8,128)}, u32[]{:S(2)}, u32[]{:S(2)}) collective-permute-start(f32[512,1024]{1,0:T(8,128)} %fusion.1), channel_id=1, source_target_pairs={{0,4},{4,0},{1,5},{5,1},{2,6},{6,2},{3,7},{7,3},{8,12},{12,8},{9,1... | collective-permute-start | bytes 6291464 | tf_op jit(solution)/shard_map/ppermute | solution.py:69
  300.6 55.8 %collective-permute-start.32 = (f32[128,2048]{1,0:T(8,128)}, f32[128,2048]{1,0:T(8,128)}, u32[]{:S(2)}, u32[]{:S(2)}) collective-permute-start(f32[128,2048]{1,0:T(8,128)} %collective-permute-done.5.refs_0_), channel_id=1, source_target_pairs={{0,1},{1,0},{2,3},{3,2},{4,5},{5,4},{6,7},{7,6},{8,9},{9,8},{10,11... | collective-permute-start | bytes 3145736 | tf_op jit(solution)/shard_map/ppermute | solution.py:30
  300.8 55.6 %collective-permute-start.33 = (f32[128,2048]{1,0:T(8,128)}, f32[128,2048]{1,0:T(8,128)}, u32[]{:S(2)}, u32[]{:S(2)}) collective-permute-start(f32[128,2048]{1,0:T(8,128)} %collective-permute-done.6.refs_1_), channel_id=1, source_target_pairs={{0,1},{1,0},{2,3},{3,2},{4,5},{5,4},{6,7},{7,6},{8,9},{9,8},{10,11... | collective-permute-start | bytes 3145736 | tf_op jit(solution)/shard_map/ppermute | solution.py:30
  301.1 55.3 %collective-permute-start.34 = (f32[128,2048]{1,0:T(8,128)}, f32[128,2048]{1,0:T(8,128)}, u32[]{:S(2)}, u32[]{:S(2)}) collective-permute-start(f32[128,2048]{1,0:T(8,128)} %collective-permute-done.12.refs_2_), channel_id=1, source_target_pairs={{0,1},{1,0},{2,3},{3,2},{4,5},{5,4},{6,7},{7,6},{8,9},{9,8},{10,11... | collective-permute-start | bytes 3145736 | tf_op jit(solution)/shard_map/ppermute | solution.py:30
  327.5 40.0 %collective-permute-start.19 = (f32[128,2048]{1,0:T(8,128)}, f32[128,2048]{1,0:T(8,128)S(1)}, u32[]{:S(2)}, u32[]{:S(2)}) collective-permute-start(f32[128,2048]{1,0:T(8,128)} %slice_add_fusion.5.refs_0_), channel_id=1, source_target_pairs={{0,2},{2,0},{1,3},{3,1},{4,6},{6,4},{5,7},{7,5},{8,10},{10,8},{9,1... | collective-permute-start | bytes 3145736 | tf_op jit(solution)/shard_map/ppermute | solution.py:69
  361.0 47.2 %collective-permute-start.41 = (f32[1024,512]{1,0:T(8,128)}, f32[1024,512]{1,0:T(8,128)S(1)}, u32[]{:S(2)}, u32[]{:S(2)}) collective-permute-start(f32[1024,512]{1,0:T(8,128)} %fusion.9), channel_id=1, source_target_pairs={{0,4},{4,0},{1,5},{5,1},{2,6},{6,2},{3,7},{7,3},{8,12},{12,8},{9,1... | collective-permute-start | bytes 6291464 | tf_op jit(solution)/shard_map/ppermute | solution.py:69
  367.5 48.4 %collective-permute-start.45 = (f32[512,512]{1,0:T(8,128)}, f32[512,512]{1,0:T(8,128)}, u32[]{:S(2)}, u32[]{:S(2)}) collective-permute-start(f32[512,512]{1,0:T(8,128)} %constant_dynamic-slice_fusion.3), channel_id=1, source_target_pairs={{0,16},{8,24},{16,0},{24,8},{1,17},{9,25},{17,1},{25,9},{2,18},{10... | collective-permute-start | bytes 3145736 | tf_op jit(solution)/shard_map/ppermute | solution.py:69
  375.1 69.1 %collective-permute-start.20 = (f32[256,2048]{1,0:T(8,128)}, f32[256,2048]{1,0:T(8,128)}, u32[]{:S(2)}, u32[]{:S(2)}) collective-permute-start(f32[256,2048]{1,0:T(8,128)} %slice.139), channel_id=1, source_target_pairs={{0,1},{1,0},{2,3},{3,2},{4,5},{5,4},{6,7},{7,6},{8,9},{9,8},{10,11... | collective-permute-start | bytes 6291464 | tf_op jit(solution)/shard_map/ppermute | solution.py:30
  409.5 33.1 %collective-permute-start.42 = (f32[256,1408]{1,0:T(8,128)}, f32[256,1408]{1,0:T(8,128)}, u32[]{:S(2)}, u32[]{:S(2)}) collective-permute-start(f32[256,1408]{1,0:T(8,128)} %get-tuple-element.170), channel_id=1, source_target_pairs={{0,4},{4,0},{1,5},{5,1},{2,6},{6,2},{3,7},{7,3},{8,12},{12,8},{9,1... | collective-permute-start | bytes 4325384 | tf_op jit(solution)/shard_map/ppermute | solution.py:69
  420.7 27.3 %collective-permute-start.25 = (f32[128,2048]{1,0:T(8,128)S(1)}, f32[128,2048]{1,0:T(8,128)S(1)}, u32[]{:S(2)}, u32[]{:S(2)}) collective-permute-start(f32[128,2048]{1,0:T(8,128)S(1)} %copy-done.3), channel_id=1, source_target_pairs={{0,1},{1,0},{2,3},{3,2},{4,5},{5,4},{6,7},{7,6},{8,9},{9,8},{10,11... | collective-permute-start | bytes 3145736 | tf_op jit(solution)/shard_map/ppermute | solution.py:30
  430.8 46.7 %collective-permute-start.47 = (f32[512,512]{1,0:T(8,128)S(1)}, f32[512,512]{1,0:T(8,128)S(1)}, u32[]{:S(2)}, u32[]{:S(2)}) collective-permute-start(f32[512,512]{1,0:T(8,128)S(1)} %constant_dynamic-slice_fusion.8), channel_id=1, source_target_pairs={{0,16},{8,24},{16,0},{24,8},{1,17},{9,25},{17,1},{25,9},{2,18},{10... | collective-permute-start | bytes 3145736 | tf_op jit(solution)/shard_map/ppermute | solution.py:69
  442.7 35.0 %collective-permute-start.43 = (f32[256,1408]{1,0:T(8,128)S(1)}, f32[256,1408]{1,0:T(8,128)S(1)}, u32[]{:S(2)}, u32[]{:S(2)}) collective-permute-start(f32[256,1408]{1,0:T(8,128)S(1)} %copy-done.67), channel_id=1, source_target_pairs={{0,4},{4,0},{1,5},{5,1},{2,6},{6,2},{3,7},{7,3},{8,12},{12,8},{9,1... | collective-permute-start | bytes 4325384 | tf_op jit(solution)/shard_map/ppermute | solution.py:69
  446.2 33.3 %collective-permute-start.21 = (f32[128,2048]{1,0:T(8,128)S(1)}, f32[128,2048]{1,0:T(8,128)S(1)}, u32[]{:S(2)}, u32[]{:S(2)}) collective-permute-start(f32[128,2048]{1,0:T(8,128)S(1)} %slice.141), channel_id=1, source_target_pairs={{0,2},{2,0},{1,3},{3,1},{4,6},{6,4},{5,7},{7,5},{8,10},{10,8},{9,1... | collective-permute-start | bytes 3145736 | tf_op jit(solution)/shard_map/ppermute | solution.py:69
  496.3 32.2 %collective-permute-start.51 = (f32[1408,256]{1,0:T(8,128)}, f32[1408,256]{1,0:T(8,128)S(1)}, u32[]{:S(2)}, u32[]{:S(2)}) collective-permute-start(f32[1408,256]{1,0:T(8,128)} %get-tuple-element.184), channel_id=1, source_target_pairs={{0,4},{4,0},{1,5},{5,1},{2,6},{6,2},{3,7},{7,3},{8,12},{12,8},{9,1... | collective-permute-start | bytes 4325384 | tf_op jit(solution)/shard_map/ppermute | solution.py:69
  501.6 28.2 %collective-permute-start.23 = (f32[128,2048]{1,0:T(8,128)}, f32[128,2048]{1,0:T(8,128)S(1)}, u32[]{:S(2)}, u32[]{:S(2)}) collective-permute-start(f32[128,2048]{1,0:T(8,128)} %slice_add_fusion.4.refs_0_), channel_id=1, source_target_pairs={{0,1},{1,0},{2,3},{3,2},{4,5},{5,4},{6,7},{7,6},{8,9},{9,8},{10,11... | collective-permute-start | bytes 3145736 | tf_op jit(solution)/shard_map/ppermute | solution.py:30
  (106 other events, 906.3 us)
Sparse Core Ops, SparseCore 0:
  15.9 83.4 all-gather.7
  100.9 79.2 all-gather.9
  216.0 78.4 all-gather.11

commit v3 on v2

v3 whole, which is shorter than its diff:
```python
import functools

import jax
import jax.numpy as jnp
from jax import lax
from jax.experimental import pallas as pl
from jax.experimental.pallas import tpu as pltpu
from jax.sharding import Mesh, PartitionSpec as P

epsilon = 1e-06
masked_value = -1e30
GROUP = 4
f32 = jnp.float32
bf16 = jnp.bfloat16

light = pl.CostEstimate(flops=1, bytes_accessed=1, transcendentals=0)


def dot(a, b):
    return jnp.dot(a, b, preferred_element_type=f32)


def dot_nt(a, b):
    return lax.dot_general(a, b, (((1,), (1,)), ((), ())), preferred_element_type=f32)


def dot_tn(a, b):
    return lax.dot_general(a, b, (((0,), (0,)), ((), ())), preferred_element_type=f32)


def arrange_kernel(places, length_ref, inputs_ref, cotangent_ref, kv_ref, inputs_out, cotangent_out, kv_out, quarter_out):
    k = pl.program_id(0)
    count = inputs_ref.shape[0]
    row = lax.broadcasted_iota(jnp.int32, (count, 1), 0) + places[k] * count
    valid = row < length_ref[0, 0]
    inputs_out[...] = inputs_ref[...]
    cotangent = jnp.where(valid, cotangent_ref[...].astype(f32), 0.0)
    cotangent_out[...] = cotangent.astype(bf16)
    kv_out[...] = jnp.where(valid, kv_ref[...].astype(f32), 0.0)

    @pl.when(k == 0)
    def _():
        quarter_out[...] = cotangent


def arrange(places, lengths, inputs, cotangent, kv):
    seq_len, width = inputs.shape
    q = seq_len // 4
    kv_width = kv.shape[1]
    picked = pl.BlockSpec((q, width), lambda k, p: (p[k], 0))
    placed = pl.BlockSpec((q, width), lambda k, p: (k, 0))
    return pl.pallas_call(
        arrange_kernel,
        grid_spec=pltpu.PrefetchScalarGridSpec(
            num_scalar_prefetch=1,
            grid=(4,),
            in_specs=[
                pl.BlockSpec((1, 1), lambda k, p: (0, 0)),
                picked,
                picked,
                pl.BlockSpec((q, kv_width), lambda k, p: (p[k], 0)),
            ],
            out_specs=[
                placed,
                placed,
                pl.BlockSpec((q, kv_width), lambda k, p: (k, 0)),
                pl.BlockSpec((q, width), lambda k, p: (0, 0)),
            ],
        ),
        out_shape=[
            jax.ShapeDtypeStruct((seq_len, width), bf16),
            jax.ShapeDtypeStruct((seq_len, width), bf16),
            jax.ShapeDtypeStruct((seq_len, kv_width), f32),
            jax.ShapeDtypeStruct((q, width), f32),
        ],
        name="arrange",
        compiler_params=pltpu.CompilerParams(vmem_limit_bytes=32 * 2**20),
        cost_estimate=light,
    )(places, lengths.reshape(1, 1), inputs, cotangent, kv)


def rotary_tables(positions, size):
    half_size = size // 2
    inverse = 10000.0 ** (-2.0 * jnp.arange(half_size, dtype=f32) / size)
    angles = positions.astype(f32)[:, None] * inverse[None, :]
    cosine, sine = jnp.cos(angles), jnp.sin(angles)
    return jnp.concatenate([cosine, cosine], axis=1), jnp.concatenate([-sine, sine], axis=1)


def rotate(values, same, crossed):
    return values * same + pltpu.roll(values, values.shape[-1] // 2, 1) * crossed


def norm_back(stream, inverse_rms, gain, grad_normed):
    weighted = gain * grad_normed
    return inverse_rms * weighted - stream * inverse_rms**3 * jnp.mean(weighted * stream, axis=-1, keepdims=True)


def inverse_rms(block):
    return lax.rsqrt(jnp.mean(block * block, axis=-1, keepdims=True) + epsilon)


def pack_z_kernel(places, *refs):
    blocks, (scale, out, picked) = refs[:6], refs[6:]
    width = picked.shape[2] // 2
    for j in range(6):
        out[j] = (blocks[j][0] * scale[...]).astype(bf16)
        for part in range(2):
            at = pl.ds(pl.multiple_of(places[part] * width, width), width)
            picked[j, :, part * width : (part + 1) * width] = (blocks[j][0, :, at] * scale[:, at]).astype(bf16)


def pack_z(own, far, scale, places, rows, tile=32):
    _, count, width = own.shape
    specs = [pl.BlockSpec((1, tile, width), lambda t, p, k=k: (p[2 + k], t, 0)) for k in range(GROUP - 1)]
    n = 2 * (GROUP - 1)
    out, picked = pl.pallas_call(
        pack_z_kernel,
        grid_spec=pltpu.PrefetchScalarGridSpec(
            num_scalar_prefetch=1,
            grid=(count // tile,),
            in_specs=specs + specs + [pl.BlockSpec((1, width), lambda t, p: (0, 0))],
            out_specs=[
                pl.BlockSpec((n, tile, width), lambda t, p: (0, t, 0)),
                pl.BlockSpec((n, tile, 2 * rows), lambda t, p: (0, t, 0)),
            ],
        ),
        out_shape=[
            jax.ShapeDtypeStruct((n, count, width), bf16),
            jax.ShapeDtypeStruct((n, count, 2 * rows), bf16),
        ],
        name="pack_z",
        compiler_params=pltpu.CompilerParams(vmem_limit_bytes=32 * 2**20),
        cost_estimate=light,
    )(places, *[own] * (GROUP - 1), *[far] * (GROUP - 1), scale.reshape(1, width))
    return out.reshape(n * count, width), picked.reshape(n * count, 2 * rows)


class Order:
    def __init__(self):
        self.core = ()
        self.links = {}

    def run(self, f, *args):
        n = len(args)
        args = lax.optimization_barrier((*args, *self.core))[:n]
        outs = f(*args)
        self.core = tuple(outs)[:1] if isinstance(outs, (list, tuple)) else (outs,)
        return outs

    def wait(self, a):
        (a,) = self.run(lambda a: lax.optimization_barrier((a,)), a)
        return a

    def move(self, a, axis, pairs, queue=True):
        before = self.links.get(axis, ()) if queue else ()
        a = lax.optimization_barrier((a, *self.core, *before))[0]
        a = lax.ppermute(a, axis, pairs)
        if queue:
            self.links[axis] = (a,)
        return a

    def swap(self, a, axis):
        return self.move(a, axis, [(0, 1), (1, 0)], queue=axis != "c")

    def pair_z(self, a, bit):
        return self.move(a, "z", [(i, i ^ bit) for i in range(GROUP)])


def split(a, axis, mine):
    n = a.shape[axis] // 2
    return lax.dynamic_slice_in_dim(a, mine * n, n, axis), lax.dynamic_slice_in_dim(a, (1 - mine) * n, n, axis)


def by_x(a, which, rows):
    n = a.shape[1] // (2 * rows)
    return jnp.concatenate([lax.dynamic_slice_in_dim(a, (2 * i + which) * rows, rows, 1) for i in range(n)], axis=1)


def call(kernel, name, ins, outs):
    return pl.pallas_call(
        kernel,
        out_shape=outs,
        name=name,
        compiler_params=pltpu.CompilerParams(vmem_limit_bytes=56 * 2**20),
        cost_estimate=light,
    )(*ins)


def probabilities(q, k, allowed, scale):
    scores = jnp.where(allowed, dot_nt(q, k) * scale, masked_value)
    exponent = jnp.exp(scores - jnp.max(scores, axis=-1, keepdims=True))
    return exponent / jnp.sum(exponent, axis=-1, keepdims=True)


def forward_kernel(
    scale, x_ref, gain_ref, wq_ref, wk_ref, wv_ref, wo_ref, same_ref, crossed_ref, pos_q_ref, pos_k_ref, length_ref,
    kept_ref, sent_ref, normed_ref, q_ref, k_ref, v_ref, attended_ref,
):
    stream = x_ref[...].astype(f32)
    normed_ref[...] = (stream * inverse_rms(stream) * gain_ref[...]).astype(bf16)
    normed = normed_ref[...]
    same, crossed = same_ref[...], crossed_ref[...]
    k = rotate(dot(normed, wk_ref[...]), same, crossed).astype(bf16)
    v = dot(normed, wv_ref[...]).astype(bf16)
    k_ref[...], v_ref[...] = k, v
    raw = dot(normed, wq_ref[...])
    length = length_ref[0, 0]
    allowed = (pos_k_ref[...] <= pos_q_ref[...]) & (pos_k_ref[...] < length)
    valid = (pos_q_ref[...] < length).astype(f32)
    size = k.shape[1]
    for h in range(raw.shape[1] // size):
        at = slice(h * size, (h + 1) * size)
        q = rotate(raw[:, at], same, crossed).astype(bf16)
        q_ref[:, at] = q
        weights = probabilities(q, k, allowed, scale).astype(bf16)
        attended_ref[:, at] = (dot(weights, v) * valid).astype(bf16)
    n = kept_ref.shape[0]
    sent_ref[...] = dot(attended_ref[n:], wo_ref[...])
    kept_ref[...] = dot(attended_ref[:n], wo_ref[...])


def backward_kernel(
    scale, ga_ref, wo_ref, wq_ref, q_ref, k_ref, v_ref, same_ref, crossed_ref, pos_q_ref, pos_k_ref, length_ref,
    kept_ref, sent_ref, kv_kept_ref, kv_sent_ref, gq_ref,
):
    k, v = k_ref[...], v_ref[...]
    same, crossed = same_ref[...], crossed_ref[...]
    length = length_ref[0, 0]
    allowed = (pos_k_ref[...] <= pos_q_ref[...]) & (pos_k_ref[...] < length)
    valid = (pos_q_ref[...] < length).astype(f32)
    grad_attended = (dot_nt(ga_ref[...], wo_ref[...]) * valid).astype(bf16)
    size = k.shape[1]
    grad_key = grad_value = 0.0
    for h in range(grad_attended.shape[1] // size):
        at = slice(h * size, (h + 1) * size)
        q, g = q_ref[:, at], grad_attended[:, at]
        probs = probabilities(q, k, allowed, scale)
        grad_probs = dot_nt(g, v)
        delta = jnp.sum(probs * grad_probs, axis=-1, keepdims=True)
        grad_scores = (probs * (grad_probs - delta)).astype(bf16)
        gq_ref[:, at] = rotate(dot(grad_scores, k) * scale, same, -crossed).astype(bf16)
        grad_key += dot_tn(grad_scores, q)
        grad_value += dot_tn(probs.astype(bf16), g)
    n = kept_ref.shape[0]
    for ref, at in ((kv_kept_ref, slice(0, n)), (kv_sent_ref, slice(n, 2 * n))):
        ref[:, :size] = grad_key[at] * scale
        ref[:, size:] = grad_value[at]
    sent_ref[...] = dot_nt(gq_ref[n:], wq_ref[...])
    kept_ref[...] = dot_nt(gq_ref[:n], wq_ref[...])


def pair_kernel(transposed, *refs):
    n = (len(refs) - 2) // 2
    kept, sent = refs[2 * n :]
    half = kept.shape[0]
    for out, at in ((sent, slice(half, 2 * half)), (kept, slice(0, half))):
        total = 0.0
        for rows, matrix in zip(refs[:n], refs[n : 2 * n]):
            total += (dot_nt if transposed else dot)(rows[at, :], matrix[...])
        out[...] = total


def pair_dots(name, rows, matrices, transposed, tile=512):
    count, depth = rows[0].shape
    width = matrices[0].shape[0 if transposed else 1]
    whole = pl.BlockSpec((count, depth), lambda t: (0, 0), pipeline_mode=pl.Buffered(1))
    part = pl.BlockSpec((tile, depth), lambda t: (t, 0)) if transposed else pl.BlockSpec((depth, tile), lambda t: (0, t))
    return pl.pallas_call(
        functools.partial(pair_kernel, transposed),
        grid=(width // tile,),
        in_specs=[whole] * len(rows) + [part] * len(matrices),
        out_specs=[pl.BlockSpec((count // 2, tile), lambda t: (0, t))] * 2,
        out_shape=[jax.ShapeDtypeStruct((count // 2, width), f32)] * 2,
        name=name,
        compiler_params=pltpu.CompilerParams(vmem_limit_bytes=48 * 2**20),
        cost_estimate=light,
    )(*rows, *matrices)


def out_kernel(places, left_ref, right_ref, out_ref):
    width = out_ref.shape[1] // GROUP
    for i in range(GROUP):
        at = pl.ds(pl.multiple_of(places[i] * width, width), width)
        out_ref[:, i * width : (i + 1) * width] = dot_tn(left_ref[...], right_ref[:, at])


def late_kernel(places, attended_ref, ga_ref, normed_ref, gq_ref, out_ref, sent_ref, kept_ref):
    width = out_ref.shape[1] // GROUP
    for i in range(GROUP):
        rows = slice(i * width, (i + 1) * width)
        sent = pl.ds(pl.multiple_of(places[i] * width, width), width)
        kept = pl.ds(pl.multiple_of(places[GROUP + i] * width, width), width)
        sent_ref[rows] = dot_tn(normed_ref[:, sent], gq_ref[...])
        kept_ref[rows] = dot_tn(normed_ref[:, kept], gq_ref[...])
        out_ref[:, rows] = dot_tn(attended_ref[...], ga_ref[:, kept])


def placed_call(kernel, name, places, ins, outs):
    def whole(shape):
        return pl.BlockSpec(shape, lambda t, p: (0,) * len(shape), pipeline_mode=pl.Buffered(1))

    return pl.pallas_call(
        kernel,
        grid_spec=pltpu.PrefetchScalarGridSpec(
            num_scalar_prefetch=1,
            grid=(1,),
            in_specs=[whole(a.shape) for a in ins],
            out_specs=[pl.BlockSpec(a.shape, lambda t, p: (0,) * len(a.shape)) for a in outs],
        ),
        out_shape=outs,
        name=name,
        compiler_params=pltpu.CompilerParams(vmem_limit_bytes=48 * 2**20),
        cost_estimate=light,
    )(places, *ins)


def rows_call(kernel, name, quarters, stacked, shared, outs, totals, tile=16, prefetch=()):
    count, width = quarters[0][0].shape
    args = [a for group in quarters for a in group] + list(stacked) + list(shared)
    specs = [pl.BlockSpec((tile, width), lambda t, *p: (t, 0))] * (4 * len(quarters))
    specs += [pl.BlockSpec((4, tile, a.shape[2]), lambda t, *p: (0, t, 0)) for a in stacked]
    specs += [pl.BlockSpec(a.shape, lambda t, *p: (0, 0)) for a in shared]
    out_specs = [pl.BlockSpec((4, tile, w), lambda t, *p: (0, t, 0)) for w, _ in outs]
    out_specs += [pl.BlockSpec((1, width), lambda t, *p: (0, 0))] * totals
    out_shape = [jax.ShapeDtypeStruct((4, count, w), kind) for w, kind in outs]
    out_shape += [jax.ShapeDtypeStruct((1, width), f32)] * totals
    return pl.pallas_call(
        kernel,
        grid_spec=pltpu.PrefetchScalarGridSpec(
            num_scalar_prefetch=len(prefetch), grid=(count // tile,), in_specs=specs, out_specs=out_specs
        ),
        out_shape=out_shape,
        name=name,
        compiler_params=pltpu.CompilerParams(vmem_limit_bytes=32 * 2**20),
        cost_estimate=light,
    )(*prefetch, *args)


def mid_kernel(places, *refs):
    hidden, (gain, out), picked = refs[:4], refs[4:6], refs[6:]
    for j in range(4):
        h = hidden[j][...]
        r = inverse_rms(h)
        out[j] = (h * r * gain[...]).astype(bf16)
        for part in range(2 * len(picked)):
            n = picked[0].shape[2] // 2
            at = pl.ds(pl.multiple_of(places[part] * n, n), n)
            picked[0][j, :, part * n : (part + 1) * n] = (hidden[j][:, at] * r * gain[:, at]).astype(bf16)


def mid_back_kernel(*refs):
    grads, hidden, (grad_out, gain, grad_hidden, rounded, total) = refs[:4], refs[4:8], refs[8:]
    gain = gain[...]
    acc = 0.0
    for j in range(4):
        h, g = hidden[j][...], grads[j][...]
        r = inverse_rms(h)
        acc += jnp.sum(g * h * r, axis=0, keepdims=True)
        back = grad_out[j].astype(f32) + norm_back(h, r, gain, g)
        grad_hidden[j] = back
        rounded[j] = back.astype(bf16)

    @pl.when(pl.program_id(0) == 0)
    def _():
        total[...] = jnp.zeros_like(total)

    total[...] += acc


def in_back_kernel(places, *refs):
    sums, (keyed, inputs, grad_hidden, gain, out, total) = refs[:4], refs[4:]
    gain = gain[...]
    acc = 0.0
    for j in range(4):
        stream = inputs[j].astype(f32)
        g = sums[j][...] + keyed[j]
        r = inverse_rms(stream)
        acc += jnp.sum(g * stream * r, axis=0, keepdims=True)
        out[places[j]] = (grad_hidden[j] + norm_back(stream, r, gain, g)).astype(bf16)

    @pl.when(pl.program_id(0) == 0)
    def _():
        total[...] = jnp.zeros_like(total)

    total[...] += acc


def add_kernel(places, *refs):
    left, right, (out,) = refs[:4], refs[4:8], refs[8:]
    for j in range(4):
        out[places[j]] = (left[j][...] + right[j][...]).astype(bf16)


def pack_kernel(n, places, *refs):
    blocks, scale, out, picked = refs[:n], refs[n], refs[n + 1], refs[n + 2]
    width = picked.shape[2] // 2
    for j in range(n):
        out[j] = (blocks[j][...] * scale[...]).astype(bf16)
        for part in range(2):
            at = pl.ds(pl.multiple_of(places[part] * width, width), width)
            picked[j, :, part * width : (part + 1) * width] = (blocks[j][:, at] * scale[:, at]).astype(bf16)


def pack(blocks, scale, places, rows, tile=32):
    n = len(blocks)
    count, width = blocks[0].shape
    block = pl.BlockSpec((tile, width), lambda t, places: (t, 0))
    out, picked = pl.pallas_call(
        functools.partial(pack_kernel, n),
        grid_spec=pltpu.PrefetchScalarGridSpec(
            num_scalar_prefetch=1,
            grid=(count // tile,),
            in_specs=[block] * n + [pl.BlockSpec((1, width), lambda t, places: (0, 0))],
            out_specs=[
                pl.BlockSpec((n, tile, width), lambda t, places: (0, t, 0)),
                pl.BlockSpec((n, tile, 2 * rows), lambda t, places: (0, t, 0)),
            ],
        ),
        out_shape=[
            jax.ShapeDtypeStruct((n, count, width), bf16),
            jax.ShapeDtypeStruct((n, count, 2 * rows), bf16),
        ],
        compiler_params=pltpu.CompilerParams(vmem_limit_bytes=32 * 2**20),
        cost_estimate=light,
    )(places, *blocks, scale.reshape(1, width))
    return out.reshape(n * count, width), picked.reshape(n * count, 2 * rows)


def ffn_kernel(own, has_prev, *refs):
    nm_ref, go_ref, nmc_ref, goc_ref, wg_ref, wu_ref, wd_ref = refs[:7]
    previous = refs[7:13] if has_prev else None
    outs = refs[13:] if has_prev else refs[7:]
    gate = dot(nm_ref[...], wg_ref[...])
    up = dot(nm_ref[...], wu_ref[...])
    grad_mixed = dot_nt(go_ref[...], wd_ref[...]).astype(bf16).astype(f32)
    sig = jax.nn.sigmoid(gate)
    gate_sig = gate * sig
    mixed = (gate_sig * up).astype(bf16)
    grad_gate = (grad_mixed * up * sig * (1.0 + gate * (1.0 - sig))).astype(bf16)
    grad_up = (grad_mixed * gate_sig).astype(bf16)
    n = nmc_ref.shape[1] // 2
    by_gate = dot_tn(nmc_ref[...], grad_gate)
    by_up = dot_tn(nmc_ref[...], grad_up)
    by_down = dot_tn(mixed, goc_ref[...])
    sums = (by_gate[:n], by_gate[n:], by_up[:n], by_up[n:], by_down[:, :n], by_down[:, n:])
    for i in range(6):
        outs[i][...] = sums[i] + previous[i][...] if has_prev else sums[i]
    if own:
        outs[6][...] = mixed
        outs[7][...] = grad_gate
        outs[8][...] = grad_up


def ffn(nm, go, nm_columns, go_columns, w_gate, w_up, w_down, previous=(), own=False, tile=512):
    count, width = nm.shape
    hidden = w_gate.shape[1]
    n = nm_columns.shape[1] // 2

    def whole(shape):
        return pl.BlockSpec(shape, lambda t: (0, 0), pipeline_mode=pl.Buffered(1))

    across = pl.BlockSpec((n, tile), lambda t: (0, t))
    down = pl.BlockSpec((tile, n), lambda t: (t, 0))
    sums = [across] * 4 + [down] * 2
    out_specs = list(sums)
    out_shape = [jax.ShapeDtypeStruct((n, hidden), f32)] * 4 + [jax.ShapeDtypeStruct((hidden, n), f32)] * 2
    if own:
        out_specs += [pl.BlockSpec((count, tile), lambda t: (0, t))] * 3
        out_shape += [jax.ShapeDtypeStruct((count, hidden), bf16)] * 3
    columns = pl.BlockSpec((width, tile), lambda t: (0, t))
    in_specs = [whole(nm.shape), whole(go.shape), whole(nm_columns.shape), whole(go_columns.shape)]
    in_specs += [columns, columns, pl.BlockSpec((tile, width), lambda t: (t, 0))]
    in_specs += sums if previous else []
    return pl.pallas_call(
        functools.partial(ffn_kernel, own, bool(previous)),
        grid=(pl.cdiv(hidden, tile),),
        in_specs=in_specs,
        out_specs=out_specs,
        out_shape=out_shape,
        compiler_params=pltpu.CompilerParams(vmem_limit_bytes=56 * 2**20),
        cost_estimate=light,
    )(nm, go, nm_columns, go_columns, w_gate, w_up, w_down, *previous)


def shards(
    sizes,
    inputs,
    seq_lengths,
    norm_in,
    w_query,
    w_key,
    w_value,
    w_out,
    norm_mid,
    w_gate,
    w_up,
    w_down,
    out_cotangent,
    kv_cotangent,
):
    n_outer, n_dp = sizes
    seq_len, width = inputs.shape
    half, quarter = seq_len // 2, seq_len // 4
    head = w_key.shape[1]
    own_heads = w_query.shape[1]
    scale = head ** (-0.5)
    rows = width // n_dp
    z, x = lax.axis_index("z"), lax.axis_index("x")
    order = Order()
    run, swap, wait = order.run, order.swap, order.wait
    one = jnp.minimum(seq_lengths[0], 1).astype(f32)
    me = 2 * lax.axis_index("c") + lax.axis_index("y")
    quarters = jnp.stack([me ^ k for k in range(4)]).astype(jnp.int32)
    others = [lax.rem(z + k, GROUP) for k in range(1, GROUP)]
    places = jnp.stack([2 * z + 1 - x, 2 * z + x, *others]).astype(jnp.int32)
    positions = (quarters[:, None] * quarter + jnp.arange(quarter, dtype=jnp.int32)[None, :]).reshape(seq_len)
    gain_in, gain_mid = norm_in.reshape(1, width), norm_mid.reshape(1, width)
    ones = jnp.ones_like(norm_mid)
    same, crossed = rotary_tables(positions, head)
    masks = (same, crossed, positions[:, None], positions[None, :], seq_lengths.reshape(1, 1))
    weights = (w_gate, w_up, w_down)

    def shape(n, kind, count=seq_len):
        return jax.ShapeDtypeStruct((count, n), kind)

    def scaled(block):
        return block * inverse_rms(block)

    def remote(gathered):
        return [lax.dynamic_index_in_dim(gathered, k, 0, keepdims=False) for k in others]

    def columns(part):
        part = part.reshape(part.shape[0], n_outer, GROUP, 2, rows) if n_outer > 1 else part
        taken = []
        for which in (1 - x, x):
            if n_outer > 1:
                cut = lax.dynamic_index_in_dim(part, z, 2, keepdims=False)
                cut = lax.dynamic_index_in_dim(cut, which, 2, keepdims=False)
                taken.append(cut.reshape(part.shape[0], n_outer * rows))
            else:
                taken.append(lax.dynamic_slice_in_dim(part, (2 * z + which) * rows, rows, 1))
        return jnp.concatenate(taken, axis=1)

    def packed_z(own, far, gain):
        if n_outer == 1:
            return run(lambda own, far: pack_z(own, far, gain, places, rows), own, far)
        return packed(remote(own), remote(far), gain)

    def packed(blocks, far, gain):
        blocks = [*blocks, *far]
        if n_outer == 1:
            return run(lambda *blocks: pack(blocks, gain, places, rows), *blocks)
        whole = run(lambda *blocks: (jnp.concatenate(blocks, axis=0) * (gain * one)).astype(bf16), *blocks)
        return whole, columns(whole)

    def add_y(kept, received):
        return kept[:quarter] + received

    def wgrads(*args):
        return ffn(*args[:4], *weights, previous=args[4:])

    inputs, grad_down_in, kv_cotangent, go_quarter = run(
        arrange, quarters, seq_lengths, inputs, out_cotangent, kv_cotangent
    )
    go_z = lax.all_gather(go_quarter, "z", axis=0, tiled=False)

    kept, sent, normed, queries, key_rot, value_rows, attended = run(
        lambda *args: call(
            functools.partial(forward_kernel, scale),
            "attention_forward",
            args,
            [shape(width, f32, half), shape(width, f32, half), shape(width, bf16), shape(own_heads, bf16),
             shape(head, bf16), shape(head, bf16), shape(own_heads, bf16)],
        ),
        inputs, gain_in, w_query, w_key, w_value, w_out, *masks,
    )
    sent = swap(sent, "c")
    go_own_columns = run(columns, grad_down_in)
    kept = run(jnp.add, kept, sent)
    received = swap(kept[quarter:], "y")

    def hidden_of(kept, received, inputs):
        own = add_y(kept, received) + inputs.astype(f32)
        return own, scaled(own)

    own, scaled_own = run(hidden_of, kept, received, inputs[:quarter])
    nm_z_own = lax.all_gather(scaled_own, "z", axis=0, tiled=False)
    other = swap(own, "y")
    far_own = swap(own, "c")
    go_remote = run(remote, go_z)
    scaled_other = run(scaled, other)
    nm_z_other = lax.all_gather(scaled_other, "z", axis=0, tiled=False)
    far_other = swap(other, "c")
    hidden = [own, other, far_own, far_other]

    picked = [(2 * rows, bf16)] if n_outer == 1 else []
    normed_mid, *nm_own_columns = run(
        lambda *hidden: rows_call(
            mid_kernel, "mid_norm", [hidden], [], [gain_mid], [(width, bf16), *picked], 0, prefetch=(places,)
        ),
        *hidden,
    )
    normed_mid = normed_mid.reshape(seq_len, width)
    nm_own_columns = nm_own_columns[0].reshape(seq_len, 2 * rows) if n_outer == 1 else columns(normed_mid)
    go_other = [swap(go_remote[0], "y")]
    *sums, mixed, grad_gate, grad_up = run(
        lambda *args: ffn(*args, *weights, own=True),
        normed_mid, grad_down_in, nm_own_columns, go_own_columns,
    )
    go_other[0] = wait(go_other[0])
    mid_kept, mid_sent = run(
        lambda *args: pair_dots("mid_part", args[:2], args[2:], True), grad_gate, grad_up, w_gate, w_up
    )
    mid_sent = swap(mid_sent, "c")
    kept = run(jnp.add, mid_kept, mid_sent)
    received = swap(kept[quarter:], "y")
    own = run(add_y, kept, received)
    other = swap(own, "y")
    nm_z_own = wait(nm_z_own)
    far_own = swap(own, "c")
    go_far, nm_far = swap(go_z, "c"), swap(nm_z_own, "c")
    down_kept, down_sent = run(lambda *args: pair_dots("down_part", args[:1], args[1:], False), mixed, w_down)
    down_sent = swap(down_sent, "c")
    go, go_columns = packed_z(go_z, go_far, ones)
    nm, nm_columns = packed_z(nm_z_own, nm_far, norm_mid)
    other = wait(other)
    go_other += [order.move(block, "y", [(0, 1), (1, 0)], queue=False) for block in go_remote[1:]]
    grad_mid = [own, other, far_own, swap(other, "c")]
    grad_hidden, grad_attention, grad_norm_mid = run(
        lambda *args: rows_call(
            mid_back_kernel, "mid_back", [args[:4], args[4:]], [grad_down_in.reshape(4, quarter, width)], [gain_mid],
            [(width, f32), (width, bf16)], 1,
        ),
        *grad_mid, *hidden,
    )
    grad_attention = grad_attention.reshape(seq_len, width)

    if n_outer == 1:
        at_x = 2 * jnp.arange(GROUP, dtype=jnp.int32)
        at_x = jnp.concatenate([at_x + 1 - x, at_x + x])
        (out_sent,) = run(
            lambda *args: placed_call(out_kernel, "out_grad", at_x, args, [shape(width // 2, f32, own_heads)]),
            attended, grad_attention,
        )
    else:
        out_sent = run(dot_tn, attended, by_x(grad_attention, 1 - x, rows))
    out_sent = swap(out_sent, "x")
    kept, sent, kv_kept, kv_sent, grad_query = run(
        lambda *args: call(
            functools.partial(backward_kernel, scale),
            "attention_backward",
            args,
            [shape(width, f32, half), shape(width, f32, half), shape(2 * head, f32, half), shape(2 * head, f32, half),
             shape(own_heads, bf16)],
        ),
        grad_attention, w_out, w_query, queries, key_rot, value_rows, *masks,
    )
    sent = swap(sent, "c")
    kv_sent = swap(kv_sent, "c")
    if n_outer == 1:
        out_kept, query_sent, query_kept = run(
            lambda *args: placed_call(
                late_kernel, "late_grads", at_x, args,
                [shape(width // 2, f32, own_heads), shape(own_heads, f32, width // 2), shape(own_heads, f32, width // 2)],
            ),
            attended, grad_attention, normed, grad_query,
        )
    else:
        out_kept = run(dot_tn, attended, by_x(grad_attention, x, rows))
        query_sent = run(dot_tn, by_x(normed, 1 - x, rows), grad_query)
        query_kept = run(dot_tn, by_x(normed, x, rows), grad_query)

    query_sent = order.move(query_sent, "x", [(0, 1), (1, 0)], queue=False)

    sums = run(wgrads, nm, go, nm_columns, go_columns, *sums)
    go_other[1:] = [wait(block) for block in go_other[1:]]
    out_half = run(jnp.add, out_kept, out_sent)
    if n_outer == 1:
        out_kept, out_sent = run(lambda a: split(a, 1, z // 2), out_half)
        out_sent = order.pair_z(out_sent, 2)
    nm_z_other = wait(nm_z_other)
    go_far = [swap(block, "c") for block in go_other]
    nm_far = swap(nm_z_other, "c")
    kept = run(jnp.add, kept, sent)
    received = swap(kept[quarter:], "y")
    kv_kept = run(jnp.add, kv_kept, kv_sent)
    kv_received = order.move(kv_kept[quarter:], "y", [(0, 1), (1, 0)], queue=False)
    down_kept = run(jnp.add, down_kept, down_sent)
    go, go_columns = packed(go_other, go_far, ones)
    nm, nm_columns = packed_z(nm_z_other, nm_far, norm_mid)
    sums = run(wgrads, nm, go, nm_columns, go_columns, *sums)
    gate_sent = swap(sums[0], "x")
    summed_own = run(add_y, kept, received)
    summed_other = swap(summed_own, "y")
    kv_own = run(add_y, kv_kept, kv_received)
    kv_other = order.move(kv_own, "y", [(0, 1), (1, 0)], queue=False)
    if n_outer == 1:
        out_half = run(jnp.add, out_kept, out_sent)
        out_kept, out_sent = run(lambda a: split(a, 1, z % 2), out_half)
        out_sent = order.pair_z(out_sent, 1)
    query_half = run(jnp.add, query_kept, query_sent)
    if n_outer == 1:
        query_kept, query_sent = run(lambda a: split(a, 0, z // 2), query_half)
        query_sent = order.pair_z(query_sent, 2)
    grad_w_gate = run(jnp.add, sums[1], gate_sent)
    up_sent = swap(sums[2], "x")

    summed_other = wait(summed_other)
    down_received = swap(down_kept[quarter:], "y")
    far = [swap(a, "c") for a in (kv_own, kv_other, summed_own, summed_other)]

    def key_value(*parts):
        grad_kv = jnp.concatenate(parts, axis=0) + kv_cotangent
        grad_key = grad_kv[:, :head]
        crossed_key = jnp.concatenate([grad_key[:, head // 2 :], grad_key[:, : head // 2]], axis=1)
        return (grad_key * same - crossed_key * crossed).astype(bf16), grad_kv[:, head:].astype(bf16)

    grad_key, grad_value = run(key_value, kv_own, kv_other, far[0], far[1])
    keyed = run(lambda k, v: dot_nt(k, w_key) + dot_nt(v, w_value), grad_key, grad_value)
    grad_inputs, grad_norm_in = run(
        lambda keyed, *summed: rows_call(
            in_back_kernel, "in_back", [summed],
            [keyed.reshape(4, quarter, width), inputs.reshape(4, quarter, width), grad_hidden], [gain_in],
            [(width, bf16)], 1, prefetch=(quarters,),
        ),
        keyed, summed_own, summed_other, far[2], far[3],
    )

    piece = rows // 4
    m = 2 * lax.axis_index("y") + lax.axis_index("c")

    def small_sums(grad_key, grad_value, grad_norm_in, grad_norm_mid):
        kv = jnp.concatenate([dot_tn(normed, grad_key), dot_tn(normed, grad_value)], axis=1)
        kv = lax.dynamic_index_in_dim(kv.reshape(n_dp, 4, piece, 2 * head), m, 1, keepdims=False)
        gains = jnp.concatenate([grad_norm_in, grad_norm_mid]).reshape(2, n_dp, rows).transpose(1, 0, 2)
        gains = jnp.pad(gains, ((0, 0), (0, 6), (0, 2 * head - rows)))
        small = jnp.concatenate([kv, gains], axis=1).reshape(n_dp // 2, 2, -1, 2 * head)
        return split(small, 1, x)

    small, small_sent = run(small_sums, grad_key, grad_value, grad_norm_in, grad_norm_mid)
    small_sent = order.move(small_sent, "x", [(0, 1), (1, 0)], queue=False)
    down_own = run(add_y, down_kept, down_received)
    down_other = swap(down_own, "y")
    small = run(jnp.add, small, small_sent).reshape(n_dp // 2, -1, 2 * head)
    if n_outer == 1:
        grad_w_out = run(jnp.add, out_kept, out_sent)
        small, small_sent = run(lambda a: split(a, 0, z // 2), small)
        small_sent = order.move(small_sent, "z", [(i, i ^ 2) for i in range(GROUP)], queue=False)
        small = run(jnp.add, small, small_sent)
        small, small_sent = run(lambda a: split(a, 0, z % 2), small)
        small_sent = order.move(small_sent, "z", [(i, i ^ 1) for i in range(GROUP)], queue=False)
    else:
        small = lax.psum_scatter(small, ("o", "z"), scatter_dimension=0, tiled=True)
        grad_w_out = lax.psum_scatter(out_half, ("o", "z"), scatter_dimension=1, tiled=True)
    grad_w_up = run(jnp.add, sums[3], up_sent)
    last_sent = swap(sums[4], "x")
    if n_outer == 1:
        small = run(jnp.add, small, small_sent)
        query_half = run(jnp.add, query_kept, query_sent)
        query_kept, query_sent = run(lambda a: split(a, 0, z % 2), query_half)
        query_sent = order.pair_z(query_sent, 1)
    kv = run(lambda a: lax.all_gather(a[0, :piece], ("y", "c"), axis=0, tiled=True), small)
    out_norm_in, out_norm_mid = small[0, piece, :rows], small[0, piece + 1, :rows]

    down_other = wait(down_other)
    down = [down_own, down_other, swap(down_own, "c"), swap(down_other, "c")]
    (result,) = run(
        lambda *args: rows_call(
            add_kernel, "result", [args[:4], args[4:]], [], [], [(width, bf16)], 0, prefetch=(quarters,)
        ),
        *down, *hidden,
    )
    if n_outer == 1:
        grad_w_query = run(jnp.add, query_kept, query_sent)
    else:
        grad_w_query = lax.psum_scatter(query_half, ("o", "z"), scatter_dimension=0, tiled=True)
    grad_w_down = run(jnp.add, sums[5], last_sent)
    if n_outer > 1:
        grad_w_down = lax.psum_scatter(grad_w_down, "o", scatter_dimension=1, tiled=True)
        grad_w_gate = lax.psum_scatter(grad_w_gate, "o", scatter_dimension=0, tiled=True)
        grad_w_up = lax.psum_scatter(grad_w_up, "o", scatter_dimension=0, tiled=True)

    return (
        result.reshape(seq_len, width),
        grad_inputs.reshape(seq_len, width),
        out_norm_in,
        grad_w_query,
        kv[:, :head],
        kv[:, head:],
        grad_w_out,
        out_norm_mid,
        grad_w_gate,
        grad_w_up,
        grad_w_down,
    )


def solution(mesh):
    n_dp = mesh.shape["dp"]
    n_outer = n_dp // (2 * GROUP)
    split = Mesh(mesh.devices.reshape(n_outer, GROUP, 2, 2, 2), ("o", "z", "x", "y", "c"))
    dp, mp = ("o", "z", "x"), ("y", "c")

    def program(*args):
        return shards((n_outer, n_dp), *args)

    return jax.shard_map(
        program,
        mesh=split,
        in_specs=(
            P(dp, None),
            P(dp),
            P(),
            P(None, mp),
            P(),
            P(),
            P(mp, None),
            P(),
            P(None, mp),
            P(None, mp),
            P(mp, None),
            P(dp, None),
            P(dp, None),
        ),
        out_specs=(
            P(dp, None),
            P(dp, None),
            P(dp),
            P(dp, mp),
            P(dp, None),
            P(dp, None),
            P(mp, dp),
            P(dp),
            P(dp, mp),
            P(dp, mp),
            P(mp, dp),
        ),
        check_vma=False,
    )
```

time: 554 us -> 492 us (0.89)
  waiting for transfers between devices: 239 us -> 171 us
  Pallas kernels: 131 us -> 168 us
  matrix products: 29.8 us -> 2.4 us
    ppermute x52 -> x46, waiting for transfers between devices: 209 us -> 139 us  [move(): a = lax.ppermute(a, axis, pairs)]
    pallas_call x0 -> x8, Pallas kernels: none -> 38.6 us  [the longest x2 16.5 us: pair_dots(): pl.pallas_call(functools.partial(pair_kernel, transposed), grid=(width //...]
    all_gather x1, waiting for transfers between devices: 4.39 us -> 31.9 us  [shards(): go_z = lax.all_gather(go_quarter, 'z', axis=0, tiled=False)]
    all_gather x2, waiting for transfers between devices: 25.1 us -> 0.01 us  [the longest x1 0.01 us: shards(): nm_z_own = lax.all_gather(scaled_own, 'z', axis=0, tiled=False)]
    dot_general x4 -> x2, matrix products: 15.2 us -> 1.44 us  [dot_nt(): lax.dot_general(a, b, (((1,), (1,)), ((), ())), preferred_element_type=f32)]
    add x21 -> x23, other arithmetic: 20.9 us -> 33.2 us  [the longest x17 24.4 us: run(): outs = f(*args)]
    dot_general x6 -> x2, matrix products: 11.1 us -> 0.96 us  [dot_tn(): lax.dot_general(a, b, (((0,), (0,)), ((), ())), preferred_element_type=f32)]
    unnamed x152 -> x110, local copies, waits for them, and re-layouts: 17.1 us -> 27 us
  transfers between devices with their start and end apart: 55 -> 49, of which waited for: 23 -> 22; matrix products, arithmetic and copies ran while one was open for 16% -> 13% of each run, Pallas kernels for 23% -> 34%
where the time goes in v3:
time: 492 us; the launch traced here: 484 us
  waiting for transfers between devices  171 us (35%)
  Pallas kernels  168 us (34%)
  local copies, waits for them, and re-layouts  48.4 us (10%)
  other arithmetic  41.4 us (8%)
  starting transfers between devices  31.8 us (6%)
  between operations  15.3 us (3%)
  blocking collectives  5.79 us (1%)
    ppermute x46, waiting for transfers between devices, move(): a = lax.ppermute(a, axis, pairs)  139 us
    pallas_call x3, Pallas kernels, ffn(): pl.pallas_call(functools.partial(ffn_kernel, own, bool(previous)), grid=(...  75.9 us
    all_gather x1, waiting for transfers between devices, shards(): go_z = lax.all_gather(go_quarter, 'z', axis=0, tiled=False)  31.9 us
    ppermute x46, starting transfers between devices, move(): a = lax.ppermute(a, axis, pairs)  31.4 us
    unnamed x110, local copies, waits for them, and re-layouts  27 us
    pallas_call x4, Pallas kernels, rows_call(): pl.pallas_call(kernel, grid_spec=pltpu.PrefetchScalarGridSpec(num_scalar_...  26.2 us
    add x17, other arithmetic, run(): outs = f(*args)  24.4 us
    pallas_call x2, Pallas kernels, call(): pl.pallas_call(kernel, out_shape=outs, name=name, compiler_params=pltpu.C...  23.4 us
  transfers between devices with their start and end apart: 49, of which 22 were waited for; matrix products, arithmetic and copies ran while one was open for 13% of the time, Pallas kernels for 34%

profile of v3, /device:TPU:0, one launch (start us, length us, event | category | flops | bytes accessed | tf_op | source)
XLA Modules:
  0.0 483.8 jit_solution(9149224347229383020)
XLA Ops:
  19.8 12.0 %attention_forward.1 = (f32[256,2048]{1,0:T(8,128)}, f32[256,2048]{1,0:T(8,128)}, bf16[512,2048]{1,0:T(8,128)(2,1)}, bf16[512,512]{1,0:T(8,128)(2,1)}, bf16[512,...) custom-call(bf16[512,2048]{1,0:T(8,128)(2,1)} %copy-done.4, f32[1,2048]{1,0:T(1,128)} %bitcast.96, ...), custom_call_target="tpu_custom_call" | custom-call | flops 1 | bytes 1 | tf_op jit(solution)/shard_map/attention_forward/pallas_call | solution.py:181
  42.5 22.4 %collective-permute-done.1 = f32[128,2048]{1,0:T(8,128)S(1)} collective-permute-done((f32[128,2048]{1,0:T(8,128)S(1)}, f32[128,2048]{1,0:T(8,128)S(1)}, u32[]{:S(2)}, u32[]{:S(2)}) %collective-permute-start.1) | collective-permute-done | bytes 1048608 | tf_op jit(solution)/shard_map/ppermute | solution.py:158
  68.5 31.9 %all-gather.8.cloned.1.call-done = f32[512,2048]{1,0:T(8,128)} async-done(((f32[128,2048]{1,0:T(8,128)}), f32[512,2048]{1,0:T(8,128)}) %all-gather.8.cloned.1.call-update) | async-done | bytes 4194320 | tf_op jit(solution)/shard_map/all_gather | solution.py:566
  108.1 5.3 %mid_norm.1 = (bf16[4,128,2048]{2,1,0:T(8,128)(2,1)S(1)}, bf16[4,128,512]{2,1,0:T(8,128)(2,1)S(1)}) custom-call(s32[5]{0:T(128)S(1)} %stack.43.places, f32[128,2048]{1,0:T(8,128)S(1)} %get-tuple-element.545.refs_0_.refs_4_, f32[128,2048]{1,0:T(8,128)S(1)} %collective-permute-done.2.refs_1_.refs_5_, f32[128,2048]{1,0:T(8,128)S(1)} %collective-permute-done.3.refs_2_.refs_6_, ...), custom_call_target="tpu_custom_call" | custom-call | flops 1 | bytes 1 | tf_op jit(solution)/shard_map/mid_norm/pallas_call | solution.py:328
  117.0 20.2 %shard_map.212 = (f32[256,1408]{1,0:T(8,128)}, f32[256,1408]{1,0:T(8,128)}, f32[256,1408]{1,0:T(8,128)}, f32[256,1408]{1,0:T(8,128)}, f32[1408,256]{1,0:T(8,128)...) custom-call(bf16[512,2048]{1,0:T(8,128)(2,1)} %bitcast.86, ...), custom_call_target="tpu_custom_call" | custom-call | flops 1 | bytes 1 | tf_op jit(solution)/shard_map/pallas_call | solution.py:475
  143.8 10.2 %mid_part.1 = (f32[256,2048]{1,0:T(8,128)S(1)}, f32[256,2048]{1,0:T(8,128)}) custom-call(bf16[512,1408]{1,0:T(8,128)(2,1)S(1)} %copy-done.22, bf16[512,1408]{1,0:T(8,128)(2,1)S(1)} %copy-done.23, bf16[2048,1408]{1,0:T(8,128)(2,1)} %refs_4_.5, bf16[2048,1408]{1,0:T(8,128)(2,1)} %refs_5_.5), custom_call_target="tpu_custom_call" | custom-call | flops 1 | bytes 1 | tf_op jit(solution)/shard_map/mid_part/pallas_call | solution.py:269
  154.0 4.4 collective-permute-done.6
  160.4 23.7 %collective-permute-done.7 = f32[128,2048]{1,0:T(8,128)S(1)} collective-permute-done((f32[128,2048]{1,0:T(8,128)S(1)}, f32[128,2048]{1,0:T(8,128)S(1)}, u32[]{:S(2)}, u32[]{:S(2)}) %collective-permute-start.7) | collective-permute-done | bytes 1048608 | tf_op jit(solution)/shard_map/ppermute | solution.py:158
  188.7 6.2 %down_part.1 = (f32[256,2048]{1,0:T(8,128)S(1)}, f32[256,2048]{1,0:T(8,128)S(1)}) custom-call(bf16[512,1408]{1,0:T(8,128)(2,1)S(1)} %copy-done.24, bf16[1408,2048]{1,0:T(8,128)(2,1)} %refs_6_.5), custom_call_target="tpu_custom_call" | custom-call | flops 1 | bytes 1 | tf_op jit(solution)/shard_map/down_part/pallas_call | solution.py:269
  195.0 5.3 %pack_z.3 = (bf16[6,128,2048]{2,1,0:T(8,128)(2,1)S(1)}, bf16[6,128,512]{2,1,0:T(8,128)(2,1)S(1)}) custom-call(s32[5]{0:T(128)S(1)} %stack.43.places, f32[4,128,2048]{2,1,0:T(8,128)S(1)} %bitcast.65, f32[4,128,2048]{2,1,0:T(8,128)S(1)} %bitcast.66, f32[4,128,2048]{2,1,0:T(8,128)S(1)} %bitcast.67, ...), custom_call_target="tpu_custom_call" | custom-call | flops 1 | bytes 1 | tf_op jit(solution)/shard_map/pack_z/pallas_call | solution.py:117
  213.8 6.5 %mid_back.1 = (f32[4,128,2048]{2,1,0:T(8,128)S(1)}, bf16[4,128,2048]{2,1,0:T(8,128)(2,1)S(1)}, f32[1,2048]{1,0:T(1,128)S(1)}) custom-call(f32[128,2048]{1,0:T(8,128)S(1)} %copy-done.8, f32[128,2048]{1,0:T(8,128)S(1)} %collective-permute-done.9.refs_1_, f32[128,2048]{1,0:T(8,128)S(1)} %collective-permute-done.12.refs_2_, ...), custom_call_target="tpu_custom_call" | custom-call | flops 1 | bytes 1 | tf_op jit(solution)/shard_map/mid_back/pallas_call | solution.py:328
  229.4 11.4 %attention_backward.1 = (f32[256,2048]{1,0:T(8,128)}, f32[256,2048]{1,0:T(8,128)}, f32[256,256]{1,0:T(8,128)}, f32[256,256]{1,0:T(8,128)}, bf16[512,512]{1,0:T(8,128)(2,1)}) custom-call(bf16[512,2048]{1,0:T(8,128)(2,1)} %bitcast.77, bf16[512,2048]{1,0:T(8,128)(2,1)} %wo_ref.1, bf16[2048,512]{1,0:T(8,128)(2,1)} %wq_ref.1, ...), custom_call_target="tpu_custom_call" | custom-call | flops 1 | bytes 1 | tf_op jit(solution)/shard_map/attention_backward/pallas_call | solution.py:181
  241.8 6.5 %late_grads.1 = (f32[512,1024]{1,0:T(8,128)S(1)}, f32[1024,512]{1,0:T(8,128)}, f32[1024,512]{1,0:T(8,128)}) custom-call(s32[8]{0:T(128)S(1)} %pad_add_fusion.1.places, bf16[512,512]{1,0:T(8,128)(2,1)S(1)} %copy-done.20, bf16[512,2048]{1,0:T(8,128)(2,1)} %bitcast.78, bf16[512,2048]{1,0:T(8,128)(2,1)} %get-tuple-element.401.normed_ref, ...), custom_call_target="tpu_custom_call" | custom-call | flops 1 | bytes 1 | tf_op jit(solution)/shard_map/late_grads/pallas_call | solution.py:303
  248.4 27.9 %shard_map.213 = (f32[256,1408]{1,0:T(8,128)}, f32[256,1408]{1,0:T(8,128)}, f32[256,1408]{1,0:T(8,128)}, f32[256,1408]{1,0:T(8,128)}, f32[1408,256]{1,0:T(8,128)}, /*index=5*/f32[1408,256]{1,0:T(8,128)}) custom-call(bf16[768,2048]{1,0:T(8,128)(2,1)} %bitcast.83, bf16[768,2048]{1,0:T(8,128)(2,1)} %bitcast.82, bf16[768,512]{1,0:T(8,128)(2,1)} %bitcast.88, ...), custom_call_target="tpu_custom_call" | custom-call | flops 1 | bytes 1 | tf_op jit(solution)/shard_map/pallas_call | solution.py:475
  281.0 9.3 %collective-permute-done.8 = f32[256,2048]{1,0:T(8,128)S(1)} collective-permute-done((f32[256,2048]{1,0:T(8,128)}, f32[256,2048]{1,0:T(8,128)S(1)}, u32[]{:S(2)}, u32[]{:S(2)}) %collective-permute-start.8) | collective-permute-done | bytes 2097184 | tf_op jit(solution)/shard_map/ppermute | solution.py:158
  310.5 27.9 %shard_map.215 = (f32[256,1408]{1,0:T(8,128)}, f32[256,1408]{1,0:T(8,128)}, f32[256,1408]{1,0:T(8,128)}, f32[256,1408]{1,0:T(8,128)}, f32[1408,256]{1,0:T(8,128)}, /*index=5*/f32[1408,256]{1,0:T(8,128)}) custom-call(bf16[768,2048]{1,0:T(8,128)(2,1)} %bitcast.85, bf16[768,2048]{1,0:T(8,128)(2,1)} %bitcast.84, bf16[768,512]{1,0:T(8,128)(2,1)} %bitcast.90, ...), custom_call_target="tpu_custom_call" | custom-call | flops 1 | bytes 1 | tf_op jit(solution)/shard_map/pallas_call | solution.py:475
  345.0 24.7 %collective-permute-done.28 = f32[128,256]{1,0:T(8,128)} collective-permute-done((f32[128,256]{1,0:T(8,128)}, f32[128,256]{1,0:T(8,128)}, u32[]{:S(2)}, u32[]{:S(2)}) %collective-permute-start.28) | collective-permute-done | bytes 131104 | tf_op jit(solution)/shard_map/ppermute | solution.py:158
  395.9 7.8 %in_back.1 = (bf16[4,128,2048]{2,1,0:T(8,128)(2,1)}, f32[1,2048]{1,0:T(1,128)S(1)}) custom-call(s32[4]{0:T(128)S(1)} %get-tuple-element.284.places, f32[128,2048]{1,0:T(8,128)} %slice_add_fusion.1.refs_0_, f32[128,2048]{1,0:T(8,128)} %collective-permute-done.24.refs_1_, f32[128,2048]{1,0:T(8,128)S(1)} %collective-permute-done.33.refs_2_, ...), custom_call_target="tpu_custom_call" | custom-call | flops 1 | bytes 1 | tf_op jit(solution)/shard_map/in_back/pallas_call | solution.py:328
  419.7 6.9 %collective-permute-done.36 = f32[4,1,72,256]{3,2,1,0:T(8,128)} collective-permute-done((f32[4,1,72,256]{3,2,1,0:T(8,128)}, f32[4,1,72,256]{3,2,1,0:T(8,128)}, u32[]{:S(2)}, u32[]{:S(2)}) %collective-permute-start.36) | collective-permute-done | bytes 294944 | tf_op jit(solution)/shard_map/ppermute | solution.py:158
  431.6 8.4 %collective-permute-done.38 = f32[2,72,256]{2,1,0:T(8,128)S(1)} collective-permute-done((f32[2,72,256]{2,1,0:T(8,128)}, f32[2,72,256]{2,1,0:T(8,128)S(1)}, u32[]{:S(2)}, u32[]{:S(2)}) %collective-permute-start.38) | collective-permute-done | bytes 147488 | tf_op jit(solution)/shard_map/ppermute | solution.py:158
  443.9 4.3 collective-permute-done.39
  449.8 5.8 %all-gather.3 = f32[1,256,256]{2,1,0:T(8,128)S(1)} all-gather(f32[1,64,256]{2,1,0:T(8,128)S(1)} %slice.78), channel_id=5, replica_groups=mesh['o'=1,'z'=4,'x'=2,'y'=2,'c'=2] {'y','c'}, dimensions={1}, use_global_device_ids=true | all-gather | bytes 327680 | tf_op jit(solution)/shard_map/all_gather | solution.py:763
  460.0 6.6 %result.1 = bf16[4,128,2048]{2,1,0:T(8,128)(2,1)} custom-call(s32[4]{0:T(128)S(1)} %get-tuple-element.284.places, f32[128,2048]{1,0:T(8,128)} %slice_add_fusion.refs_0_, f32[128,2048]{1,0:T(8,128)} %collective-permute-done.35.refs_1_, f32[128,2048]{1,0:T(8,128)S(1)} %collective-permute-done.42.refs_2_, f32[128,2048]{1,0:T(8,128)S(1)} %collective-permute-done.43.refs_3_, ...), custom_call_target="tpu_custom_call" | custom-call | flops 1 | bytes 1 | tf_op jit(solution)/shard_map/result/pallas_call | solution.py:328
  471.2 4.5 collective-permute-done.45
  (276 shorter events, 168.3 us)
Async XLA Ops:
  7.2 93.2 %all-gather.8.cloned.1.call-start = ((), (), s32[]{:S(2)}) async-start(), calls=%async_computation | async-start | bytes 5242880 | tf_op jit(solution)/shard_map/all_gather | solution.py:566
  16.8 168.4 %all-gather.10.cloned.1.call-start = ((), (), s32[]{:S(2)}) async-start(), calls=%async_computation.1 | async-start | bytes 5242880 | tf_op jit(solution)/shard_map/all_gather | solution.py:588
  38.4 26.4 %collective-permute-start.1 = (f32[128,2048]{1,0:T(8,128)S(1)}, f32[128,2048]{1,0:T(8,128)S(1)}, u32[]{:S(2)}, u32[]{:S(2)}) collective-permute-start(f32[128,2048]{1,0:T(8,128)S(1)} %slice.83), channel_id=1, source_target_pairs={{0,2},{2,0},{1,3},{3,1},{4,6},{6,4},{5,7},{7,5},{8,10},{10,8},{9,1... | collective-permute-start | bytes 3145736 | tf_op jit(solution)/shard_map/ppermute | solution.py:158
  65.2 38.9 %collective-permute-start.2 = (f32[128,2048]{1,0:T(8,128)S(1)}, f32[128,2048]{1,0:T(8,128)S(1)}, u32[]{:S(2)}, u32[]{:S(2)}) collective-permute-start(f32[128,2048]{1,0:T(8,128)S(1)} %get-tuple-element.545.refs_0_.refs_4_), channel_id=1, source_target_pairs={{0,2},{2,0},{1,3},{3,1},{4,6},{6,4},{5,7},{7,5},{8,10},{10,8},{9,1... | collective-permute-start | bytes 3145736 | tf_op jit(solution)/shard_map/ppermute | solution.py:158
  67.0 38.4 %collective-permute-start.3 = (f32[128,2048]{1,0:T(8,128)S(1)}, f32[128,2048]{1,0:T(8,128)S(1)}, u32[]{:S(2)}, u32[]{:S(2)}) collective-permute-start(f32[128,2048]{1,0:T(8,128)S(1)} %get-tuple-element.545.refs_0_.refs_4_), channel_id=1, source_target_pairs={{0,1},{1,0},{2,3},{3,2},{4,5},{5,4},{6,7},{7,6},{8,9},{9,8},{10,11... | collective-permute-start | bytes 3145736 | tf_op jit(solution)/shard_map/ppermute | solution.py:158
  68.1 211.9 %all-gather.12.cloned.1.call-start = ((), (), s32[]{:S(2)}) async-start(), calls=%async_computation.2 | async-start | bytes 5242880 | tf_op jit(solution)/shard_map/all_gather | solution.py:593
  115.5 25.2 %collective-permute-start.5 = (f32[128,2048]{1,0:T(8,128)S(1)}, f32[128,2048]{1,0:T(8,128)S(1)}, u32[]{:S(2)}, u32[]{:S(2)}) collective-permute-start(f32[128,2048]{1,0:T(8,128)S(1)} %copy-done.50), channel_id=1, source_target_pairs={{0,2},{2,0},{1,3},{3,1},{4,6},{6,4},{5,7},{7,5},{8,10},{10,8},{9,1... | collective-permute-start | bytes 3145736 | tf_op jit(solution)/shard_map/ppermute | solution.py:158
  158.8 25.3 %collective-permute-start.7 = (f32[128,2048]{1,0:T(8,128)S(1)}, f32[128,2048]{1,0:T(8,128)S(1)}, u32[]{:S(2)}, u32[]{:S(2)}) collective-permute-start(f32[128,2048]{1,0:T(8,128)S(1)} %slice.84), channel_id=1, source_target_pairs={{0,2},{2,0},{1,3},{3,1},{4,6},{6,4},{5,7},{7,5},{8,10},{10,8},{9,1... | collective-permute-start | bytes 3145736 | tf_op jit(solution)/shard_map/ppermute | solution.py:158
  185.8 25.3 %collective-permute-start.9 = (f32[128,2048]{1,0:T(8,128)}, f32[128,2048]{1,0:T(8,128)S(1)}, u32[]{:S(2)}, u32[]{:S(2)}) collective-permute-start(f32[128,2048]{1,0:T(8,128)} %slice_add_fusion.2.refs_0_), channel_id=1, source_target_pairs={{0,2},{2,0},{1,3},{3,1},{4,6},{6,4},{5,7},{7,5},{8,10},{10,8},{9,1... | collective-permute-start | bytes 3145736 | tf_op jit(solution)/shard_map/ppermute | solution.py:158
  225.0 51.3 %collective-permute-start.16 = (f32[512,1024]{1,0:T(8,128)}, f32[512,1024]{1,0:T(8,128)}, u32[]{:S(2)}, u32[]{:S(2)}) collective-permute-start(f32[512,1024]{1,0:T(8,128)} %out_grad.1), channel_id=1, source_target_pairs={{0,4},{4,0},{1,5},{5,1},{2,6},{6,2},{3,7},{7,3},{8,12},{12,8},{9,1... | collective-permute-start | bytes 6291464 | tf_op jit(solution)/shard_map/ppermute | solution.py:158
  226.5 49.8 %collective-permute-start.18 = (f32[128,2048]{1,0:T(8,128)}, f32[128,2048]{1,0:T(8,128)}, u32[]{:S(2)}, u32[]{:S(2)}) collective-permute-start(f32[128,2048]{1,0:T(8,128)} %get-tuple-element.406), channel_id=1, source_target_pairs={{0,2},{2,0},{1,3},{3,1},{4,6},{6,4},{5,7},{7,5},{8,10},{10,8},{9,1... | collective-permute-start | bytes 3145736 | tf_op jit(solution)/shard_map/ppermute | solution.py:158
  228.0 48.3 %collective-permute-start.17 = (f32[128,2048]{1,0:T(8,128)}, f32[128,2048]{1,0:T(8,128)}, u32[]{:S(2)}, u32[]{:S(2)}) collective-permute-start(f32[128,2048]{1,0:T(8,128)} %get-tuple-element.405), channel_id=1, source_target_pairs={{0,2},{2,0},{1,3},{3,1},{4,6},{6,4},{5,7},{7,5},{8,10},{10,8},{9,1... | collective-permute-start | bytes 3145736 | tf_op jit(solution)/shard_map/ppermute | solution.py:158
  280.0 26.6 %collective-permute-start.20 = (f32[4,128,2048]{2,1,0:T(8,128)}, f32[4,128,2048]{2,1,0:T(8,128)S(1)}, u32[]{:S(2)}, u32[]{:S(2)}) collective-permute-start(f32[4,128,2048]{2,1,0:T(8,128)} %bitcast.68), channel_id=1, source_target_pairs={{0,1},{1,0},{2,3},{3,2},{4,5},{5,4},{6,7},{7,6},{8,9},{9,8},{10,11... | collective-permute-start | bytes 12582920 | tf_op jit(solution)/shard_map/ppermute | solution.py:158
  296.6 41.8 %collective-permute-start.19 = (f32[128,2048]{1,0:T(8,128)}, f32[128,2048]{1,0:T(8,128)}, u32[]{:S(2)}, u32[]{:S(2)}) collective-permute-start(f32[128,2048]{1,0:T(8,128)} %slice.86), channel_id=1, source_target_pairs={{0,2},{2,0},{1,3},{3,1},{4,6},{6,4},{5,7},{7,5},{8,10},{10,8},{9,1... | collective-permute-start | bytes 3145736 | tf_op jit(solution)/shard_map/ppermute | solution.py:158
  298.1 76.7 %collective-permute-start.26 = (f32[1024,512]{1,0:T(8,128)}, f32[1024,512]{1,0:T(8,128)}, u32[]{:S(2)}, u32[]{:S(2)}) collective-permute-start(f32[1024,512]{1,0:T(8,128)} %get-tuple-element.476), channel_id=1, source_target_pairs={{0,4},{4,0},{1,5},{5,1},{2,6},{6,2},{3,7},{7,3},{8,12},{12,8},{9,1... | collective-permute-start | bytes 6291464 | tf_op jit(solution)/shard_map/ppermute | solution.py:158
  298.7 72.7 %collective-permute-start.27 = (f32[512,512]{1,0:T(8,128)}, f32[512,512]{1,0:T(8,128)}, u32[]{:S(2)}, u32[]{:S(2)}) collective-permute-start(f32[512,512]{1,0:T(8,128)} %get-tuple-element.477), channel_id=1, source_target_pairs={{0,16},{8,24},{16,0},{24,8},{1,17},{9,25},{17,1},{25,9},{2,18},{10... | collective-permute-start | bytes 3145736 | tf_op jit(solution)/shard_map/ppermute | solution.py:158
  338.4 40.6 %collective-permute-start.25 = (f32[256,1408]{1,0:T(8,128)}, f32[256,1408]{1,0:T(8,128)}, u32[]{:S(2)}, u32[]{:S(2)}) collective-permute-start(f32[256,1408]{1,0:T(8,128)} %get-tuple-element.473), channel_id=1, source_target_pairs={{0,4},{4,0},{1,5},{5,1},{2,6},{6,2},{3,7},{7,3},{8,12},{12,8},{9,1... | collective-permute-start | bytes 4325384 | tf_op jit(solution)/shard_map/ppermute | solution.py:158
  342.3 39.3 %collective-permute-start.24 = (f32[128,2048]{1,0:T(8,128)}, f32[128,2048]{1,0:T(8,128)}, u32[]{:S(2)}, u32[]{:S(2)}) collective-permute-start(f32[128,2048]{1,0:T(8,128)} %slice_add_fusion.1.refs_0_), channel_id=1, source_target_pairs={{0,2},{2,0},{1,3},{3,1},{4,6},{6,4},{5,7},{7,5},{8,10},{10,8},{9,1... | collective-permute-start | bytes 3145736 | tf_op jit(solution)/shard_map/ppermute | solution.py:158
  343.5 26.2 %collective-permute-start.28 = (f32[128,256]{1,0:T(8,128)}, f32[128,256]{1,0:T(8,128)}, u32[]{:S(2)}, u32[]{:S(2)}) collective-permute-start(f32[128,256]{1,0:T(8,128)} %slice.87), channel_id=1, source_target_pairs={{0,2},{2,0},{1,3},{3,1},{4,6},{6,4},{5,7},{7,5},{8,10},{10,8},{9,1... | collective-permute-start | bytes 393224 | tf_op jit(solution)/shard_map/ppermute | solution.py:158
  386.8 61.5 %collective-permute-start.41 = (f32[512,512]{1,0:T(8,128)}, f32[512,512]{1,0:T(8,128)}, u32[]{:S(2)}, u32[]{:S(2)}) collective-permute-start(f32[512,512]{1,0:T(8,128)} %get-tuple-element.534), channel_id=1, source_target_pairs={{0,16},{8,24},{16,0},{24,8},{1,17},{9,25},{17,1},{25,9},{2,18},{10... | collective-permute-start | bytes 3145736 | tf_op jit(solution)/shard_map/ppermute | solution.py:158
  388.8 51.3 %collective-permute-start.40 = (f32[256,1408]{1,0:T(8,128)}, f32[256,1408]{1,0:T(8,128)}, u32[]{:S(2)}, u32[]{:S(2)}) collective-permute-start(f32[256,1408]{1,0:T(8,128)} %get-tuple-element.529), channel_id=1, source_target_pairs={{0,4},{4,0},{1,5},{5,1},{2,6},{6,2},{3,7},{7,3},{8,12},{12,8},{9,1... | collective-permute-start | bytes 4325384 | tf_op jit(solution)/shard_map/ppermute | solution.py:158
  389.9 25.4 %collective-permute-start.29 = (f32[128,2048]{1,0:T(8,128)}, f32[128,2048]{1,0:T(8,128)}, u32[]{:S(2)}, u32[]{:S(2)}) collective-permute-start(f32[128,2048]{1,0:T(8,128)} %slice.85), channel_id=1, source_target_pairs={{0,2},{2,0},{1,3},{3,1},{4,6},{6,4},{5,7},{7,5},{8,10},{10,8},{9,1... | collective-permute-start | bytes 3145736 | tf_op jit(solution)/shard_map/ppermute | solution.py:158
  419.1 36.5 %collective-permute-start.35 = (f32[128,2048]{1,0:T(8,128)}, f32[128,2048]{1,0:T(8,128)}, u32[]{:S(2)}, u32[]{:S(2)}) collective-permute-start(f32[128,2048]{1,0:T(8,128)} %slice_add_fusion.refs_0_), channel_id=1, source_target_pairs={{0,2},{2,0},{1,3},{3,1},{4,6},{6,4},{5,7},{7,5},{8,10},{10,8},{9,1... | collective-permute-start | bytes 3145736 | tf_op jit(solution)/shard_map/ppermute | solution.py:158
  443.3 32.4 %collective-permute-start.45 = (f32[1408,256]{1,0:T(8,128)S(1)}, f32[1408,256]{1,0:T(8,128)S(1)}, u32[]{:S(2)}, u32[]{:S(2)}) collective-permute-start(f32[1408,256]{1,0:T(8,128)S(1)} %copy-done.54), channel_id=1, source_target_pairs={{0,4},{4,0},{1,5},{5,1},{2,6},{6,2},{3,7},{7,3},{8,12},{12,8},{9,1... | collective-permute-start | bytes 4325384 | tf_op jit(solution)/shard_map/ppermute | solution.py:158
  (80 other events, 515.3 us)
Sparse Core Ops, SparseCore 0:
  16.9 83.4 all-gather.7
  102.0 79.2 all-gather.9
  185.9 79.3 all-gather.11

commit v4 on v3

--- a/solution.py
+++ b/solution.py
@@ -100,26 +100,33 @@
     return lax.rsqrt(jnp.mean(block * block, axis=-1, keepdims=True) + epsilon)
 
 
-def pack_z_kernel(places, *refs):
-    blocks, (scale, out, picked) = refs[:6], refs[6:]
+def pack_kernel(n, places, *refs):
+    blocks, (scale, out, picked) = refs[:n], refs[n:]
     width = picked.shape[2] // 2
-    for j in range(6):
+    for j in range(n):
         out[j] = (blocks[j][0] * scale[...]).astype(bf16)
         for part in range(2):
             at = pl.ds(pl.multiple_of(places[part] * width, width), width)
             picked[j, :, part * width : (part + 1) * width] = (blocks[j][0, :, at] * scale[:, at]).astype(bf16)
 
 
-def pack_z(own, far, scale, places, rows, tile=32):
-    _, count, width = own.shape
-    specs = [pl.BlockSpec((1, tile, width), lambda t, p, k=k: (p[2 + k], t, 0)) for k in range(GROUP - 1)]
-    n = 2 * (GROUP - 1)
+def pack(blocks, scale, places, rows, tile=32):
+    count, width = blocks[0].shape[1:]
+    args, specs = [], []
+    for a in blocks:
+        for k in range(GROUP - 1 if a.shape[0] == GROUP else a.shape[0]):
+            args.append(a)
+            if a.shape[0] == GROUP:
+                specs.append(pl.BlockSpec((1, tile, width), lambda t, p, k=k: (p[2 + k], t, 0)))
+            else:
+                specs.append(pl.BlockSpec((1, tile, width), lambda t, p, k=k: (k, t, 0)))
+    n = len(args)
     out, picked = pl.pallas_call(
-        pack_z_kernel,
+        functools.partial(pack_kernel, n),
         grid_spec=pltpu.PrefetchScalarGridSpec(
             num_scalar_prefetch=1,
             grid=(count // tile,),
-            in_specs=specs + specs + [pl.BlockSpec((1, width), lambda t, p: (0, 0))],
+            in_specs=specs + [pl.BlockSpec((1, width), lambda t, p: (0, 0))],
             out_specs=[
                 pl.BlockSpec((n, tile, width), lambda t, p: (0, t, 0)),
                 pl.BlockSpec((n, tile, 2 * rows), lambda t, p: (0, t, 0)),
@@ -129,10 +136,10 @@
             jax.ShapeDtypeStruct((n, count, width), bf16),
             jax.ShapeDtypeStruct((n, count, 2 * rows), bf16),
         ],
-        name="pack_z",
+        name="pack",
         compiler_params=pltpu.CompilerParams(vmem_limit_bytes=32 * 2**20),
         cost_estimate=light,
-    )(places, *[own] * (GROUP - 1), *[far] * (GROUP - 1), scale.reshape(1, width))
+    )(places, *args, scale.reshape(1, width))
     return out.reshape(n * count, width), picked.reshape(n * count, 2 * rows)
 
 
@@ -390,41 +397,6 @@
     left, right, (out,) = refs[:4], refs[4:8], refs[8:]
     for j in range(4):
         out[places[j]] = (left[j][...] + right[j][...]).astype(bf16)
-
-
-def pack_kernel(n, places, *refs):
-    blocks, scale, out, picked = refs[:n], refs[n], refs[n + 1], refs[n + 2]
-    width = picked.shape[2] // 2
-    for j in range(n):
-        out[j] = (blocks[j][...] * scale[...]).astype(bf16)
-        for part in range(2):
-            at = pl.ds(pl.multiple_of(places[part] * width, width), width)
-            picked[j, :, part * width : (part + 1) * width] = (blocks[j][:, at] * scale[:, at]).astype(bf16)
-
-
-def pack(blocks, scale, places, rows, tile=32):
-    n = len(blocks)
-    count, width = blocks[0].shape
-    block = pl.BlockSpec((tile, width), lambda t, places: (t, 0))
-    out, picked = pl.pallas_call(
-        functools.partial(pack_kernel, n),
-        grid_spec=pltpu.PrefetchScalarGridSpec(
-            num_scalar_prefetch=1,
-            grid=(count // tile,),
-            in_specs=[block] * n + [pl.BlockSpec((1, width), lambda t, places: (0, 0))],
-            out_specs=[
-                pl.BlockSpec((n, tile, width), lambda t, places: (0, t, 0)),
-                pl.BlockSpec((n, tile, 2 * rows), lambda t, places: (0, t, 0)),
-            ],
-        ),
-        out_shape=[
-            jax.ShapeDtypeStruct((n, count, width), bf16),
-            jax.ShapeDtypeStruct((n, count, 2 * rows), bf16),
-        ],
-        compiler_params=pltpu.CompilerParams(vmem_limit_bytes=32 * 2**20),
-        cost_estimate=light,
-    )(places, *blocks, scale.reshape(1, width))
-    return out.reshape(n * count, width), picked.reshape(n * count, 2 * rows)
 
 
 def ffn_kernel(own, has_prev, *refs):
@@ -542,15 +514,10 @@
                 taken.append(lax.dynamic_slice_in_dim(part, (2 * z + which) * rows, rows, 1))
         return jnp.concatenate(taken, axis=1)
 
-    def packed_z(own, far, gain):
-        if n_outer == 1:
-            return run(lambda own, far: pack_z(own, far, gain, places, rows), own, far)
-        return packed(remote(own), remote(far), gain)
-
-    def packed(blocks, far, gain):
-        blocks = [*blocks, *far]
+    def packed(blocks, gain):
         if n_outer == 1:
             return run(lambda *blocks: pack(blocks, gain, places, rows), *blocks)
+        blocks = [b for a in blocks for b in (remote(a) if a.shape[0] == GROUP else list(a))]
         whole = run(lambda *blocks: (jnp.concatenate(blocks, axis=0) * (gain * one)).astype(bf16), *blocks)
         return whole, columns(whole)
 
@@ -588,7 +555,6 @@
     nm_z_own = lax.all_gather(scaled_own, "z", axis=0, tiled=False)
     other = swap(own, "y")
     far_own = swap(own, "c")
-    go_remote = run(remote, go_z)
     scaled_other = run(scaled, other)
     nm_z_other = lax.all_gather(scaled_other, "z", axis=0, tiled=False)
     far_other = swap(other, "c")
@@ -603,29 +569,32 @@
     )
     normed_mid = normed_mid.reshape(seq_len, width)
     nm_own_columns = nm_own_columns[0].reshape(seq_len, 2 * rows) if n_outer == 1 else columns(normed_mid)
-    go_other = [swap(go_remote[0], "y")]
+    go_z = wait(go_z)
+    go_first = run(lambda a: lax.dynamic_index_in_dim(a, others[0], 0), go_z)
+    go_first = swap(go_first, "y")
+    go_far = swap(go_z, "c")
     *sums, mixed, grad_gate, grad_up = run(
         lambda *args: ffn(*args, *weights, own=True),
         normed_mid, grad_down_in, nm_own_columns, go_own_columns,
     )
-    go_other[0] = wait(go_other[0])
+    go_first = wait(go_first)
     mid_kept, mid_sent = run(
         lambda *args: pair_dots("mid_part", args[:2], args[2:], True), grad_gate, grad_up, w_gate, w_up
     )
     mid_sent = swap(mid_sent, "c")
     kept = run(jnp.add, mid_kept, mid_sent)
     received = swap(kept[quarter:], "y")
+    go_rest = run(lambda a: jnp.concatenate([lax.dynamic_index_in_dim(a, k, 0) for k in others[1:]], axis=0), go_z)
+    go, go_columns = packed([go_z, go_far], ones)
     own = run(add_y, kept, received)
     other = swap(own, "y")
+    far_own = swap(own, "c")
+    down_kept, down_sent = run(lambda *args: pair_dots("down_part", args[:1], args[1:], False), mixed, w_down)
     nm_z_own = wait(nm_z_own)
-    far_own = swap(own, "c")
-    go_far, nm_far = swap(go_z, "c"), swap(nm_z_own, "c")
-    down_kept, down_sent = run(lambda *args: pair_dots("down_part", args[:1], args[1:], False), mixed, w_down)
+    nm_far = swap(nm_z_own, "c")
     down_sent = swap(down_sent, "c")
-    go, go_columns = packed_z(go_z, go_far, ones)
-    nm, nm_columns = packed_z(nm_z_own, nm_far, norm_mid)
     other = wait(other)
-    go_other += [order.move(block, "y", [(0, 1), (1, 0)], queue=False) for block in go_remote[1:]]
+    go_rest = order.move(go_rest, "y", [(0, 1), (1, 0)], queue=False)
     grad_mid = [own, other, far_own, swap(other, "c")]
     grad_hidden, grad_attention, grad_norm_mid = run(
         lambda *args: rows_call(
@@ -646,6 +615,8 @@
     else:
         out_sent = run(dot_tn, attended, by_x(grad_attention, 1 - x, rows))
     out_sent = swap(out_sent, "x")
+    nm, nm_columns = packed([nm_z_own, nm_far], norm_mid)
+    down_kept = run(jnp.add, down_kept, down_sent)
     kept, sent, kv_kept, kv_sent, grad_query = run(
         lambda *args: call(
             functools.partial(backward_kernel, scale),
@@ -674,40 +645,33 @@
     query_sent = order.move(query_sent, "x", [(0, 1), (1, 0)], queue=False)
 
     sums = run(wgrads, nm, go, nm_columns, go_columns, *sums)
-    go_other[1:] = [wait(block) for block in go_other[1:]]
+    go_rest = wait(go_rest)
     out_half = run(jnp.add, out_kept, out_sent)
-    if n_outer == 1:
-        out_kept, out_sent = run(lambda a: split(a, 1, z // 2), out_half)
-        out_sent = order.pair_z(out_sent, 2)
-    nm_z_other = wait(nm_z_other)
-    go_far = [swap(block, "c") for block in go_other]
-    nm_far = swap(nm_z_other, "c")
+    kv_kept = run(jnp.add, kv_kept, kv_sent)
+    kv_received = order.move(kv_kept[quarter:], "y", [(0, 1), (1, 0)], queue=False)
     kept = run(jnp.add, kept, sent)
     received = swap(kept[quarter:], "y")
-    kv_kept = run(jnp.add, kv_kept, kv_sent)
-    kv_received = order.move(kv_kept[quarter:], "y", [(0, 1), (1, 0)], queue=False)
-    down_kept = run(jnp.add, down_kept, down_sent)
-    go, go_columns = packed(go_other, go_far, ones)
-    nm, nm_columns = packed_z(nm_z_other, nm_far, norm_mid)
+    down_received = order.move(down_kept[quarter:], "y", [(0, 1), (1, 0)], queue=False)
+    nm_z_other = wait(nm_z_other)
+    nm_far = swap(nm_z_other, "c")
+    go_far = [swap(go_first, "c"), swap(go_rest, "c")]
+    grad_w_out = lax.psum_scatter(out_half, ("o", "z"), scatter_dimension=1, tiled=True)
+    go, go_columns = packed([go_first, go_rest, *go_far], ones)
+    nm, nm_columns = packed([nm_z_other, nm_far], norm_mid)
     sums = run(wgrads, nm, go, nm_columns, go_columns, *sums)
     gate_sent = swap(sums[0], "x")
     summed_own = run(add_y, kept, received)
-    summed_other = swap(summed_own, "y")
+    summed_other = order.move(summed_own, "y", [(0, 1), (1, 0)], queue=False)
     kv_own = run(add_y, kv_kept, kv_received)
     kv_other = order.move(kv_own, "y", [(0, 1), (1, 0)], queue=False)
-    if n_outer == 1:
-        out_half = run(jnp.add, out_kept, out_sent)
-        out_kept, out_sent = run(lambda a: split(a, 1, z % 2), out_half)
-        out_sent = order.pair_z(out_sent, 1)
+    down_own = run(add_y, down_kept, down_received)
+    down_other = order.move(down_own, "y", [(0, 1), (1, 0)], queue=False)
     query_half = run(jnp.add, query_kept, query_sent)
-    if n_outer == 1:
-        query_kept, query_sent = run(lambda a: split(a, 0, z // 2), query_half)
-        query_sent = order.pair_z(query_sent, 2)
+    grad_w_query = lax.psum_scatter(query_half, ("o", "z"), scatter_dimension=0, tiled=True)
+    up_sent = order.move(sums[2], "x", [(0, 1), (1, 0)], queue=False)
     grad_w_gate = run(jnp.add, sums[1], gate_sent)
-    up_sent = swap(sums[2], "x")
-
     summed_other = wait(summed_other)
-    down_received = swap(down_kept[quarter:], "y")
+
     far = [swap(a, "c") for a in (kv_own, kv_other, summed_own, summed_other)]
 
     def key_value(*parts):
@@ -740,41 +704,28 @@
 
     small, small_sent = run(small_sums, grad_key, grad_value, grad_norm_in, grad_norm_mid)
     small_sent = order.move(small_sent, "x", [(0, 1), (1, 0)], queue=False)
-    down_own = run(add_y, down_kept, down_received)
-    down_other = swap(down_own, "y")
+    down_other = wait(down_other)
     small = run(jnp.add, small, small_sent).reshape(n_dp // 2, -1, 2 * head)
+    last_sent = order.move(sums[4], "x", [(0, 1), (1, 0)], queue=False)
+    grad_w_up = run(jnp.add, sums[3], up_sent)
+    down = [down_own, down_other, swap(down_own, "c"), swap(down_other, "c")]
+    (result,) = run(
+        lambda *args: rows_call(
+            add_kernel, "result", [args[:4], args[4:]], [], [], [(width, bf16)], 0, prefetch=(quarters,)
+        ),
+        *down, *hidden,
+    )
     if n_outer == 1:
-        grad_w_out = run(jnp.add, out_kept, out_sent)
         small, small_sent = run(lambda a: split(a, 0, z // 2), small)
         small_sent = order.move(small_sent, "z", [(i, i ^ 2) for i in range(GROUP)], queue=False)
         small = run(jnp.add, small, small_sent)
         small, small_sent = run(lambda a: split(a, 0, z % 2), small)
         small_sent = order.move(small_sent, "z", [(i, i ^ 1) for i in range(GROUP)], queue=False)
+        small = run(jnp.add, small, small_sent)
     else:
         small = lax.psum_scatter(small, ("o", "z"), scatter_dimension=0, tiled=True)
-        grad_w_out = lax.psum_scatter(out_half, ("o", "z"), scatter_dimension=1, tiled=True)
-    grad_w_up = run(jnp.add, sums[3], up_sent)
-    last_sent = swap(sums[4], "x")
-    if n_outer == 1:
-        small = run(jnp.add, small, small_sent)
-        query_half = run(jnp.add, query_kept, query_sent)
-        query_kept, query_sent = run(lambda a: split(a, 0, z % 2), query_half)
-        query_sent = order.pair_z(query_sent, 1)
     kv = run(lambda a: lax.all_gather(a[0, :piece], ("y", "c"), axis=0, tiled=True), small)
     out_norm_in, out_norm_mid = small[0, piece, :rows], small[0, piece + 1, :rows]
-
-    down_other = wait(down_other)
-    down = [down_own, down_other, swap(down_own, "c"), swap(down_other, "c")]
-    (result,) = run(
-        lambda *args: rows_call(
-            add_kernel, "result", [args[:4], args[4:]], [], [], [(width, bf16)], 0, prefetch=(quarters,)
-        ),
-        *down, *hidden,
-    )
-    if n_outer == 1:
-        grad_w_query = run(jnp.add, query_kept, query_sent)
-    else:
-        grad_w_query = lax.psum_scatter(query_half, ("o", "z"), scatter_dimension=0, tiled=True)
     grad_w_down = run(jnp.add, sums[5], last_sent)
     if n_outer > 1:
         grad_w_down = lax.psum_scatter(grad_w_down, "o", scatter_dimension=1, tiled=True)

time: 492 us -> 482 us (0.980)
  waiting for transfers between devices: 171 us -> 159 us
    all_gather x1, waiting for transfers between devices: 31.9 us -> 0.01 us  [shards(): go_z = lax.all_gather(go_quarter, 'z', axis=0, tiled=False)]
    ppermute x46 -> x40, waiting for transfers between devices: 139 us -> 158 us  [move(): a = lax.ppermute(a, axis, pairs)]
    pallas_call x1 -> x4, Pallas kernels: 3.51 us -> 14.2 us  [pack(): pl.pallas_call(functools.partial(pack_kernel, n), grid_spec=pltpu.Prefetc...]
    pallas_call x3 -> x0, Pallas kernels: 10.4 us -> none  [pack_z(): pl.pallas_call(pack_z_kernel, grid_spec=pltpu.PrefetchScalarGridSpec(num_...]
    unnamed x110 -> x112, local copies, waits for them, and re-layouts: 27 us -> 33.2 us
    add x17 -> x13, other arithmetic: 24.4 us -> 22.8 us  [run(): outs = f(*args)]
    ppermute x46 -> x40, starting transfers between devices: 31.4 us -> 31.9 us  [move(): a = lax.ppermute(a, axis, pairs)]
  transfers between devices with their start and end apart: 49 -> 45, of which waited for: 22 -> 19; matrix products, arithmetic and copies ran while one was open for 13% -> 13% of each run, Pallas kernels for 34% -> 35%
where the time goes in v4:
time: 482 us; the launch traced here: 474 us
  Pallas kernels  168 us (35%)
  waiting for transfers between devices  159 us (33%)
  local copies, waits for them, and re-layouts  50.5 us (10%)
  other arithmetic  40.9 us (8%)
  starting transfers between devices  32.7 us (7%)
  between operations  15.2 us (3%)
  blocking collectives  5.79 us (1%)
    ppermute x40, waiting for transfers between devices, move(): a = lax.ppermute(a, axis, pairs)  158 us
    pallas_call x3, Pallas kernels, ffn(): pl.pallas_call(functools.partial(ffn_kernel, own, bool(previous)), grid=(...  77.1 us
    unnamed x112, local copies, waits for them, and re-layouts  33.2 us
    ppermute x40, starting transfers between devices, move(): a = lax.ppermute(a, axis, pairs)  31.9 us
    pallas_call x4, Pallas kernels, rows_call(): pl.pallas_call(kernel, grid_spec=pltpu.PrefetchScalarGridSpec(num_scalar_...  25.9 us
    pallas_call x2, Pallas kernels, call(): pl.pallas_call(kernel, out_shape=outs, name=name, compiler_params=pltpu.C...  23.4 us
    add x13, other arithmetic, run(): outs = f(*args)  22.8 us
    pallas_call x2, Pallas kernels, pair_dots(): pl.pallas_call(functools.partial(pair_kernel, transposed), grid=(width //...  16.2 us
  transfers between devices with their start and end apart: 45, of which 19 were waited for; matrix products, arithmetic and copies ran while one was open for 13% of the time, Pallas kernels for 35%

profile of v4, /device:TPU:0, one launch (start us, length us, event | category | flops | bytes accessed | tf_op | source)
XLA Modules:
  0.0 473.9 jit_solution(10934007967686819472)
XLA Ops:
  19.7 12.0 %attention_forward.1 = (f32[256,2048]{1,0:T(8,128)}, f32[256,2048]{1,0:T(8,128)}, bf16[512,2048]{1,0:T(8,128)(2,1)}, bf16[512,512]{1,0:T(8,128)(2,1)}, bf16[512,...) custom-call(bf16[512,2048]{1,0:T(8,128)(2,1)} %copy-done.4, f32[1,2048]{1,0:T(1,128)} %bitcast.91, ...), custom_call_target="tpu_custom_call" | custom-call | flops 1 | bytes 1 | tf_op jit(solution)/shard_map/attention_forward/pallas_call | solution.py:188
  42.4 22.4 %collective-permute-done.1 = f32[128,2048]{1,0:T(8,128)S(1)} collective-permute-done((f32[128,2048]{1,0:T(8,128)S(1)}, f32[128,2048]{1,0:T(8,128)S(1)}, u32[]{:S(2)}, u32[]{:S(2)}) %collective-permute-start.1) | collective-permute-done | bytes 1048608 | tf_op jit(solution)/shard_map/ppermute | solution.py:165
  68.3 21.7 %collective-permute-done.2.refs_1_.refs_5_ = f32[128,2048]{1,0:T(8,128)S(1)} collective-permute-done((f32[128,2048]{1,0:T(8,128)S(1)}, f32[128,2048]{1,0:T(8,128)S(1)}, u32[]{:S(2)}, u32[]{:S(2)}) %collective-permute-start.2) | collective-permute-done | bytes 1048608 | tf_op jit(solution)/shard_map/ppermute | solution.py:165
  94.1 5.2 %mid_norm.1 = (bf16[4,128,2048]{2,1,0:T(8,128)(2,1)S(1)}, bf16[4,128,512]{2,1,0:T(8,128)(2,1)S(1)}) custom-call(s32[5]{0:T(128)S(1)} %stack.43.places, f32[128,2048]{1,0:T(8,128)S(1)} %get-tuple-element.510.refs_0_.refs_4_, f32[128,2048]{1,0:T(8,128)S(1)} %collective-permute-done.2.refs_1_.refs_5_, f32[128,2048]{1,0:T(8,128)S(1)} %collective-permute-done.3.refs_2_.refs_6_, ...), custom_call_target="tpu_custom_call" | custom-call | flops 1 | bytes 1 | tf_op jit(solution)/shard_map/mid_norm/pallas_call | solution.py:335
  104.3 20.8 %shard_map.212 = (f32[256,1408]{1,0:T(8,128)}, f32[256,1408]{1,0:T(8,128)}, f32[256,1408]{1,0:T(8,128)}, f32[256,1408]{1,0:T(8,128)}, f32[1408,256]{1,0:T(8,128)...) custom-call(bf16[512,2048]{1,0:T(8,128)(2,1)} %bitcast.81, ...), custom_call_target="tpu_custom_call" | custom-call | flops 1 | bytes 1 | tf_op jit(solution)/shard_map/pallas_call | solution.py:447
  131.2 10.2 %mid_part.1 = (f32[256,2048]{1,0:T(8,128)S(1)}, f32[256,2048]{1,0:T(8,128)}) custom-call(bf16[512,1408]{1,0:T(8,128)(2,1)S(1)} %copy-done.22, bf16[512,1408]{1,0:T(8,128)(2,1)S(1)} %copy-done.23, bf16[2048,1408]{1,0:T(8,128)(2,1)} %refs_4_.5, bf16[2048,1408]{1,0:T(8,128)(2,1)} %refs_5_.5), custom_call_target="tpu_custom_call" | custom-call | flops 1 | bytes 1 | tf_op jit(solution)/shard_map/mid_part/pallas_call | solution.py:276
  141.4 4.4 collective-permute-done.6
  159.9 14.1 %collective-permute-done.7 = f32[128,2048]{1,0:T(8,128)} collective-permute-done((f32[128,2048]{1,0:T(8,128)}, f32[128,2048]{1,0:T(8,128)}, u32[]{:S(2)}, u32[]{:S(2)}) %collective-permute-start.7) | collective-permute-done | bytes 1048608 | tf_op jit(solution)/shard_map/ppermute | solution.py:165
  176.4 6.0 %down_part.1 = (f32[256,2048]{1,0:T(8,128)S(1)}, f32[256,2048]{1,0:T(8,128)S(1)}) custom-call(bf16[512,1408]{1,0:T(8,128)(2,1)S(1)} %copy-done.24, bf16[1408,2048]{1,0:T(8,128)(2,1)} %refs_6_.5), custom_call_target="tpu_custom_call" | custom-call | flops 1 | bytes 1 | tf_op jit(solution)/shard_map/down_part/pallas_call | solution.py:276
  187.6 23.9 %collective-permute-done.11.refs_1_ = f32[128,2048]{1,0:T(8,128)S(1)} collective-permute-done((f32[128,2048]{1,0:T(8,128)}, f32[128,2048]{1,0:T(8,128)S(1)}, u32[]{:S(2)}, u32[]{:S(2)}) %collective-permute-start.11) | collective-permute-done | bytes 1048608 | tf_op jit(solution)/shard_map/ppermute | solution.py:165
  216.9 5.9 %mid_back.1 = (f32[4,128,2048]{2,1,0:T(8,128)S(1)}, bf16[4,128,2048]{2,1,0:T(8,128)(2,1)S(1)}, f32[1,2048]{1,0:T(1,128)S(1)}) custom-call(f32[128,2048]{1,0:T(8,128)S(1)} %copy-done.8, f32[128,2048]{1,0:T(8,128)S(1)} %collective-permute-done.11.refs_1_, f32[128,2048]{1,0:T(8,128)S(1)} %collective-permute-done.12.refs_2_, ...), custom_call_target="tpu_custom_call" | custom-call | flops 1 | bytes 1 | tf_op jit(solution)/shard_map/mid_back/pallas_call | solution.py:335
  235.8 11.4 %attention_backward.1 = (f32[256,2048]{1,0:T(8,128)}, f32[256,2048]{1,0:T(8,128)}, f32[256,256]{1,0:T(8,128)}, f32[256,256]{1,0:T(8,128)}, bf16[512,512]{1,0:T(8,128)(2,1)}) custom-call(bf16[512,2048]{1,0:T(8,128)(2,1)} %bitcast.72, bf16[512,2048]{1,0:T(8,128)(2,1)} %wo_ref.1, bf16[2048,512]{1,0:T(8,128)(2,1)} %wq_ref.1, ...), custom_call_target="tpu_custom_call" | custom-call | flops 1 | bytes 1 | tf_op jit(solution)/shard_map/attention_backward/pallas_call | solution.py:188
  248.8 6.0 %late_grads.1 = (f32[512,1024]{1,0:T(8,128)S(1)}, f32[1024,512]{1,0:T(8,128)S(1)}, f32[1024,512]{1,0:T(8,128)}) custom-call(s32[8]{0:T(128)S(1)} %pad_add_fusion.1.places, bf16[512,512]{1,0:T(8,128)(2,1)S(1)} %copy-done.20, bf16[512,2048]{1,0:T(8,128)(2,1)} %bitcast.73, bf16[512,2048]{1,0:T(8,128)(2,1)} %get-tuple-element.390.normed_ref, ...), custom_call_target="tpu_custom_call" | custom-call | flops 1 | bytes 1 | tf_op jit(solution)/shard_map/late_grads/pallas_call | solution.py:310
  254.8 28.4 %shard_map.213 = (f32[256,1408]{1,0:T(8,128)}, f32[256,1408]{1,0:T(8,128)}, f32[256,1408]{1,0:T(8,128)}, f32[256,1408]{1,0:T(8,128)}, f32[1408,256]{1,0:T(8,128)}, /*index=5*/f32[1408,256]{1,0:T(8,128)}) custom-call(bf16[768,2048]{1,0:T(8,128)(2,1)} %bitcast.78, bf16[768,2048]{1,0:T(8,128)(2,1)} %bitcast.77, bf16[768,512]{1,0:T(8,128)(2,1)} %bitcast.83, ...), custom_call_target="tpu_custom_call" | custom-call | flops 1 | bytes 1 | tf_op jit(solution)/shard_map/pallas_call | solution.py:447
  288.6 3.9 add.229
  300.5 3.8 collective-permute-done.22.refs_3_
  318.1 27.9 %shard_map.214 = (f32[256,1408]{1,0:T(8,128)}, f32[256,1408]{1,0:T(8,128)}, f32[256,1408]{1,0:T(8,128)}, f32[256,1408]{1,0:T(8,128)}, f32[1408,256]{1,0:T(8,128)}, /*index=5*/f32[1408,256]{1,0:T(8,128)}) custom-call(bf16[768,2048]{1,0:T(8,128)(2,1)} %bitcast.80, bf16[768,2048]{1,0:T(8,128)(2,1)} %bitcast.79, bf16[768,512]{1,0:T(8,128)(2,1)} %bitcast.85, ...), custom_call_target="tpu_custom_call" | custom-call | flops 1 | bytes 1 | tf_op jit(solution)/shard_map/pallas_call | solution.py:447
  351.6 25.6 %collective-permute-done.19 = f32[128,256]{1,0:T(8,128)S(1)} collective-permute-done((f32[128,256]{1,0:T(8,128)S(1)}, f32[128,256]{1,0:T(8,128)S(1)}, u32[]{:S(2)}, u32[]{:S(2)}) %collective-permute-start.19) | collective-permute-done | bytes 131104 | tf_op jit(solution)/shard_map/ppermute | solution.py:165
  394.9 7.8 %in_back.1 = (bf16[4,128,2048]{2,1,0:T(8,128)(2,1)}, f32[1,2048]{1,0:T(1,128)S(1)}) custom-call(s32[4]{0:T(128)S(1)} %get-tuple-element.269.places, f32[128,2048]{1,0:T(8,128)} %slice_add_fusion.1.refs_0_, f32[128,2048]{1,0:T(8,128)} %collective-permute-done.26.refs_1_, f32[128,2048]{1,0:T(8,128)S(1)} %collective-permute-done.31.refs_2_, ...), custom_call_target="tpu_custom_call" | custom-call | flops 1 | bytes 1 | tf_op jit(solution)/shard_map/in_back/pallas_call | solution.py:335
  411.6 15.9 %collective-permute-done.34 = f32[4,1,72,256]{3,2,1,0:T(8,128)S(1)} collective-permute-done((f32[4,1,72,256]{3,2,1,0:T(8,128)S(1)}, f32[4,1,72,256]{3,2,1,0:T(8,128)S(1)}, u32[]{:S(2)}, u32[]{:S(2)}) %collective-permute-start.34) | collective-permute-done | bytes 294944 | tf_op jit(solution)/shard_map/ppermute | solution.py:165
  434.7 6.9 %result.1 = bf16[4,128,2048]{2,1,0:T(8,128)(2,1)} custom-call(s32[4]{0:T(128)S(1)} %get-tuple-element.269.places, f32[128,2048]{1,0:T(8,128)} %slice_add_fusion.refs_0_, f32[128,2048]{1,0:T(8,128)} %collective-permute-done.24.refs_1_, f32[128,2048]{1,0:T(8,128)} %collective-permute-done.35.refs_2_, f32[128,2048]{1,0:T(8,128)} %collective-permute-done.36.refs_3_, ...), custom_call_target="tpu_custom_call" | custom-call | flops 1 | bytes 1 | tf_op jit(solution)/shard_map/result/pallas_call | solution.py:335
  444.4 7.3 %collective-permute-done.37 = f32[2,72,256]{2,1,0:T(8,128)S(1)} collective-permute-done((f32[2,72,256]{2,1,0:T(8,128)S(1)}, f32[2,72,256]{2,1,0:T(8,128)S(1)}, u32[]{:S(2)}, u32[]{:S(2)}) %collective-permute-start.37) | collective-permute-done | bytes 147488 | tf_op jit(solution)/shard_map/ppermute | solution.py:165
  452.5 3.6 collective-permute-done.38
  456.2 5.8 %all-gather.3 = f32[1,256,256]{2,1,0:T(8,128)S(1)} all-gather(f32[1,64,256]{2,1,0:T(8,128)S(1)} %slice.79), channel_id=5, replica_groups=mesh['o'=1,'z'=4,'x'=2,'y'=2,'c'=2] {'y','c'}, dimensions={1}, use_global_device_ids=true | all-gather | bytes 327680 | tf_op jit(solution)/shard_map/all_gather | solution.py:727
  (266 shorter events, 157.7 us)
Async XLA Ops:
  7.2 94.3 %all-gather.8.cloned.1.call-start = ((), (), s32[]{:S(2)}) async-start(), calls=%async_computation.4 | async-start | bytes 5242880 | tf_op jit(solution)/shard_map/all_gather | solution.py:533
  16.7 168.3 %all-gather.10.cloned.1.call-start = ((), (), s32[]{:S(2)}) async-start(), calls=%async_computation.5 | async-start | bytes 5242880 | tf_op jit(solution)/shard_map/all_gather | solution.py:555
  38.4 26.4 %collective-permute-start.1 = (f32[128,2048]{1,0:T(8,128)S(1)}, f32[128,2048]{1,0:T(8,128)S(1)}, u32[]{:S(2)}, u32[]{:S(2)}) collective-permute-start(f32[128,2048]{1,0:T(8,128)S(1)} %slice.83), channel_id=1, source_target_pairs={{0,2},{2,0},{1,3},{3,1},{4,6},{6,4},{5,7},{7,5},{8,10},{10,8},{9,1... | collective-permute-start | bytes 3145736 | tf_op jit(solution)/shard_map/ppermute | solution.py:165
  68.1 224.4 %all-gather.12.cloned.1.call-start = ((), (), s32[]{:S(2)}) async-start(), calls=%async_computation.6 | async-start | bytes 5242880 | tf_op jit(solution)/shard_map/all_gather | solution.py:559
  104.3 48.8 %collective-permute-start.8 = (f32[4,128,2048]{2,1,0:T(8,128)}, f32[4,128,2048]{2,1,0:T(8,128)}, u32[]{:S(2)}, u32[]{:S(2)}) collective-permute-start(f32[4,128,2048]{2,1,0:T(8,128)} %bitcast.58), channel_id=1, source_target_pairs={{0,1},{1,0},{2,3},{3,2},{4,5},{5,4},{6,7},{7,6},{8,9},{9,8},{10,11... | collective-permute-start | bytes 12582920 | tf_op jit(solution)/shard_map/ppermute | solution.py:165
  148.5 25.5 %collective-permute-start.7 = (f32[128,2048]{1,0:T(8,128)}, f32[128,2048]{1,0:T(8,128)}, u32[]{:S(2)}, u32[]{:S(2)}) collective-permute-start(f32[128,2048]{1,0:T(8,128)} %slice.84), channel_id=1, source_target_pairs={{0,2},{2,0},{1,3},{3,1},{4,6},{6,4},{5,7},{7,5},{8,10},{10,8},{9,1... | collective-permute-start | bytes 3145736 | tf_op jit(solution)/shard_map/ppermute | solution.py:165
  185.0 43.9 %collective-permute-start.10 = (f32[4,128,2048]{2,1,0:T(8,128)}, f32[4,128,2048]{2,1,0:T(8,128)}, u32[]{:S(2)}, u32[]{:S(2)}) collective-permute-start(f32[4,128,2048]{2,1,0:T(8,128)} %bitcast.63), channel_id=1, source_target_pairs={{0,1},{1,0},{2,3},{3,2},{4,5},{5,4},{6,7},{7,6},{8,9},{9,8},{10,11... | collective-permute-start | bytes 12582920 | tf_op jit(solution)/shard_map/ppermute | solution.py:165
  185.1 282.1 %reduce-scatter.5.cloned.1.call-start = ((), (), s32[]{:S(2)}) async-start(), calls=%async_computation.3 | async-start | bytes 2621440 | tf_op jit(solution)/shard_map/reduce_scatter | solution.py:658
  185.6 25.8 %collective-permute-start.11 = (f32[128,2048]{1,0:T(8,128)}, f32[128,2048]{1,0:T(8,128)S(1)}, u32[]{:S(2)}, u32[]{:S(2)}) collective-permute-start(f32[128,2048]{1,0:T(8,128)} %slice_add_fusion.2.refs_0_), channel_id=1, source_target_pairs={{0,2},{2,0},{1,3},{3,1},{4,6},{6,4},{5,7},{7,5},{8,10},{10,8},{9,1... | collective-permute-start | bytes 3145736 | tf_op jit(solution)/shard_map/ppermute | solution.py:165
  187.1 45.4 %collective-permute-start.9 = (f32[256,2048]{1,0:T(8,128)}, f32[256,2048]{1,0:T(8,128)S(1)}, u32[]{:S(2)}, u32[]{:S(2)}) collective-permute-start(f32[256,2048]{1,0:T(8,128)} %copy-done.38), channel_id=1, source_target_pairs={{0,1},{1,0},{2,3},{3,2},{4,5},{5,4},{6,7},{7,6},{8,9},{9,8},{10,11... | collective-permute-start | bytes 6291464 | tf_op jit(solution)/shard_map/ppermute | solution.py:165
  187.3 25.6 %collective-permute-start.12 = (f32[128,2048]{1,0:T(8,128)}, f32[128,2048]{1,0:T(8,128)S(1)}, u32[]{:S(2)}, u32[]{:S(2)}) collective-permute-start(f32[128,2048]{1,0:T(8,128)} %slice_add_fusion.2.refs_0_), channel_id=1, source_target_pairs={{0,1},{1,0},{2,3},{3,2},{4,5},{5,4},{6,7},{7,6},{8,9},{9,8},{10,11... | collective-permute-start | bytes 3145736 | tf_op jit(solution)/shard_map/ppermute | solution.py:165
  211.5 71.8 %collective-permute-start.17 = (f32[2,128,2048]{2,1,0:T(8,128)}, f32[2,128,2048]{2,1,0:T(8,128)}, u32[]{:S(2)}, u32[]{:S(2)}) collective-permute-start(f32[2,128,2048]{2,1,0:T(8,128)} %pad_maximum_fusion), channel_id=1, source_target_pairs={{0,2},{2,0},{1,3},{3,1},{4,6},{6,4},{5,7},{7,5},{8,10},{10,8},{9,1... | collective-permute-start | bytes 6291464 | tf_op jit(solution)/shard_map/ppermute | solution.py:165
  227.5 55.8 %collective-permute-start.16 = (f32[512,1024]{1,0:T(8,128)}, f32[512,1024]{1,0:T(8,128)}, u32[]{:S(2)}, u32[]{:S(2)}) collective-permute-start(f32[512,1024]{1,0:T(8,128)} %out_grad.1), channel_id=1, source_target_pairs={{0,4},{4,0},{1,5},{5,1},{2,6},{6,2},{3,7},{7,3},{8,12},{12,8},{9,1... | collective-permute-start | bytes 6291464 | tf_op jit(solution)/shard_map/ppermute | solution.py:165
  247.3 41.3 %collective-permute-start.14 = (f32[256,2048]{1,0:T(8,128)}, f32[256,2048]{1,0:T(8,128)}, u32[]{:S(2)}, u32[]{:S(2)}) collective-permute-start(f32[256,2048]{1,0:T(8,128)} %get-tuple-element.382), channel_id=1, source_target_pairs={{0,1},{1,0},{2,3},{3,2},{4,5},{5,4},{6,7},{7,6},{8,9},{9,8},{10,11... | collective-permute-start | bytes 6291464 | tf_op jit(solution)/shard_map/ppermute | solution.py:165
  247.3 39.5 %collective-permute-start.15 = (f32[256,256]{1,0:T(8,128)}, f32[256,256]{1,0:T(8,128)S(1)}, u32[]{:S(2)}, u32[]{:S(2)}) collective-permute-start(f32[256,256]{1,0:T(8,128)} %get-tuple-element.385), channel_id=1, source_target_pairs={{0,1},{1,0},{2,3},{3,2},{4,5},{5,4},{6,7},{7,6},{8,9},{9,8},{10,11... | collective-permute-start | bytes 786440 | tf_op jit(solution)/shard_map/ppermute | solution.py:165
  292.6 174.6 %reduce-scatter.3.cloned.1.call-start = ((), (), s32[]{:S(2)}) async-start(), calls=%async_computation.2 | async-start | bytes 2621440 | tf_op jit(solution)/shard_map/reduce_scatter | solution.py:670
  295.6 50.5 %collective-permute-start.20 = (f32[128,2048]{1,0:T(8,128)}, f32[128,2048]{1,0:T(8,128)}, u32[]{:S(2)}, u32[]{:S(2)}) collective-permute-start(f32[128,2048]{1,0:T(8,128)} %slice.87), channel_id=1, source_target_pairs={{0,2},{2,0},{1,3},{3,1},{4,6},{6,4},{5,7},{7,5},{8,10},{10,8},{9,1... | collective-permute-start | bytes 3145736 | tf_op jit(solution)/shard_map/ppermute | solution.py:165
  297.1 83.7 %collective-permute-start.28 = (f32[1024,512]{1,0:T(8,128)}, f32[1024,512]{1,0:T(8,128)S(1)}, u32[]{:S(2)}, u32[]{:S(2)}) collective-permute-start(f32[1024,512]{1,0:T(8,128)} %copy-done.37), channel_id=1, source_target_pairs={{0,4},{4,0},{1,5},{5,1},{2,6},{6,2},{3,7},{7,3},{8,12},{12,8},{9,1... | collective-permute-start | bytes 6291464 | tf_op jit(solution)/shard_map/ppermute | solution.py:165
  304.4 73.5 %collective-permute-start.18 = (f32[128,2048]{1,0:T(8,128)}, f32[128,2048]{1,0:T(8,128)}, u32[]{:S(2)}, u32[]{:S(2)}) collective-permute-start(f32[128,2048]{1,0:T(8,128)} %slice.85), channel_id=1, source_target_pairs={{0,2},{2,0},{1,3},{3,1},{4,6},{6,4},{5,7},{7,5},{8,10},{10,8},{9,1... | collective-permute-start | bytes 3145736 | tf_op jit(solution)/shard_map/ppermute | solution.py:165
  346.0 36.6 %collective-permute-start.27 = (f32[256,1408]{1,0:T(8,128)}, f32[256,1408]{1,0:T(8,128)}, u32[]{:S(2)}, u32[]{:S(2)}) collective-permute-start(f32[256,1408]{1,0:T(8,128)} %get-tuple-element.463), channel_id=1, source_target_pairs={{0,4},{4,0},{1,5},{5,1},{2,6},{6,2},{3,7},{7,3},{8,12},{12,8},{9,1... | collective-permute-start | bytes 4325384 | tf_op jit(solution)/shard_map/ppermute | solution.py:165
  349.5 36.1 %collective-permute-start.26 = (f32[128,2048]{1,0:T(8,128)}, f32[128,2048]{1,0:T(8,128)}, u32[]{:S(2)}, u32[]{:S(2)}) collective-permute-start(f32[128,2048]{1,0:T(8,128)} %slice_add_fusion.1.refs_0_), channel_id=1, source_target_pairs={{0,2},{2,0},{1,3},{3,1},{4,6},{6,4},{5,7},{7,5},{8,10},{10,8},{9,1... | collective-permute-start | bytes 3145736 | tf_op jit(solution)/shard_map/ppermute | solution.py:165
  350.0 27.2 %collective-permute-start.19 = (f32[128,256]{1,0:T(8,128)S(1)}, f32[128,256]{1,0:T(8,128)S(1)}, u32[]{:S(2)}, u32[]{:S(2)}) collective-permute-start(f32[128,256]{1,0:T(8,128)S(1)} %slice.86), channel_id=1, source_target_pairs={{0,2},{2,0},{1,3},{3,1},{4,6},{6,4},{5,7},{7,5},{8,10},{10,8},{9,1... | collective-permute-start | bytes 393224 | tf_op jit(solution)/shard_map/ppermute | solution.py:165
  387.7 39.9 %collective-permute-start.33 = (f32[256,1408]{1,0:T(8,128)}, f32[256,1408]{1,0:T(8,128)}, u32[]{:S(2)}, u32[]{:S(2)}) collective-permute-start(f32[256,1408]{1,0:T(8,128)} %get-tuple-element.498), channel_id=1, source_target_pairs={{0,4},{4,0},{1,5},{5,1},{2,6},{6,2},{3,7},{7,3},{8,12},{12,8},{9,1... | collective-permute-start | bytes 4325384 | tf_op jit(solution)/shard_map/ppermute | solution.py:165
  430.7 33.8 %collective-permute-start.39 = (f32[1408,256]{1,0:T(8,128)}, f32[1408,256]{1,0:T(8,128)}, u32[]{:S(2)}, u32[]{:S(2)}) collective-permute-start(f32[1408,256]{1,0:T(8,128)} %get-tuple-element.524), channel_id=1, source_target_pairs={{0,4},{4,0},{1,5},{5,1},{2,6},{6,2},{3,7},{7,3},{8,12},{12,8},{9,1... | collective-permute-start | bytes 4325384 | tf_op jit(solution)/shard_map/ppermute | solution.py:165
  (77 other events, 626.3 us)
Sparse Core Ops, SparseCore 0:
  16.9 83.4 all-gather.7
  101.9 79.2 all-gather.9
  185.2 82.0 all-gather.11
  292.7 44.8 reduce-scatter.4
  388.8 43.7 reduce-scatter.2

commit v5 on v4

--- a/solution.py
+++ b/solution.py
@@ -646,16 +646,17 @@
 
     sums = run(wgrads, nm, go, nm_columns, go_columns, *sums)
     go_rest = wait(go_rest)
+    out_sent, sent, kv_sent = wait(out_sent), wait(sent), wait(kv_sent)
+    nm_z_other = wait(nm_z_other)
+    nm_far = swap(nm_z_other, "c")
+    go_far = [swap(go_first, "c"), swap(go_rest, "c")]
     out_half = run(jnp.add, out_kept, out_sent)
+    grad_w_out = lax.psum_scatter(out_half, ("o", "z"), scatter_dimension=1, tiled=True)
     kv_kept = run(jnp.add, kv_kept, kv_sent)
     kv_received = order.move(kv_kept[quarter:], "y", [(0, 1), (1, 0)], queue=False)
     kept = run(jnp.add, kept, sent)
     received = swap(kept[quarter:], "y")
     down_received = order.move(down_kept[quarter:], "y", [(0, 1), (1, 0)], queue=False)
-    nm_z_other = wait(nm_z_other)
-    nm_far = swap(nm_z_other, "c")
-    go_far = [swap(go_first, "c"), swap(go_rest, "c")]
-    grad_w_out = lax.psum_scatter(out_half, ("o", "z"), scatter_dimension=1, tiled=True)
     go, go_columns = packed([go_first, go_rest, *go_far], ones)
     nm, nm_columns = packed([nm_z_other, nm_far], norm_mid)
     sums = run(wgrads, nm, go, nm_columns, go_columns, *sums)

time: 482 us -> 477 us (0.990)
    unnamed x112 -> x116, local copies, waits for them, and re-layouts: 33.2 us -> 35.1 us
  transfers between devices with their start and end apart: 45 -> 45, of which waited for: 19 -> 18; matrix products, arithmetic and copies ran while one was open for 13% -> 13% of each run, Pallas kernels for 35% -> 35%
where the time goes in v5:
time: 477 us; the launch traced here: 469 us
  Pallas kernels  168 us (35%)
  waiting for transfers between devices  155 us (32%)
  local copies, waits for them, and re-layouts  50 us (10%)
  other arithmetic  42.3 us (9%)
  starting transfers between devices  31.3 us (7%)
  between operations  15.3 us (3%)
  blocking collectives  5.79 us (1%)
    ppermute x40, waiting for transfers between devices, move(): a = lax.ppermute(a, axis, pairs)  154 us
    pallas_call x3, Pallas kernels, ffn(): pl.pallas_call(functools.partial(ffn_kernel, own, bool(previous)), grid=(...  76.5 us
    unnamed x116, local copies, waits for them, and re-layouts  35.1 us
    ppermute x40, starting transfers between devices, move(): a = lax.ppermute(a, axis, pairs)  30.4 us
    pallas_call x4, Pallas kernels, rows_call(): pl.pallas_call(kernel, grid_spec=pltpu.PrefetchScalarGridSpec(num_scalar_...  26.1 us
    add x13, other arithmetic, run(): outs = f(*args)  23.7 us
    pallas_call x2, Pallas kernels, call(): pl.pallas_call(kernel, out_shape=outs, name=name, compiler_params=pltpu.C...  23.4 us
    pallas_call x2, Pallas kernels, pair_dots(): pl.pallas_call(functools.partial(pair_kernel, transposed), grid=(width //...  16.2 us
  transfers between devices with their start and end apart: 45, of which 18 were waited for; matrix products, arithmetic and copies ran while one was open for 13% of the time, Pallas kernels for 35%

profile of v5, /device:TPU:0, one launch (start us, length us, event | category | flops | bytes accessed | tf_op | source)
XLA Modules:
  0.0 469.1 jit_solution(14057632827596636386)
XLA Ops:
  19.8 12.0 %attention_forward.1 = (f32[256,2048]{1,0:T(8,128)}, f32[256,2048]{1,0:T(8,128)}, bf16[512,2048]{1,0:T(8,128)(2,1)}, bf16[512,512]{1,0:T(8,128)(2,1)}, bf16[512,...) custom-call(bf16[512,2048]{1,0:T(8,128)(2,1)} %copy-done.4, f32[1,2048]{1,0:T(1,128)} %bitcast.91, ...), custom_call_target="tpu_custom_call" | custom-call | flops 1 | bytes 1 | tf_op jit(solution)/shard_map/attention_forward/pallas_call | solution.py:188
  42.5 22.4 %collective-permute-done.1 = f32[128,2048]{1,0:T(8,128)S(1)} collective-permute-done((f32[128,2048]{1,0:T(8,128)S(1)}, f32[128,2048]{1,0:T(8,128)S(1)}, u32[]{:S(2)}, u32[]{:S(2)}) %collective-permute-start.1) | collective-permute-done | bytes 1048608 | tf_op jit(solution)/shard_map/ppermute | solution.py:165
  68.4 21.6 %collective-permute-done.2.refs_1_.refs_5_ = f32[128,2048]{1,0:T(8,128)S(1)} collective-permute-done((f32[128,2048]{1,0:T(8,128)S(1)}, f32[128,2048]{1,0:T(8,128)S(1)}, u32[]{:S(2)}, u32[]{:S(2)}) %collective-permute-start.2) | collective-permute-done | bytes 1048608 | tf_op jit(solution)/shard_map/ppermute | solution.py:165
  94.1 5.2 %mid_norm.1 = (bf16[4,128,2048]{2,1,0:T(8,128)(2,1)S(1)}, bf16[4,128,512]{2,1,0:T(8,128)(2,1)S(1)}) custom-call(s32[5]{0:T(128)S(1)} %stack.43.places, f32[128,2048]{1,0:T(8,128)S(1)} %get-tuple-element.516.refs_0_.refs_4_, f32[128,2048]{1,0:T(8,128)S(1)} %collective-permute-done.2.refs_1_.refs_5_, f32[128,2048]{1,0:T(8,128)S(1)} %collective-permute-done.3.refs_2_.refs_6_, ...), custom_call_target="tpu_custom_call" | custom-call | flops 1 | bytes 1 | tf_op jit(solution)/shard_map/mid_norm/pallas_call | solution.py:335
  104.3 20.8 %shard_map.212 = (f32[256,1408]{1,0:T(8,128)}, f32[256,1408]{1,0:T(8,128)}, f32[256,1408]{1,0:T(8,128)}, f32[256,1408]{1,0:T(8,128)}, f32[1408,256]{1,0:T(8,128)...) custom-call(bf16[512,2048]{1,0:T(8,128)(2,1)} %bitcast.81, ...), custom_call_target="tpu_custom_call" | custom-call | flops 1 | bytes 1 | tf_op jit(solution)/shard_map/pallas_call | solution.py:447
  131.2 10.2 %mid_part.1 = (f32[256,2048]{1,0:T(8,128)S(1)}, f32[256,2048]{1,0:T(8,128)}) custom-call(bf16[512,1408]{1,0:T(8,128)(2,1)S(1)} %copy-done.23, bf16[512,1408]{1,0:T(8,128)(2,1)S(1)} %copy-done.24, bf16[2048,1408]{1,0:T(8,128)(2,1)} %refs_4_.5, bf16[2048,1408]{1,0:T(8,128)(2,1)} %refs_5_.5), custom_call_target="tpu_custom_call" | custom-call | flops 1 | bytes 1 | tf_op jit(solution)/shard_map/mid_part/pallas_call | solution.py:276
  141.4 4.4 collective-permute-done.6
  154.6 3.6 pack.4
  159.9 14.2 %collective-permute-done.7 = f32[128,2048]{1,0:T(8,128)} collective-permute-done((f32[128,2048]{1,0:T(8,128)}, f32[128,2048]{1,0:T(8,128)}, u32[]{:S(2)}, u32[]{:S(2)}) %collective-permute-start.7) | collective-permute-done | bytes 1048608 | tf_op jit(solution)/shard_map/ppermute | solution.py:165
  176.4 6.0 %down_part.1 = (f32[256,2048]{1,0:T(8,128)S(1)}, f32[256,2048]{1,0:T(8,128)S(1)}) custom-call(bf16[512,1408]{1,0:T(8,128)(2,1)S(1)} %copy-done.25, bf16[1408,2048]{1,0:T(8,128)(2,1)} %refs_6_.5), custom_call_target="tpu_custom_call" | custom-call | flops 1 | bytes 1 | tf_op jit(solution)/shard_map/down_part/pallas_call | solution.py:276
  187.5 23.8 %collective-permute-done.11.refs_1_ = f32[128,2048]{1,0:T(8,128)S(1)} collective-permute-done((f32[128,2048]{1,0:T(8,128)}, f32[128,2048]{1,0:T(8,128)S(1)}, u32[]{:S(2)}, u32[]{:S(2)}) %collective-permute-start.11) | collective-permute-done | bytes 1048608 | tf_op jit(solution)/shard_map/ppermute | solution.py:165
  216.9 5.9 %mid_back.1 = (f32[4,128,2048]{2,1,0:T(8,128)S(1)}, bf16[4,128,2048]{2,1,0:T(8,128)(2,1)S(1)}, f32[1,2048]{1,0:T(1,128)S(1)}) custom-call(f32[128,2048]{1,0:T(8,128)S(1)} %copy-done.8, f32[128,2048]{1,0:T(8,128)S(1)} %collective-permute-done.11.refs_1_, f32[128,2048]{1,0:T(8,128)S(1)} %collective-permute-done.12.refs_2_, ...), custom_call_target="tpu_custom_call" | custom-call | flops 1 | bytes 1 | tf_op jit(solution)/shard_map/mid_back/pallas_call | solution.py:335
  235.8 11.4 %attention_backward.1 = (f32[256,2048]{1,0:T(8,128)}, f32[256,2048]{1,0:T(8,128)}, f32[256,256]{1,0:T(8,128)}, f32[256,256]{1,0:T(8,128)}, bf16[512,512]{1,0:T(8,128)(2,1)}) custom-call(bf16[512,2048]{1,0:T(8,128)(2,1)} %bitcast.72, bf16[512,2048]{1,0:T(8,128)(2,1)} %wo_ref.1, bf16[2048,512]{1,0:T(8,128)(2,1)} %wq_ref.1, ...), custom_call_target="tpu_custom_call" | custom-call | flops 1 | bytes 1 | tf_op jit(solution)/shard_map/attention_backward/pallas_call | solution.py:188
  248.8 6.0 %late_grads.1 = (f32[512,1024]{1,0:T(8,128)S(1)}, f32[1024,512]{1,0:T(8,128)S(1)}, f32[1024,512]{1,0:T(8,128)}) custom-call(s32[8]{0:T(128)S(1)} %pad_add_fusion.1.places, bf16[512,512]{1,0:T(8,128)(2,1)S(1)} %copy-done.21, bf16[512,2048]{1,0:T(8,128)(2,1)} %bitcast.73, bf16[512,2048]{1,0:T(8,128)(2,1)} %get-tuple-element.399.normed_ref, ...), custom_call_target="tpu_custom_call" | custom-call | flops 1 | bytes 1 | tf_op jit(solution)/shard_map/late_grads/pallas_call | solution.py:310
  257.5 28.0 %shard_map.213 = (f32[256,1408]{1,0:T(8,128)}, f32[256,1408]{1,0:T(8,128)}, f32[256,1408]{1,0:T(8,128)}, f32[256,1408]{1,0:T(8,128)}, f32[1408,256]{1,0:T(8,128)}, /*index=5*/f32[1408,256]{1,0:T(8,128)}) custom-call(bf16[768,2048]{1,0:T(8,128)(2,1)} %bitcast.78, bf16[768,2048]{1,0:T(8,128)(2,1)} %bitcast.77, bf16[768,512]{1,0:T(8,128)(2,1)} %bitcast.83, ...), custom_call_target="tpu_custom_call" | custom-call | flops 1 | bytes 1 | tf_op jit(solution)/shard_map/pallas_call | solution.py:447
  285.7 4.1 add.227
  312.0 27.7 %shard_map.214 = (f32[256,1408]{1,0:T(8,128)}, f32[256,1408]{1,0:T(8,128)}, f32[256,1408]{1,0:T(8,128)}, f32[256,1408]{1,0:T(8,128)}, f32[1408,256]{1,0:T(8,128)}, /*index=5*/f32[1408,256]{1,0:T(8,128)}) custom-call(bf16[768,2048]{1,0:T(8,128)(2,1)} %bitcast.80, bf16[768,2048]{1,0:T(8,128)(2,1)} %bitcast.79, bf16[768,512]{1,0:T(8,128)(2,1)} %bitcast.85, ...), custom_call_target="tpu_custom_call" | custom-call | flops 1 | bytes 1 | tf_op jit(solution)/shard_map/pallas_call | solution.py:447
  345.5 25.3 %collective-permute-done.19 = f32[128,256]{1,0:T(8,128)S(1)} collective-permute-done((f32[128,256]{1,0:T(8,128)S(1)}, f32[128,256]{1,0:T(8,128)S(1)}, u32[]{:S(2)}, u32[]{:S(2)}) %collective-permute-start.19) | collective-permute-done | bytes 131104 | tf_op jit(solution)/shard_map/ppermute | solution.py:165
  390.2 8.0 %in_back.1 = (bf16[4,128,2048]{2,1,0:T(8,128)(2,1)}, f32[1,2048]{1,0:T(1,128)S(1)}) custom-call(s32[4]{0:T(128)S(1)} %get-tuple-element.272.places, f32[128,2048]{1,0:T(8,128)} %slice_add_fusion.1.refs_0_, f32[128,2048]{1,0:T(8,128)} %collective-permute-done.26.refs_1_, f32[128,2048]{1,0:T(8,128)S(1)} %collective-permute-done.31.refs_2_, ...), custom_call_target="tpu_custom_call" | custom-call | flops 1 | bytes 1 | tf_op jit(solution)/shard_map/in_back/pallas_call | solution.py:335
  407.8 14.9 %collective-permute-done.34 = f32[4,1,72,256]{3,2,1,0:T(8,128)S(1)} collective-permute-done((f32[4,1,72,256]{3,2,1,0:T(8,128)S(1)}, f32[4,1,72,256]{3,2,1,0:T(8,128)S(1)}, u32[]{:S(2)}, u32[]{:S(2)}) %collective-permute-start.34) | collective-permute-done | bytes 294944 | tf_op jit(solution)/shard_map/ppermute | solution.py:165
  429.9 6.9 %result.1 = bf16[4,128,2048]{2,1,0:T(8,128)(2,1)} custom-call(s32[4]{0:T(128)S(1)} %get-tuple-element.272.places, f32[128,2048]{1,0:T(8,128)} %slice_add_fusion.refs_0_, f32[128,2048]{1,0:T(8,128)} %collective-permute-done.24.refs_1_, f32[128,2048]{1,0:T(8,128)} %collective-permute-done.35.refs_2_, f32[128,2048]{1,0:T(8,128)} %collective-permute-done.36.refs_3_, ...), custom_call_target="tpu_custom_call" | custom-call | flops 1 | bytes 1 | tf_op jit(solution)/shard_map/result/pallas_call | solution.py:335
  439.5 7.4 %collective-permute-done.37 = f32[2,72,256]{2,1,0:T(8,128)S(1)} collective-permute-done((f32[2,72,256]{2,1,0:T(8,128)S(1)}, f32[2,72,256]{2,1,0:T(8,128)S(1)}, u32[]{:S(2)}, u32[]{:S(2)}) %collective-permute-start.37) | collective-permute-done | bytes 147488 | tf_op jit(solution)/shard_map/ppermute | solution.py:165
  447.6 3.7 collective-permute-done.38
  451.4 5.8 %all-gather.3 = f32[1,256,256]{2,1,0:T(8,128)S(1)} all-gather(f32[1,64,256]{2,1,0:T(8,128)S(1)} %slice.79), channel_id=5, replica_groups=mesh['o'=1,'z'=4,'x'=2,'y'=2,'c'=2] {'y','c'}, dimensions={1}, use_global_device_ids=true | all-gather | bytes 327680 | tf_op jit(solution)/shard_map/all_gather | solution.py:728
  (270 shorter events, 154.3 us)
Async XLA Ops:
  7.2 94.3 %all-gather.8.cloned.1.call-start = ((), (), s32[]{:S(2)}) async-start(), calls=%async_computation.4 | async-start | bytes 5242880 | tf_op jit(solution)/shard_map/all_gather | solution.py:533
  16.7 168.2 %all-gather.10.cloned.1.call-start = ((), (), s32[]{:S(2)}) async-start(), calls=%async_computation.5 | async-start | bytes 5242880 | tf_op jit(solution)/shard_map/all_gather | solution.py:555
  38.4 26.4 %collective-permute-start.1 = (f32[128,2048]{1,0:T(8,128)S(1)}, f32[128,2048]{1,0:T(8,128)S(1)}, u32[]{:S(2)}, u32[]{:S(2)}) collective-permute-start(f32[128,2048]{1,0:T(8,128)S(1)} %slice.83), channel_id=1, source_target_pairs={{0,2},{2,0},{1,3},{3,1},{4,6},{6,4},{5,7},{7,5},{8,10},{10,8},{9,1... | collective-permute-start | bytes 3145736 | tf_op jit(solution)/shard_map/ppermute | solution.py:165
  68.1 217.4 %all-gather.12.cloned.1.call-start = ((), (), s32[]{:S(2)}) async-start(), calls=%async_computation.6 | async-start | bytes 5242880 | tf_op jit(solution)/shard_map/all_gather | solution.py:559
  104.3 48.9 %collective-permute-start.8 = (f32[4,128,2048]{2,1,0:T(8,128)}, f32[4,128,2048]{2,1,0:T(8,128)}, u32[]{:S(2)}, u32[]{:S(2)}) collective-permute-start(f32[4,128,2048]{2,1,0:T(8,128)} %bitcast.58), channel_id=1, source_target_pairs={{0,1},{1,0},{2,3},{3,2},{4,5},{5,4},{6,7},{7,6},{8,9},{9,8},{10,11... | collective-permute-start | bytes 12582920 | tf_op jit(solution)/shard_map/ppermute | solution.py:165
  148.5 25.5 %collective-permute-start.7 = (f32[128,2048]{1,0:T(8,128)}, f32[128,2048]{1,0:T(8,128)}, u32[]{:S(2)}, u32[]{:S(2)}) collective-permute-start(f32[128,2048]{1,0:T(8,128)} %slice.84), channel_id=1, source_target_pairs={{0,2},{2,0},{1,3},{3,1},{4,6},{6,4},{5,7},{7,5},{8,10},{10,8},{9,1... | collective-permute-start | bytes 3145736 | tf_op jit(solution)/shard_map/ppermute | solution.py:165
  185.0 43.9 %collective-permute-start.10 = (f32[4,128,2048]{2,1,0:T(8,128)}, f32[4,128,2048]{2,1,0:T(8,128)}, u32[]{:S(2)}, u32[]{:S(2)}) collective-permute-start(f32[4,128,2048]{2,1,0:T(8,128)} %bitcast.63), channel_id=1, source_target_pairs={{0,1},{1,0},{2,3},{3,2},{4,5},{5,4},{6,7},{7,6},{8,9},{9,8},{10,11... | collective-permute-start | bytes 12582920 | tf_op jit(solution)/shard_map/ppermute | solution.py:165
  185.0 277.4 %reduce-scatter.5.cloned.1.call-start = ((), (), s32[]{:S(2)}) async-start(), calls=%async_computation.3 | async-start | bytes 2621440 | tf_op jit(solution)/shard_map/reduce_scatter | solution.py:654
  185.5 25.8 %collective-permute-start.11 = (f32[128,2048]{1,0:T(8,128)}, f32[128,2048]{1,0:T(8,128)S(1)}, u32[]{:S(2)}, u32[]{:S(2)}) collective-permute-start(f32[128,2048]{1,0:T(8,128)} %slice_add_fusion.2.refs_0_), channel_id=1, source_target_pairs={{0,2},{2,0},{1,3},{3,1},{4,6},{6,4},{5,7},{7,5},{8,10},{10,8},{9,1... | collective-permute-start | bytes 3145736 | tf_op jit(solution)/shard_map/ppermute | solution.py:165
  187.0 45.4 %collective-permute-start.9 = (f32[256,2048]{1,0:T(8,128)}, f32[256,2048]{1,0:T(8,128)S(1)}, u32[]{:S(2)}, u32[]{:S(2)}) collective-permute-start(f32[256,2048]{1,0:T(8,128)} %copy-done.40), channel_id=1, source_target_pairs={{0,1},{1,0},{2,3},{3,2},{4,5},{5,4},{6,7},{7,6},{8,9},{9,8},{10,11... | collective-permute-start | bytes 6291464 | tf_op jit(solution)/shard_map/ppermute | solution.py:165
  187.3 25.6 %collective-permute-start.12 = (f32[128,2048]{1,0:T(8,128)}, f32[128,2048]{1,0:T(8,128)S(1)}, u32[]{:S(2)}, u32[]{:S(2)}) collective-permute-start(f32[128,2048]{1,0:T(8,128)} %slice_add_fusion.2.refs_0_), channel_id=1, source_target_pairs={{0,1},{1,0},{2,3},{3,2},{4,5},{5,4},{6,7},{7,6},{8,9},{9,8},{10,11... | collective-permute-start | bytes 3145736 | tf_op jit(solution)/shard_map/ppermute | solution.py:165
  211.5 74.0 %collective-permute-start.16 = (f32[2,128,2048]{2,1,0:T(8,128)}, f32[2,128,2048]{2,1,0:T(8,128)}, u32[]{:S(2)}, u32[]{:S(2)}) collective-permute-start(f32[2,128,2048]{2,1,0:T(8,128)} %pad_maximum_fusion), channel_id=1, source_target_pairs={{0,2},{2,0},{1,3},{3,1},{4,6},{6,4},{5,7},{7,5},{8,10},{10,8},{9,1... | collective-permute-start | bytes 6291464 | tf_op jit(solution)/shard_map/ppermute | solution.py:165
  227.5 58.0 %collective-permute-start.15 = (f32[512,1024]{1,0:T(8,128)}, f32[512,1024]{1,0:T(8,128)}, u32[]{:S(2)}, u32[]{:S(2)}) collective-permute-start(f32[512,1024]{1,0:T(8,128)} %out_grad.1), channel_id=1, source_target_pairs={{0,4},{4,0},{1,5},{5,1},{2,6},{6,2},{3,7},{7,3},{8,12},{12,8},{9,1... | collective-permute-start | bytes 6291464 | tf_op jit(solution)/shard_map/ppermute | solution.py:165
  247.2 38.3 %collective-permute-start.14 = (f32[256,2048]{1,0:T(8,128)}, f32[256,2048]{1,0:T(8,128)}, u32[]{:S(2)}, u32[]{:S(2)}) collective-permute-start(f32[256,2048]{1,0:T(8,128)} %get-tuple-element.385), channel_id=1, source_target_pairs={{0,1},{1,0},{2,3},{3,2},{4,5},{5,4},{6,7},{7,6},{8,9},{9,8},{10,11... | collective-permute-start | bytes 6291464 | tf_op jit(solution)/shard_map/ppermute | solution.py:165
  247.2 38.3 %collective-permute-start.17 = (f32[256,256]{1,0:T(8,128)}, f32[256,256]{1,0:T(8,128)}, u32[]{:S(2)}, u32[]{:S(2)}) collective-permute-start(f32[256,256]{1,0:T(8,128)} %get-tuple-element.418), channel_id=1, source_target_pairs={{0,1},{1,0},{2,3},{3,2},{4,5},{5,4},{6,7},{7,6},{8,9},{9,8},{10,11... | collective-permute-start | bytes 786440 | tf_op jit(solution)/shard_map/ppermute | solution.py:165
  289.8 172.6 %reduce-scatter.3.cloned.1.call-start = ((), (), s32[]{:S(2)}) async-start(), calls=%async_computation.2 | async-start | bytes 2621440 | tf_op jit(solution)/shard_map/reduce_scatter | solution.py:671
  295.6 44.2 %collective-permute-start.20 = (f32[128,2048]{1,0:T(8,128)}, f32[128,2048]{1,0:T(8,128)}, u32[]{:S(2)}, u32[]{:S(2)}) collective-permute-start(f32[128,2048]{1,0:T(8,128)} %slice.87), channel_id=1, source_target_pairs={{0,2},{2,0},{1,3},{3,1},{4,6},{6,4},{5,7},{7,5},{8,10},{10,8},{9,1... | collective-permute-start | bytes 3145736 | tf_op jit(solution)/shard_map/ppermute | solution.py:165
  297.1 78.3 %collective-permute-start.28 = (f32[1024,512]{1,0:T(8,128)S(1)}, f32[1024,512]{1,0:T(8,128)}, u32[]{:S(2)}, u32[]{:S(2)}) collective-permute-start(f32[1024,512]{1,0:T(8,128)S(1)} %copy-done.39), channel_id=1, source_target_pairs={{0,4},{4,0},{1,5},{5,1},{2,6},{6,2},{3,7},{7,3},{8,12},{12,8},{9,1... | collective-permute-start | bytes 6291464 | tf_op jit(solution)/shard_map/ppermute | solution.py:165
  299.4 72.1 %collective-permute-start.18 = (f32[128,2048]{1,0:T(8,128)}, f32[128,2048]{1,0:T(8,128)}, u32[]{:S(2)}, u32[]{:S(2)}) collective-permute-start(f32[128,2048]{1,0:T(8,128)} %slice.85), channel_id=1, source_target_pairs={{0,2},{2,0},{1,3},{3,1},{4,6},{6,4},{5,7},{7,5},{8,10},{10,8},{9,1... | collective-permute-start | bytes 3145736 | tf_op jit(solution)/shard_map/ppermute | solution.py:165
  339.8 39.0 %collective-permute-start.27 = (f32[256,1408]{1,0:T(8,128)}, f32[256,1408]{1,0:T(8,128)}, u32[]{:S(2)}, u32[]{:S(2)}) collective-permute-start(f32[256,1408]{1,0:T(8,128)} %get-tuple-element.469), channel_id=1, source_target_pairs={{0,4},{4,0},{1,5},{5,1},{2,6},{6,2},{3,7},{7,3},{8,12},{12,8},{9,1... | collective-permute-start | bytes 4325384 | tf_op jit(solution)/shard_map/ppermute | solution.py:165
  343.4 38.5 %collective-permute-start.26 = (f32[128,2048]{1,0:T(8,128)}, f32[128,2048]{1,0:T(8,128)}, u32[]{:S(2)}, u32[]{:S(2)}) collective-permute-start(f32[128,2048]{1,0:T(8,128)} %slice_add_fusion.1.refs_0_), channel_id=1, source_target_pairs={{0,2},{2,0},{1,3},{3,1},{4,6},{6,4},{5,7},{7,5},{8,10},{10,8},{9,1... | collective-permute-start | bytes 3145736 | tf_op jit(solution)/shard_map/ppermute | solution.py:165
  344.9 25.9 %collective-permute-start.19 = (f32[128,256]{1,0:T(8,128)S(1)}, f32[128,256]{1,0:T(8,128)S(1)}, u32[]{:S(2)}, u32[]{:S(2)}) collective-permute-start(f32[128,256]{1,0:T(8,128)S(1)} %slice.86), channel_id=1, source_target_pairs={{0,2},{2,0},{1,3},{3,1},{4,6},{6,4},{5,7},{7,5},{8,10},{10,8},{9,1... | collective-permute-start | bytes 393224 | tf_op jit(solution)/shard_map/ppermute | solution.py:165
  382.9 39.9 %collective-permute-start.33 = (f32[256,1408]{1,0:T(8,128)}, f32[256,1408]{1,0:T(8,128)}, u32[]{:S(2)}, u32[]{:S(2)}) collective-permute-start(f32[256,1408]{1,0:T(8,128)} %get-tuple-element.504), channel_id=1, source_target_pairs={{0,4},{4,0},{1,5},{5,1},{2,6},{6,2},{3,7},{7,3},{8,12},{12,8},{9,1... | collective-permute-start | bytes 4325384 | tf_op jit(solution)/shard_map/ppermute | solution.py:165
  425.9 33.8 %collective-permute-start.39 = (f32[1408,256]{1,0:T(8,128)}, f32[1408,256]{1,0:T(8,128)}, u32[]{:S(2)}, u32[]{:S(2)}) collective-permute-start(f32[1408,256]{1,0:T(8,128)} %get-tuple-element.530), channel_id=1, source_target_pairs={{0,4},{4,0},{1,5},{5,1},{2,6},{6,2},{3,7},{7,3},{8,12},{12,8},{9,1... | collective-permute-start | bytes 4325384 | tf_op jit(solution)/shard_map/ppermute | solution.py:165
  (79 other events, 545.0 us)
Sparse Core Ops, SparseCore 0:
  16.9 83.4 all-gather.7
  101.9 79.2 all-gather.9
  185.1 82.0 all-gather.11
  289.9 44.8 reduce-scatter.4
  384.1 44.5 reduce-scatter.2
